TPU v7x, 32 devices: a whole 2x2x4 slice. The times are simulated.
32 devices in a mesh: groups: 2 (over y), tensor: 4 (over z), seq: 2 (over x), kv: 2 (over core).
Axes of the slice: x: 2, y: 2, z: 4, core: 2. Of those that a mesh axis runs over, the one named last changes fastest.
Arguments:
- hidden_rows: bfloat16 [384, 8192], P(('groups', 'tensor', 'seq')), parts along dimension 0, may hold values from -40 to 40
- kv_weight: bfloat16 [2, 8192, 8192], P('kv', 'seq', 'tensor'), may hold values from -0.0625 to 0.0625
- block_lengths: int32 [8], P('groups'), parts along dimension 0, may hold values from 1 to 96, 192 in all
- sign_bits: int32 [8192], replicated, may hold values from 0 to 1
Outputs:
- cache_rows: bfloat16 [2, 384, 8192], P('kv', ('groups', 'tensor', 'seq')), parts along dimension 1
- token_scales: float32 [2, 384], P('kv', ('groups', 'tensor', 'seq')), parts along dimension 1
There are 2 independent parts, one for each index of `groups`. A program takes and returns all parts, laid end to end along the dimension named above; an argument that names none is the same for every part. Nothing has to cross between parts.
Inputs may be any that keep to these rules, and one draw needn't show every extreme that they name: `block_lengths`: the four lengths sum to 192; the largest is exactly 96.
All inputs are finite; a program needn't handle non-finite values. Where the computation divides by a largest or mean magnitude, that divisor is 1e-20 or more.
Results may differ from a plain program's by a relative error of at most 0.001.
Values may be sent and summed in bfloat16 or wider, within the bound.
No kernel may reach another device: no remote copies, remote signals or barrier semaphores. Data moves between devices by JAX's collectives and lax.ppermute only.
A program may use at most 128 MiB of HBM per device.

v0:
```python
import jax
import jax.numpy as jnp
from jax import lax
from jax.sharding import PartitionSpec as P

HEADS = 64
HEAD = 128


def sylvester(order):
    index = jnp.arange(order, dtype=jnp.int32)
    both = jnp.bitwise_and(index[:, None], index[None, :])
    parity = jnp.zeros((order, order), jnp.int32)
    for bit in range(order.bit_length() - 1):
        parity = parity + jnp.bitwise_and(jnp.right_shift(both, bit), 1)
    return (1 - 2 * (parity % 2)).astype(jnp.float32) / jnp.sqrt(jnp.float32(order))


def positions(glob, starts):
    hits = glob[:, None] >= starts[None, :]
    start_of = jnp.max(jnp.where(hits, starts[None, :], 0), axis=1)
    return (glob - start_of).astype(jnp.float32)


def rotary(feats, place):
    half = HEAD // 2
    freq = jnp.float32(1000000.0) ** (-2.0 * jnp.arange(half, dtype=jnp.float32) / HEAD)
    angle = place[:, None] * freq[None, :]
    cosine = jnp.cos(angle)[:, None, :]
    sine = jnp.sin(angle)[:, None, :]
    first = feats[..., :half]
    second = feats[..., half:]
    return jnp.concatenate(
        [first * cosine - second * sine, second * cosine + first * sine], axis=-1
    )


def per_device(hidden_rows, kv_weight, block_lengths, sign_bits):
    tok_dev = hidden_rows.shape[0]
    columns = kv_weight.shape[2]
    heads_dev = columns // HEAD
    which = lax.axis_index("kv")
    tensor_at = lax.axis_index("tensor")
    seq_at = lax.axis_index("seq")
    seq_count = lax.axis_size("seq")
    w_full = lax.all_gather(kv_weight[0], "seq", axis=0, tiled=True)
    starts = jnp.cumsum(block_lengths) - block_lengths
    flip_all = (1 - 2 * sign_bits).astype(jnp.float32)
    flip = lax.dynamic_slice_in_dim(flip_all, tensor_at * columns, columns, 0)
    flip = flip.reshape(heads_dev, HEAD)
    inner = sylvester(HEAD)
    outer = sylvester(HEADS)
    piece = lax.all_gather(hidden_rows, "tensor", axis=0, tiled=True)
    count = piece.shape[0]
    local = jnp.arange(count, dtype=jnp.int32)
    glob = (local // tok_dev * seq_count + seq_at) * tok_dev + local % tok_dev
    place = positions(glob, starts)
    feats = jnp.dot(piece, w_full, preferred_element_type=jnp.float32).reshape(
        count, heads_dev, HEAD
    )
    feats = jnp.where(which == 0, rotary(feats, place), feats) * flip
    slab = feats.reshape(count, columns)
    mine = lax.all_to_all(slab, "tensor", split_axis=0, concat_axis=1, tiled=True)
    feats = mine.reshape(tok_dev, HEADS, HEAD)
    feats = jnp.einsum("the,ed->thd", feats, inner, precision=lax.Precision.HIGHEST)
    feats = jnp.einsum("the,hg->tge", feats, outer, precision=lax.Precision.HIGHEST)
    feats = feats.reshape(tok_dev, HEADS * HEAD)
    top = jnp.max(jnp.abs(feats), axis=1)
    cache = (feats / (top + 1e-06)[:, None]).astype(jnp.bfloat16)
    return (cache[None], top[None])


def solution(mesh):
    return jax.shard_map(
        per_device,
        mesh=mesh,
        in_specs=(P(("groups", "tensor", "seq"), None), P("kv", "seq", "tensor"), P("groups"), P()),
        out_specs=(
            P("kv", ("groups", "tensor", "seq"), None),
            P("kv", ("groups", "tensor", "seq")),
        ),
        check_vma=False,
    )
```

profile of v0, /device:TPU:0, one launch (start us, length us, event | category | flops | bytes accessed | tf_op | source)
XLA Modules:
  0.0 488.4 jit_solution(7891618701083887356)
XLA Ops:
  7.2 0.0 copy-start.1
  7.2 0.0 all-gather.4.cloned.1.call-start
  7.2 0.7 all-gather.4.cloned.1.call-update
  7.9 0.0 all-gather.6.cloned.1.call-start
  8.0 0.7 all-gather.6.cloned.1.call-update
  8.7 0.0 copy-done.1
  8.7 0.2 reduce-window.9
  8.9 0.7 fusion.40
  9.6 0.1 select_reduce_fusion
  9.7 0.2 multiply_cosine_fusion
  10.0 39.4 %all-gather.4.cloned.1.call-done = bf16[96,8192]{1,0:T(8,128)(2,1)} async-done(((bf16[24,8192]{1,0:T(8,128)(2,1)}), bf16[96,8192]{1,0:T(8,128)(2,1)}) %all-gather.4.cloned.1.call-update) | async-done | bytes 1572880 | tf_op jit(solution)/shard_map/all_gather | solution.py:53
  49.4 389.0 %all-gather.6.cloned.1.call-done = bf16[1,8192,2048]{2,1,0:T(8,128)(2,1)} async-done(((bf16[1,4096,2048]{2,1,0:T(8,128)(2,1)}), bf16[1,8192,2048]{2,1,0:T(8,128)(2,1)}) %all-gather.6.cloned.1.call-update) | async-done | bytes 33554448 | tf_op jit(solution)/shard_map/all_gather | solution.py:46
  438.4 13.8 %fusion = f32[96,2048]{1,0:T(8,128)S(1)} fusion(bf16[96,8192]{1,0:T(8,128)(2,1)} %all-gather.4.cloned.1.call-done, bf16[1,8192,2048]{2,1,0:T(8,128)(2,1)} %all-gather.6.cloned.1.call-done), kind=kOutput, calls=%fused_computation | convolution fusion | flops 3221225472 | bytes 35913728 | tf_op jit(solution)/shard_map/dot_general | solution.py:58
  452.2 0.1 copy.9
  452.3 0.3 multiply_subtract_fusion
  452.6 0.3 pad_maximum_fusion
  452.9 0.4 fusion.2
  453.3 24.5 %all_to_all.16 = f32[4,24,2048]{2,1,0:T(8,128)S(1)} all-to-all(f32[4,24,2048]{2,1,0:T(8,128)S(1)} %bitcast.32), channel_id=1, replica_groups=mesh['groups'=2,'tensor'=4,'seq'=2,'kv'=2] {'tensor'}, dimensions={0} | all-to-all | bytes 1572864 | tf_op jit(solution)/shard_map/all_to_all | solution.py:63
  477.8 0.5 copy.8
  478.3 0.4 reshape.166
  478.7 0.8 fusion.9
  479.6 1.0 abs_reduce_fusion
  480.6 0.0 copy-start
  480.6 0.1 reshape.167
  480.7 0.9 divide_convert_fusion
  481.6 0.0 copy-done
  (5 shorter events, 0.0 us)
Async XLA Ops:
  7.2 1.5 copy-start.1
  7.2 42.2 %all-gather.4.cloned.1.call-start = ((), (), s32[]{:S(2)}) async-start(), calls=%async_computation.1 | async-start | bytes 1966080 | tf_op jit(solution)/shard_map/all_gather | solution.py:53
  7.9 430.5 %all-gather.6.cloned.1.call-start = ((), (), s32[]{:S(2)}) async-start(), calls=%async_computation.2 | async-start | bytes 50331648 | tf_op jit(solution)/shard_map/all_gather | solution.py:46
  480.6 1.0 copy-start
Sparse Core Ops, SparseCore 0:
  9.6 39.7 all-gather.3
  51.0 387.4 all-gather.5
where the time goes:
time: 489 us; the launch traced here: 488 us
  waiting for transfers between devices  430 us (88%)
  blocking collectives  24.5 us (5%)
  matrix products  15.6 us (3%)
  between operations  14.1 us (3%)
    all_gather x1, waiting for transfers between devices, per_device(): w_full = lax.all_gather(kv_weight[0], 'seq', axis=0, tiled=True)  389 us
    all_gather x1, waiting for transfers between devices, per_device(): piece = lax.all_gather(hidden_rows, 'tensor', axis=0, tiled=True)  39.4 us
    all_to_all x1, blocking collectives, per_device(): lax.all_to_all(slab, 'tensor', split_axis=0, concat_axis=1, tiled=True)  24.5 us
    dot_general x1, matrix products, per_device(): jnp.dot(piece, w_full, preferred_element_type=jnp.float32)  13.8 us
  transfers between devices with their start and end apart: 2, of which 2 were waited for; matrix products, arithmetic and copies ran while one was open for 0% of the time, Pallas kernels for 0%

commit v1 on v0

v1 whole, which is shorter than its diff:
```python
import functools

import jax
import jax.numpy as jnp
from jax import lax
from jax.experimental import pallas as pl
from jax.experimental.pallas import tpu as pltpu
from jax.sharding import PartitionSpec as P

HEAD = 128
LANES = 128
FULL = 32000.0
STEPS = 64.0
TINY = 1e-30


def encode(block):
    top = jnp.max(jnp.abs(block), axis=1, keepdims=True)
    code = jnp.ceil(jnp.log2(jnp.maximum(top, TINY)) * STEPS)
    coded = jnp.round(block * (jnp.exp2(code * (-1.0 / STEPS)) * FULL))
    return coded.astype(jnp.int32).astype(jnp.int16), code


def scale_of(codes):
    return jnp.exp2(codes.astype(jnp.int32).astype(jnp.float32) * (1.0 / STEPS)) * (1.0 / FULL)


def decode(coded, scale):
    return coded.astype(jnp.int32).astype(jnp.float32) * scale


def lane_of(rows):
    return lax.broadcasted_iota(jnp.int32, (rows, LANES), 1)


def first_half(at_ref, rows_ref, w_ref, acc_ref):
    acc_ref[...] = jnp.dot(rows_ref[...], w_ref[...], preferred_element_type=jnp.float32)


def second_half(own, tile, at_ref, rows_ref, w_ref, acc_ref, keep_ref, send_ref, codes):
    step = pl.program_id(0)
    columns = keep_ref.shape[1] * pl.num_programs(0)
    total = acc_ref[...] + jnp.dot(rows_ref[...], w_ref[...], preferred_element_type=jnp.float32)
    keep_ref[...] = total[:own]
    away = total.shape[0] - own

    @pl.when(step == 0)
    def _():
        codes[...] = jnp.zeros_like(codes)

    found = codes[...]
    lane = lane_of(away)
    for head in range(tile // HEAD):
        coded, code = encode(total[own:, head * HEAD : (head + 1) * HEAD])
        send_ref[:, pl.ds(pl.multiple_of(step * tile + head * HEAD, HEAD), HEAD)] = coded
        found = jnp.where(lane == step * (tile // HEAD) + head, code, found)
    codes[...] = found

    @pl.when(step == pl.num_programs(0) - 1)
    def _():
        send_ref[:, send_ref.shape[1] - LANES :] = codes[...].astype(jnp.int32).astype(jnp.int16)


def middle(tok_dev, count, *refs):
    keep_ref, got_refs, own_ref, out_refs = refs[0], refs[1 : count], refs[count], refs[count + 1 :]
    heads = keep_ref.shape[1] // HEAD
    columns = heads * HEAD
    rows = keep_ref.shape[0]
    away = rows - tok_dev
    scales = [scale_of(ref[:, columns:]) for ref in got_refs]
    codes = jnp.zeros((away, LANES), jnp.float32)
    lane = lane_of(away)
    for head in range(heads):
        at = pl.ds(head * HEAD, HEAD)
        total = keep_ref[:, at]
        for ref, scale in zip(got_refs, scales):
            total = total + decode(ref[:, at], scale[:, head : head + 1])
        own_ref[:, at] = total[:tok_dev]
        coded, code = encode(total[tok_dev:])
        codes = jnp.where(lane == head, code, codes)
        for k, ref in enumerate(out_refs):
            ref[:, at] = coded[k * tok_dev : (k + 1) * tok_dev]
    codes = codes.astype(jnp.int32).astype(jnp.int16)
    for k, ref in enumerate(out_refs):
        ref[:, columns:] = codes[k * tok_dev : (k + 1) * tok_dev]


def butterflies(blocks):
    blocks = list(blocks)
    span = 1
    while span < len(blocks):
        for i in range(len(blocks)):
            if not i & span:
                a, b = blocks[i], blocks[i + span]
                blocks[i], blocks[i + span] = a + b, a - b
        span *= 2
    return blocks


def final(count, *refs):
    own_ref, got_refs = refs[0], refs[1:count]
    cos_ref, sin_ref, flip_ref, inner_ref, signs_ref, out_ref, top_ref, stage = refs[count:]
    tok = own_ref.shape[0]
    columns = own_ref.shape[1]
    heads = columns // HEAD
    cosine, sine, inner = cos_ref[...], sin_ref[...], inner_ref[...]
    for k in range(count):
        scale = None if k == 0 else scale_of(got_refs[k - 1][:, columns:])
        for head in range(heads):
            at = pl.ds(head * HEAD, HEAD)
            if k == 0:
                block = own_ref[:, at]
            else:
                block = decode(got_refs[k - 1][:, at], scale[:, head : head + 1])
            block = block * cosine + pltpu.roll(block, HEAD // 2, 1) * sine
            block = block * flip_ref[pl.ds(k, 1), at]
            stage[pl.ds((k * heads + head) * tok, tok), :] = block
    whole = stage[...]
    high = whole.astype(jnp.bfloat16)
    rest = whole - high.astype(jnp.float32)
    mid = rest.astype(jnp.bfloat16)
    low = (rest - mid.astype(jnp.float32)).astype(jnp.bfloat16)
    dot = functools.partial(jnp.dot, preferred_element_type=jnp.float32)
    stage[...] = dot(low, inner) + dot(mid, inner) + dot(high, inner)
    norm = 1.0 / float(HEAD * heads * count) ** 0.5
    for k in range(count):
        blocks = [stage[pl.ds((k * heads + head) * tok, tok), :] for head in range(heads)]
        for head, block in enumerate(butterflies(blocks)):
            stage[pl.ds((k * heads + head) * tok, tok), :] = block
    top = jnp.zeros((tok, HEAD), jnp.float32)
    for head in range(heads):
        blocks = [stage[pl.ds((k * heads + head) * tok, tok), :] for k in range(count)]
        for k, block in enumerate(butterflies(blocks)):
            block = block * norm
            stage[pl.ds((k * heads + head) * tok, tok), :] = block
            top = jnp.maximum(top, jnp.abs(block))
    top = jnp.max(top, axis=1, keepdims=True)
    top_ref[...] = jnp.broadcast_to(top, (tok, HEAD))
    inverse = 1.0 / (top + 1e-06)
    for k in range(count):
        factor = inverse * signs_ref[k]
        for head in range(heads):
            block = stage[pl.ds((k * heads + head) * tok, tok), :] * factor
            out_ref[:, pl.ds((k * heads + head) * HEAD, HEAD)] = block.astype(jnp.bfloat16)


def parity_signs(both, bits):
    parity = jnp.zeros_like(both)
    for bit in range(bits):
        parity = parity + jnp.bitwise_and(jnp.right_shift(both, bit), 1)
    return (1 - 2 * (parity % 2)).astype(jnp.float32)


def swap(array, axis, count, offset):
    return lax.ppermute(array, axis, [(i, i ^ offset) for i in range(count)])


def gather(block, count, at):
    if count != 4:
        return [block] + [swap(block, "tensor", count, k) for k in range(1, count)]
    two = swap(block, "tensor", count, 2)
    one = swap(block, "tensor", count, 1)
    near = lax.ppermute(block, "tensor", [(1, 2), (2, 1)])
    far = lax.ppermute(two, "tensor", [(1, 0), (2, 3)])
    inside = jnp.logical_or(at == 1, at == 2)
    return [block, one, two, jnp.where(inside, near, far)]


def per_device(hidden_rows, kv_weight, block_lengths, sign_bits):
    tok_dev, depth = hidden_rows.shape
    rows_dev, columns = kv_weight.shape[1:]
    which, tensor_at, seq_at = (lax.axis_index(name) for name in ("kv", "tensor", "seq"))
    cores, tensors, seqs = (lax.axis_size(name) for name in ("kv", "tensor", "seq"))
    heads = columns // HEAD
    weight = kv_weight[0]
    part = rows_dev // cores
    vmem = pl.BlockSpec(memory_space=pltpu.VMEM)
    big = 48 << 20

    def columns_for(seq):
        return lax.dynamic_slice_in_dim(hidden_rows, (seq * cores + which) * part, part, 1)

    pieces = gather(columns_for(seq_at), tensors, tensor_at)
    for j in range(1, seqs):
        there = jnp.bitwise_xor(seq_at, j)
        pieces += gather(swap(columns_for(there), "seq", seqs, j), tensors, tensor_at)
    mine = jnp.concatenate(pieces, axis=0)
    other = swap(mine, "kv", cores, 1)
    rows = mine.shape[0]
    own = rows // seqs
    tile = min(256, columns)
    steps = columns // tile

    def matmul(kernel, at, given, specs, outs, out_specs, scratch):
        return pl.pallas_call(
            kernel,
            grid_spec=pltpu.PrefetchScalarGridSpec(
                num_scalar_prefetch=1,
                grid=(steps,),
                in_specs=[
                    pl.BlockSpec((rows, part), lambda n, at: (0, 0)),
                    pl.BlockSpec((part, tile), lambda n, at: (at[0], n)),
                ]
                + specs,
                out_specs=out_specs,
                scratch_shapes=scratch,
            ),
            out_shape=outs,
            compiler_params=pltpu.CompilerParams(vmem_limit_bytes=big),
            cost_estimate=pl.CostEstimate(
                flops=2 * rows * part * columns, bytes_accessed=2 * part * columns, transcendentals=0
            ),
        )(at[None], *given)

    strip = pl.BlockSpec((rows, tile), lambda n, at: (0, n))
    acc = matmul(
        first_half, which, (mine, weight), [], jax.ShapeDtypeStruct((rows, columns), jnp.float32), strip, []
    )
    wide = columns + LANES
    keep, send = matmul(
        functools.partial(second_half, own, tile),
        1 - which,
        (other, weight, acc),
        [strip],
        (
            jax.ShapeDtypeStruct((own, columns), jnp.float32),
            jax.ShapeDtypeStruct((rows - own, wide), jnp.int16),
        ),
        (
            pl.BlockSpec((own, tile), lambda n, at: (0, n)),
            pl.BlockSpec((rows - own, wide), lambda n, at: (0, 0)),
        ),
        [pltpu.VMEM((rows - own, LANES), jnp.float32)],
    )
    got = [swap(send[(j - 1) * own : j * own], "seq", seqs, j) for j in range(1, seqs)]
    parts = pl.pallas_call(
        functools.partial(middle, tok_dev, seqs),
        in_specs=[vmem] * seqs,
        out_specs=[vmem] * tensors,
        out_shape=[jax.ShapeDtypeStruct((tok_dev, columns), jnp.float32)]
        + [jax.ShapeDtypeStruct((tok_dev, wide), jnp.int16)] * (tensors - 1),
        compiler_params=pltpu.CompilerParams(vmem_limit_bytes=big),
    )(keep, *got)
    blocks = [parts[0]] + [swap(parts[k], "tensor", tensors, k) for k in range(1, tensors)]

    starts = jnp.cumsum(block_lengths) - block_lengths
    glob = (tensor_at * seqs + seq_at) * tok_dev + jnp.arange(tok_dev, dtype=jnp.int32)
    hits = glob[:, None] >= starts[None, :]
    place = (glob - jnp.max(jnp.where(hits, starts[None, :], 0), axis=1)).astype(jnp.float32)
    half = HEAD // 2
    freq = jnp.float32(1000000.0) ** (-2.0 * jnp.arange(half, dtype=jnp.float32) / HEAD)
    angle = place[:, None] * freq[None, :]
    cosine = jnp.where(which == 0, jnp.cos(angle), 1.0)
    sine = jnp.where(which == 0, jnp.sin(angle), 0.0)
    cosine = jnp.concatenate([cosine, cosine], axis=1)
    sine = jnp.concatenate([-sine, sine], axis=1)
    order = jnp.bitwise_xor(jnp.arange(tensors, dtype=jnp.int32), tensor_at)
    flip = (1 - 2 * sign_bits).astype(jnp.float32).reshape(tensors, columns)[order]
    bits = (tensors - 1).bit_length()
    signs = parity_signs(jnp.bitwise_and(jnp.arange(tensors, dtype=jnp.int32), tensor_at), bits)
    index = jnp.arange(HEAD, dtype=jnp.int32)
    inner = parity_signs(jnp.bitwise_and(index[:, None], index[None, :]), 7).astype(jnp.bfloat16)

    cache, top = pl.pallas_call(
        functools.partial(final, tensors),
        in_specs=[vmem] * (tensors + 4) + [pl.BlockSpec(memory_space=pltpu.SMEM)],
        out_specs=[vmem] * 2,
        out_shape=[
            jax.ShapeDtypeStruct((tok_dev, depth), jnp.bfloat16),
            jax.ShapeDtypeStruct((tok_dev, HEAD), jnp.float32),
        ],
        scratch_shapes=[pltpu.VMEM((tensors * heads * tok_dev, HEAD), jnp.float32)],
        compiler_params=pltpu.CompilerParams(vmem_limit_bytes=big),
    )(*blocks, cosine, sine, flip, inner, signs)
    return (cache[None], top[:, 0][None])


def solution(mesh):
    return jax.shard_map(
        per_device,
        mesh=mesh,
        in_specs=(P(("groups", "tensor", "seq"), None), P("kv", "seq", "tensor"), P("groups"), P()),
        out_specs=(
            P("kv", ("groups", "tensor", "seq"), None),
            P("kv", ("groups", "tensor", "seq")),
        ),
        check_vma=False,
    )
```

time: 489 us -> 75 us (0.15)
  waiting for transfers between devices: 430 us -> 29.4 us
  blocking collectives: 24.5 us -> 0 us
  starting transfers between devices: 0.08 us -> 20.4 us
  Pallas kernels: 0 us -> 18.9 us
  matrix products: 15.6 us -> 0 us
  between operations: 14.1 us -> 0.85 us
    all_gather x2 -> x0, waiting for transfers between devices: 428 us -> none  [the longest x1 389 us: per_device(): w_full = lax.all_gather(kv_weight[0], 'seq', axis=0, tiled=True)]
    ppermute x0 -> x14, waiting for transfers between devices: none -> 29.4 us  [the longest x10 18 us: swap(): return lax.ppermute(array, axis, [(i, i ^ offset) for i in range(count)])]
    all_to_all x1 -> x0, blocking collectives: 24.5 us -> none  [per_device(): lax.all_to_all(slab, 'tensor', split_axis=0, concat_axis=1, tiled=True)]
    ppermute x0 -> x14, starting transfers between devices: none -> 20.4 us  [the longest x10 16.5 us: swap(): return lax.ppermute(array, axis, [(i, i ^ offset) for i in range(count)])]
    pallas_call x0 -> x4, Pallas kernels: none -> 18.9 us  [the longest x2 15 us: matmul(): pl.pallas_call(kernel, grid_spec=pltpu.PrefetchScalarGridSpec(num_scalar_...]
    dot_general x3 -> x0, matrix products: 15.6 us -> none  [the longest x1 13.8 us: per_device(): jnp.dot(piece, w_full, preferred_element_type=jnp.float32)]
  transfers between devices with their start and end apart: 2 -> 14, of which waited for: 2 -> 6; matrix products, arithmetic and copies ran while one was open for 0% -> 4% of each run, Pallas kernels for 0% -> 10%
where the time goes in v1:
time: 75 us; the launch traced here: 74.5 us
  waiting for transfers between devices  29.4 us (39%)
  starting transfers between devices  20.4 us (27%)
  Pallas kernels  18.9 us (25%)
  other arithmetic  2.74 us (4%)
  local copies, waits for them, and re-layouts  2.23 us (3%)
  between operations  0.85 us (1%)
    ppermute x10, waiting for transfers between devices, swap(): return lax.ppermute(array, axis, [(i, i ^ offset) for i in range(count)])  18 us
    ppermute x10, starting transfers between devices, swap(): return lax.ppermute(array, axis, [(i, i ^ offset) for i in range(count)])  16.5 us
    pallas_call x2, Pallas kernels, matmul(): pl.pallas_call(kernel, grid_spec=pltpu.PrefetchScalarGridSpec(num_scalar_...  15 us
    ppermute x2, waiting for transfers between devices, gather(): far = lax.ppermute(two, 'tensor', [(1, 0), (2, 3)])  11.4 us
    ppermute x2, starting transfers between devices, gather(): far = lax.ppermute(two, 'tensor', [(1, 0), (2, 3)])  2.58 us
    pallas_call x1, Pallas kernels, per_device(): pl.pallas_call(functools.partial(final, tensors), in_specs=[vmem] * (tens...  2.43 us
  transfers between devices with their start and end apart: 14, of which 6 were waited for; matrix products, arithmetic and copies ran while one was open for 4% of the time, Pallas kernels for 10%

profile of v1, /device:TPU:0, one launch (start us, length us, event | category | flops | bytes accessed | tf_op | source)
XLA Modules:
  0.0 74.5 jit_solution(13949260682810179593)
XLA Ops:
  0.6 1.0 %constant_dynamic-update-slice_fusion.5 = (bf16[192,2048]{1,0:T(8,128)(2,1)S(1)}, bf16[24,2048]{1,0:T(8,128)(2,1)S(1)}, bf16[24,2048]{1,0:T(8,128)(2,1)S(1)}) fusion(bf16[24,8192]{1,0:T(8,128)(2,1)} %param.4, s32[]{:T(128)S(6)} %select_n.57, s32[]{:T(128)S(6)} %select_n.60), kind=kLoop, calls=%fused_computation.19 | loop fusion | bytes 491528
  1.6 3.1 %collective-permute-start = (bf16[24,2048]{1,0:T(8,128)(2,1)S(1)}, bf16[24,2048]{1,0:T(8,128)(2,1)S(1)}, u32[]{:S(2)}, u32[]{:S(2)}) collective-permute-start(bf16[24,2048]{1,0:T(8,128)(2,1)S(1)} %get-tuple-element.19), channel_id=1, source_target_pairs={{0,4},{4,0},{8,12},{12,8},{1,5},{5,1},{9,13},{13,9},{2,6},{6,2},{1... | collective-permute-start | bytes 294920 | tf_op jit(solution)/shard_map/ppermute | solution.py:155
  4.7 2.6 %collective-permute-start.1 = (bf16[24,2048]{1,0:T(8,128)(2,1)S(1)}, bf16[24,2048]{1,0:T(8,128)(2,1)S(1)}, u32[]{:S(2)}, u32[]{:S(2)}) collective-permute-start(bf16[24,2048]{1,0:T(8,128)(2,1)S(1)} %get-tuple-element.19), channel_id=1, source_target_pairs={{0,8},{4,12},{8,0},{12,4},{1,9},{5,13},{9,1},{13,5},{2,10},{6,14},... | collective-permute-start | bytes 294920 | tf_op jit(solution)/shard_map/ppermute | solution.py:155
  7.3 0.7 collective-permute-start.2
  8.0 1.6 %collective-permute-start.4 = (bf16[24,2048]{1,0:T(8,128)(2,1)S(1)}, bf16[24,2048]{1,0:T(8,128)(2,1)S(1)}, u32[]{:S(2)}, u32[]{:S(2)}) collective-permute-start(bf16[24,2048]{1,0:T(8,128)(2,1)S(1)} %get-tuple-element.20), channel_id=1, source_target_pairs={{0,2},{2,0},{1,3},{3,1},{4,6},{6,4},{5,7},{7,5},{8,10},{10,8},{9,1... | collective-permute-start | bytes 294920 | tf_op jit(solution)/shard_map/ppermute | solution.py:155
  9.5 0.8 %reduce-window.9 = s32[4,1]{0,1:T(1,128)S(1)} reduce-window(s32[4,1]{0,1:T(1,128)} %bitcast.14, s32[]{:T(128)} %constant.24.clone.1), window={size=4x1 pad=3_0x0_0}, to_apply=%region_0.1 | reduce-window | flops 12 | bytes 36 | tf_op jit(solution)/shard_map/reduce-window.4
  10.4 0.8 %subtract_convert_fusion = f32[8192]{0:T(1024)S(1)} fusion(s32[8192]{0:T(1024)} %param.7), kind=kLoop, calls=%fused_computation.11 | loop fusion | flops 24576 | bytes 65536 | tf_op jit(solution)/shard_map/convert_element_type | solution.py:258
  11.1 0.6 gather_fusion
  11.7 0.9 %collective-permute-done.4 = bf16[24,2048]{1,0:T(8,128)(2,1)S(1)} collective-permute-done((bf16[24,2048]{1,0:T(8,128)(2,1)S(1)}, bf16[24,2048]{1,0:T(8,128)(2,1)S(1)}, u32[]{:S(2)}, u32[]{:S(2)}) %collective-permute-start.4) | collective-permute-done | bytes 98336 | tf_op jit(solution)/shard_map/ppermute | solution.py:155
  12.6 2.1 %collective-permute-start.5 = (bf16[24,2048]{1,0:T(8,128)(2,1)S(1)}, bf16[24,2048]{1,0:T(8,128)(2,1)S(1)}, u32[]{:S(2)}, u32[]{:S(2)}) collective-permute-start(bf16[24,2048]{1,0:T(8,128)(2,1)S(1)} %collective-permute-done.4), channel_id=1, source_target_pairs={{0,4},{4,0},{8,12},{12,8},{1,5},{5,1},{9,13},{13,9},{2,6},{6,2},{1... | collective-permute-start | bytes 294920 | tf_op jit(solution)/shard_map/ppermute | solution.py:155
  14.8 1.0 %collective-permute-start.6 = (bf16[24,2048]{1,0:T(8,128)(2,1)S(1)}, bf16[24,2048]{1,0:T(8,128)(2,1)S(1)}, u32[]{:S(2)}, u32[]{:S(2)}) collective-permute-start(bf16[24,2048]{1,0:T(8,128)(2,1)S(1)} %collective-permute-done.4), channel_id=1, source_target_pairs={{0,8},{4,12},{8,0},{12,4},{1,9},{5,13},{9,1},{13,5},{2,10},{6,14},... | collective-permute-start | bytes 294920 | tf_op jit(solution)/shard_map/ppermute | solution.py:155
  15.8 0.0 collective-permute-done
  15.8 0.7 collective-permute-start.7
  16.5 0.0 collective-permute-done.1
  16.5 1.3 %collective-permute-start.3 = (bf16[24,2048]{1,0:T(8,128)(2,1)S(1)}, bf16[24,2048]{1,0:T(8,128)(2,1)S(1)}, u32[]{:S(2)}, u32[]{:S(2)}) collective-permute-start(bf16[24,2048]{1,0:T(8,128)(2,1)S(1)} %collective-permute-done.1), channel_id=1, source_target_pairs={{4,0},{8,12},{5,1},{9,13},{6,2},{10,14},{7,3},{11,15},{20,16},{24,... | collective-permute-start | bytes 294920 | tf_op jit(solution)/shard_map/ppermute | solution.py:164
  17.8 0.0 collective-permute-done.2
  17.8 6.2 %collective-permute-done.3 = bf16[24,2048]{1,0:T(8,128)(2,1)S(1)} collective-permute-done((bf16[24,2048]{1,0:T(8,128)(2,1)S(1)}, bf16[24,2048]{1,0:T(8,128)(2,1)S(1)}, u32[]{:S(2)}, u32[]{:S(2)}) %collective-permute-start.3) | collective-permute-done | bytes 98336 | tf_op jit(solution)/shard_map/ppermute | solution.py:164
  24.1 0.0 collective-permute-done.6
  24.1 1.3 %collective-permute-start.8 = (bf16[24,2048]{1,0:T(8,128)(2,1)S(1)}, bf16[24,2048]{1,0:T(8,128)(2,1)S(1)}, u32[]{:S(2)}, u32[]{:S(2)}) collective-permute-start(bf16[24,2048]{1,0:T(8,128)(2,1)S(1)} %collective-permute-done.6), channel_id=1, source_target_pairs={{4,0},{8,12},{5,1},{9,13},{6,2},{10,14},{7,3},{11,15},{20,16},{24,... | collective-permute-start | bytes 294920 | tf_op jit(solution)/shard_map/ppermute | solution.py:164
  25.4 0.0 collective-permute-done.5
  25.5 0.0 collective-permute-done.7
  25.5 5.2 %collective-permute-done.8 = bf16[24,2048]{1,0:T(8,128)(2,1)S(1)} collective-permute-done((bf16[24,2048]{1,0:T(8,128)(2,1)S(1)}, bf16[24,2048]{1,0:T(8,128)(2,1)S(1)}, u32[]{:S(2)}, u32[]{:S(2)}) %collective-permute-start.8) | collective-permute-done | bytes 98336 | tf_op jit(solution)/shard_map/ppermute | solution.py:164
  30.7 0.1 collective-permute-start.9
  30.8 0.7 bitcast_subtract_fusion
  31.4 0.1 select_reduce_fusion
  31.5 7.1 %shard_map.59.acc_ref = f32[192,2048]{1,0:T(8,128)S(1)} custom-call(s32[1]{0:T(128)} %bitcast.2.at_ref, bf16[192,2048]{1,0:T(8,128)(2,1)S(1)} %select_dynamic-update-slice_fusion.rows_ref, bf16[4096,2048]{1,0:T(8,128)(2,1)} %bitcast.10), custom_call_target="tpu_custom_call" | custom-call | flops 1610612736 | bytes 8388608 | tf_op jit(solution)/shard_map/pallas_call | solution.py:195
  38.7 0.0 collective-permute-done.9.rows_ref
  38.7 7.9 %shard_map.60 = (f32[96,2048]{1,0:T(8,128)S(1)}, s16[96,2176]{1,0:T(8,128)(2,1)S(1)}) custom-call(s32[1]{0:T(128)} %bitcast.at_ref, bf16[192,2048]{1,0:T(8,128)(2,1)S(1)} %collective-permute-done.9.rows_ref, bf16[4096,2048]{1,0:T(8,128)(2,1)} %bitcast.11, f32[192,2048]{1,0:T(8,128)S(1)} %shard_map.59.acc_ref), custom_call_target="tpu_custom_call" | custom-call | flops 1610612736 | bytes 8388608 | tf_op jit(solution)/shard_map/pallas_call | solution.py:195
  46.5 1.6 %collective-permute-start.10 = (s16[96,2176]{1,0:T(8,128)(2,1)S(1)}, s16[96,2176]{1,0:T(8,128)(2,1)S(1)}, u32[]{:S(2)}, u32[]{:S(2)}) collective-permute-start(s16[96,2176]{1,0:T(8,128)(2,1)S(1)} %get-tuple-element.11), channel_id=1, source_target_pairs={{0,2},{2,0},{1,3},{3,1},{4,6},{6,4},{5,7},{7,5},{8,10},{10,8},{9,1... | collective-permute-start | bytes 1253384 | tf_op jit(solution)/shard_map/ppermute | solution.py:155
  48.1 0.1 fusion.7
  48.2 0.1 pad_maximum_fusion
  48.3 0.1 fusion.4.refs_7_
  48.4 10.2 %collective-permute-done.10.refs_1_ = s16[96,2176]{1,0:T(8,128)(2,1)S(1)} collective-permute-done((s16[96,2176]{1,0:T(8,128)(2,1)S(1)}, s16[96,2176]{1,0:T(8,128)(2,1)S(1)}, u32[]{:S(2)}, u32[]{:S(2)}) %collective-permute-start.10) | collective-permute-done | bytes 417824 | tf_op jit(solution)/shard_map/ppermute | solution.py:155
  58.6 1.5 %shard_map.61 = (f32[24,2048]{1,0:T(8,128)S(1)}, s16[24,2176]{1,0:T(8,128)(2,1)S(1)}, s16[24,2176]{1,0:T(8,128)(2,1)S(1)}, s16[24,2176]{1,0:T(8,128)(2,1)S(1)}) custom-call(f32[96,2048]{1,0:T(8,128)S(1)} %get-tuple-element.10.refs_0_, s16[96,2176]{1,0:T(8,128)(2,1)S(1)} %collective-permute-done.10.refs_1_), custom_call_target="tpu_custom_call" | custom-call | tf_op jit(solution)/shard_map/pallas_call | solution.py:236
  60.1 0.1 collective-permute-start.11
  60.2 3.0 %collective-permute-start.12 = (s16[24,2176]{1,0:T(8,128)(2,1)S(1)}, s16[24,2176]{1,0:T(8,128)(2,1)S(1)}, u32[]{:S(2)}, u32[]{:S(2)}) collective-permute-start(s16[24,2176]{1,0:T(8,128)(2,1)S(1)} %get-tuple-element.14), channel_id=1, source_target_pairs={{0,8},{4,12},{8,0},{12,4},{1,9},{5,13},{9,1},{13,5},{2,10},{6,14},... | collective-permute-start | bytes 313352 | tf_op jit(solution)/shard_map/ppermute | solution.py:155
  63.2 1.4 %collective-permute-start.13 = (s16[24,2176]{1,0:T(8,128)(2,1)S(1)}, s16[24,2176]{1,0:T(8,128)(2,1)S(1)}, u32[]{:S(2)}, u32[]{:S(2)}) collective-permute-start(s16[24,2176]{1,0:T(8,128)(2,1)S(1)} %get-tuple-element.15), channel_id=1, source_target_pairs={{0,12},{4,8},{8,4},{12,0},{1,13},{5,9},{9,5},{13,1},{2,14},{6,10},... | collective-permute-start | bytes 313352 | tf_op jit(solution)/shard_map/ppermute | solution.py:155
  64.6 1.6 %collective-permute-done.11.refs_1_ = s16[24,2176]{1,0:T(8,128)(2,1)S(1)} collective-permute-done((s16[24,2176]{1,0:T(8,128)(2,1)S(1)}, s16[24,2176]{1,0:T(8,128)(2,1)S(1)}, u32[]{:S(2)}, u32[]{:S(2)}) %collective-permute-start.11) | collective-permute-done | bytes 104480 | tf_op jit(solution)/shard_map/ppermute | solution.py:155
  66.2 5.2 %collective-permute-done.12.refs_2_ = s16[24,2176]{1,0:T(8,128)(2,1)S(1)} collective-permute-done((s16[24,2176]{1,0:T(8,128)(2,1)S(1)}, s16[24,2176]{1,0:T(8,128)(2,1)S(1)}, u32[]{:S(2)}, u32[]{:S(2)}) %collective-permute-start.12) | collective-permute-done | bytes 104480 | tf_op jit(solution)/shard_map/ppermute | solution.py:155
  71.4 0.0 collective-permute-done.13.refs_3_
  71.4 2.4 %shard_map.62 = (bf16[24,8192]{1,0:T(8,128)(2,1)}, f32[24,128]{1,0:T(8,128)S(1)}) custom-call(f32[24,2048]{1,0:T(8,128)S(1)} %get-tuple-element.12.refs_0_, s16[24,2176]{1,0:T(8,128)(2,1)S(1)} %collective-permute-done.11.refs_1_, s16[24,2176]{1,0:T(8,128)(2,1)S(1)} %collective-permute-done.12.refs_2_, s16[24,2176]{1,0:T(8,128)(2,1)S(1)} %collective-permute-done.13.refs_3_, ...), custom_call_target="tpu_custom_call" | custom-call | tf_op jit(solution)/shard_map/pallas_call | solution.py:264
  73.8 0.6 slice_reduce_fusion
  (14 shorter events, 0.2 us)
Async XLA Ops:
  1.6 14.2 %collective-permute-start = (bf16[24,2048]{1,0:T(8,128)(2,1)S(1)}, bf16[24,2048]{1,0:T(8,128)(2,1)S(1)}, u32[]{:S(2)}, u32[]{:S(2)}) collective-permute-start(bf16[24,2048]{1,0:T(8,128)(2,1)S(1)} %get-tuple-element.19), channel_id=1, source_target_pairs={{0,4},{4,0},{8,12},{12,8},{1,5},{5,1},{9,13},{13,9},{2,6},{6,2},{1... | collective-permute-start | bytes 294920 | tf_op jit(solution)/shard_map/ppermute | solution.py:155
  4.7 11.8 %collective-permute-start.1 = (bf16[24,2048]{1,0:T(8,128)(2,1)S(1)}, bf16[24,2048]{1,0:T(8,128)(2,1)S(1)}, u32[]{:S(2)}, u32[]{:S(2)}) collective-permute-start(bf16[24,2048]{1,0:T(8,128)(2,1)S(1)} %get-tuple-element.19), channel_id=1, source_target_pairs={{0,8},{4,12},{8,0},{12,4},{1,9},{5,13},{9,1},{13,5},{2,10},{6,14},... | collective-permute-start | bytes 294920 | tf_op jit(solution)/shard_map/ppermute | solution.py:155
  7.3 10.5 %collective-permute-start.2 = (bf16[24,2048]{1,0:T(8,128)(2,1)S(1)}, bf16[24,2048]{1,0:T(8,128)(2,1)S(1)}, u32[]{:S(2)}, u32[]{:S(2)}) collective-permute-start(bf16[24,2048]{1,0:T(8,128)(2,1)S(1)} %get-tuple-element.19), channel_id=1, source_target_pairs={{4,8},{8,4},{5,9},{9,5},{6,10},{10,6},{7,11},{11,7},{20,24},{24,20... | collective-permute-start | bytes 294920 | tf_op jit(solution)/shard_map/ppermute | solution.py:163
  8.0 4.7 %collective-permute-start.4 = (bf16[24,2048]{1,0:T(8,128)(2,1)S(1)}, bf16[24,2048]{1,0:T(8,128)(2,1)S(1)}, u32[]{:S(2)}, u32[]{:S(2)}) collective-permute-start(bf16[24,2048]{1,0:T(8,128)(2,1)S(1)} %get-tuple-element.20), channel_id=1, source_target_pairs={{0,2},{2,0},{1,3},{3,1},{4,6},{6,4},{5,7},{7,5},{8,10},{10,8},{9,1... | collective-permute-start | bytes 294920 | tf_op jit(solution)/shard_map/ppermute | solution.py:155
  12.6 12.8 %collective-permute-start.5 = (bf16[24,2048]{1,0:T(8,128)(2,1)S(1)}, bf16[24,2048]{1,0:T(8,128)(2,1)S(1)}, u32[]{:S(2)}, u32[]{:S(2)}) collective-permute-start(bf16[24,2048]{1,0:T(8,128)(2,1)S(1)} %collective-permute-done.4), channel_id=1, source_target_pairs={{0,4},{4,0},{8,12},{12,8},{1,5},{5,1},{9,13},{13,9},{2,6},{6,2},{1... | collective-permute-start | bytes 294920 | tf_op jit(solution)/shard_map/ppermute | solution.py:155
  14.8 9.3 %collective-permute-start.6 = (bf16[24,2048]{1,0:T(8,128)(2,1)S(1)}, bf16[24,2048]{1,0:T(8,128)(2,1)S(1)}, u32[]{:S(2)}, u32[]{:S(2)}) collective-permute-start(bf16[24,2048]{1,0:T(8,128)(2,1)S(1)} %collective-permute-done.4), channel_id=1, source_target_pairs={{0,8},{4,12},{8,0},{12,4},{1,9},{5,13},{9,1},{13,5},{2,10},{6,14},... | collective-permute-start | bytes 294920 | tf_op jit(solution)/shard_map/ppermute | solution.py:155
  15.8 9.7 %collective-permute-start.7 = (bf16[24,2048]{1,0:T(8,128)(2,1)S(1)}, bf16[24,2048]{1,0:T(8,128)(2,1)S(1)}, u32[]{:S(2)}, u32[]{:S(2)}) collective-permute-start(bf16[24,2048]{1,0:T(8,128)(2,1)S(1)} %collective-permute-done.4), channel_id=1, source_target_pairs={{4,8},{8,4},{5,9},{9,5},{6,10},{10,6},{7,11},{11,7},{20,24},{24,20... | collective-permute-start | bytes 294920 | tf_op jit(solution)/shard_map/ppermute | solution.py:163
  16.5 7.6 %collective-permute-start.3 = (bf16[24,2048]{1,0:T(8,128)(2,1)S(1)}, bf16[24,2048]{1,0:T(8,128)(2,1)S(1)}, u32[]{:S(2)}, u32[]{:S(2)}) collective-permute-start(bf16[24,2048]{1,0:T(8,128)(2,1)S(1)} %collective-permute-done.1), channel_id=1, source_target_pairs={{4,0},{8,12},{5,1},{9,13},{6,2},{10,14},{7,3},{11,15},{20,16},{24,... | collective-permute-start | bytes 294920 | tf_op jit(solution)/shard_map/ppermute | solution.py:164
  24.1 6.5 %collective-permute-start.8 = (bf16[24,2048]{1,0:T(8,128)(2,1)S(1)}, bf16[24,2048]{1,0:T(8,128)(2,1)S(1)}, u32[]{:S(2)}, u32[]{:S(2)}) collective-permute-start(bf16[24,2048]{1,0:T(8,128)(2,1)S(1)} %collective-permute-done.6), channel_id=1, source_target_pairs={{4,0},{8,12},{5,1},{9,13},{6,2},{10,14},{7,3},{11,15},{20,16},{24,... | collective-permute-start | bytes 294920 | tf_op jit(solution)/shard_map/ppermute | solution.py:164
  30.7 8.0 %collective-permute-start.9 = (bf16[192,2048]{1,0:T(8,128)(2,1)S(1)}, bf16[192,2048]{1,0:T(8,128)(2,1)S(1)}, u32[]{:S(2)}, u32[]{:S(2)}) collective-permute-start(bf16[192,2048]{1,0:T(8,128)(2,1)S(1)} %select_dynamic-update-slice_fusion.rows_ref), channel_id=1, source_target_pairs={{0,1},{1,0},{2,3},{3,2},{4,5},{5,4},{6,7},{7,6},{8,9},{9,8},{10,11... | collective-permute-start | bytes 2359304 | tf_op jit(solution)/shard_map/ppermute | solution.py:155
  46.5 12.1 %collective-permute-start.10 = (s16[96,2176]{1,0:T(8,128)(2,1)S(1)}, s16[96,2176]{1,0:T(8,128)(2,1)S(1)}, u32[]{:S(2)}, u32[]{:S(2)}) collective-permute-start(s16[96,2176]{1,0:T(8,128)(2,1)S(1)} %get-tuple-element.11), channel_id=1, source_target_pairs={{0,2},{2,0},{1,3},{3,1},{4,6},{6,4},{5,7},{7,5},{8,10},{10,8},{9,1... | collective-permute-start | bytes 1253384 | tf_op jit(solution)/shard_map/ppermute | solution.py:155
  60.1 6.1 %collective-permute-start.11 = (s16[24,2176]{1,0:T(8,128)(2,1)S(1)}, s16[24,2176]{1,0:T(8,128)(2,1)S(1)}, u32[]{:S(2)}, u32[]{:S(2)}) collective-permute-start(s16[24,2176]{1,0:T(8,128)(2,1)S(1)} %get-tuple-element.13), channel_id=1, source_target_pairs={{0,4},{4,0},{8,12},{12,8},{1,5},{5,1},{9,13},{13,9},{2,6},{6,2},{1... | collective-permute-start | bytes 313352 | tf_op jit(solution)/shard_map/ppermute | solution.py:155
  60.2 11.2 %collective-permute-start.12 = (s16[24,2176]{1,0:T(8,128)(2,1)S(1)}, s16[24,2176]{1,0:T(8,128)(2,1)S(1)}, u32[]{:S(2)}, u32[]{:S(2)}) collective-permute-start(s16[24,2176]{1,0:T(8,128)(2,1)S(1)} %get-tuple-element.14), channel_id=1, source_target_pairs={{0,8},{4,12},{8,0},{12,4},{1,9},{5,13},{9,1},{13,5},{2,10},{6,14},... | collective-permute-start | bytes 313352 | tf_op jit(solution)/shard_map/ppermute | solution.py:155
  63.2 8.2 %collective-permute-start.13 = (s16[24,2176]{1,0:T(8,128)(2,1)S(1)}, s16[24,2176]{1,0:T(8,128)(2,1)S(1)}, u32[]{:S(2)}, u32[]{:S(2)}) collective-permute-start(s16[24,2176]{1,0:T(8,128)(2,1)S(1)} %get-tuple-element.15), channel_id=1, source_target_pairs={{0,12},{4,8},{8,4},{12,0},{1,13},{5,9},{9,5},{13,1},{2,14},{6,10},... | collective-permute-start | bytes 313352 | tf_op jit(solution)/shard_map/ppermute | solution.py:155

commit v2 on v1

v2 whole, which is shorter than its diff:
```python
import functools

import jax
import jax.numpy as jnp
from jax import lax
from jax.experimental import pallas as pl
from jax.experimental.pallas import tpu as pltpu
from jax.sharding import PartitionSpec as P

HEAD = 128
LANES = 128
FULL = 32000.0
STEPS = 64.0
TINY = 1e-30


def encode(block):
    top = jnp.max(jnp.abs(block), axis=1, keepdims=True)
    code = jnp.ceil(jnp.log2(jnp.maximum(top, TINY)) * STEPS)
    coded = jnp.round(block * (jnp.exp2(code * (-1.0 / STEPS)) * FULL))
    return coded.astype(jnp.int32).astype(jnp.int16), code


def scale_of(codes):
    return jnp.exp2(codes.astype(jnp.int32).astype(jnp.float32) * (1.0 / STEPS)) * (1.0 / FULL)


def decode(coded, scale):
    return coded.astype(jnp.int32).astype(jnp.float32) * scale


def lane_of(rows):
    return lax.broadcasted_iota(jnp.int32, (rows, LANES), 1)


def load(offset, pieces, w_ref, out_ref, sems):
    rows = out_ref.shape[0]
    index = lax.rem(lax.axis_index("kv") + offset, lax.axis_size("kv"))
    piece = rows // pieces
    copies = []
    for i in range(pieces):
        start = pl.multiple_of(index * rows + i * piece, piece)
        copies.append(
            pltpu.make_async_copy(w_ref.at[pl.ds(start, piece)], out_ref.at[pl.ds(i * piece, piece)], sems.at[i])
        )
    for copy in copies:
        copy.start()
    for copy in copies:
        copy.wait()


def first_half(tile, rows_ref, w_ref, acc_ref):
    for first in range(0, acc_ref.shape[1], tile):
        at = slice(first, first + tile)
        acc_ref[:, at] = jnp.dot(rows_ref[...], w_ref[:, at], preferred_element_type=jnp.float32)


def second_half(begin, tile, rows_ref, w_ref, acc_ref, keep_ref, send_ref):
    own, width = keep_ref.shape
    away = send_ref.shape[0]
    codes = jnp.zeros((away, LANES), jnp.float32)
    lane = lane_of(away)
    for first in range(0, width, tile):
        at = slice(begin + first, begin + first + tile)
        total = acc_ref[:, at] + jnp.dot(rows_ref[...], w_ref[:, at], preferred_element_type=jnp.float32)
        keep_ref[:, first : first + tile] = total[:own]
        for head in range(tile // HEAD):
            coded, code = encode(total[own:, head * HEAD : (head + 1) * HEAD])
            send_ref[:, first + head * HEAD : first + (head + 1) * HEAD] = coded
            codes = jnp.where(lane == first // HEAD + head, code, codes)
    send_ref[:, width:] = codes.astype(jnp.int32).astype(jnp.int16)


def middle(tok_dev, count, *refs):
    keep_ref, got_refs, own_ref, out_refs = refs[0], refs[1 : count], refs[count], refs[count + 1 :]
    heads = keep_ref.shape[1] // HEAD
    columns = heads * HEAD
    rows = keep_ref.shape[0]
    away = rows - tok_dev
    scales = [scale_of(ref[:, columns:]) for ref in got_refs]
    codes = jnp.zeros((away, LANES), jnp.float32)
    lane = lane_of(away)
    for head in range(heads):
        at = pl.ds(head * HEAD, HEAD)
        total = keep_ref[:, at]
        for ref, scale in zip(got_refs, scales):
            total = total + decode(ref[:, at], scale[:, head : head + 1])
        own_ref[:, at] = total[:tok_dev]
        coded, code = encode(total[tok_dev:])
        codes = jnp.where(lane == head, code, codes)
        for k, ref in enumerate(out_refs):
            ref[:, at] = coded[k * tok_dev : (k + 1) * tok_dev]
    codes = codes.astype(jnp.int32).astype(jnp.int16)
    for k, ref in enumerate(out_refs):
        ref[:, columns:] = codes[k * tok_dev : (k + 1) * tok_dev]


def butterflies(blocks):
    blocks = list(blocks)
    span = 1
    while span < len(blocks):
        for i in range(len(blocks)):
            if not i & span:
                a, b = blocks[i], blocks[i + span]
                blocks[i], blocks[i + span] = a + b, a - b
        span *= 2
    return blocks


def parity_signs(both, bits):
    parity = jnp.zeros_like(both)
    for bit in range(bits):
        parity = parity + jnp.bitwise_and(jnp.right_shift(both, bit), 1)
    return (1 - 2 * jnp.bitwise_and(parity, 1)).astype(jnp.float32)


def final(count, chunks, *refs):
    block_refs = refs[: count * chunks]
    cos_ref, sin_ref, bits_ref, out_ref, top_ref, stage = refs[count * chunks :]
    tok, width = block_refs[0].shape
    per_chunk = width // HEAD
    heads = per_chunk * chunks
    columns = heads * HEAD
    bits = (count - 1).bit_length()
    tensor_at = lax.axis_index("tensor")
    cosine, sine = cos_ref[...], sin_ref[...]
    both = lax.broadcasted_iota(jnp.int32, (HEAD, HEAD), 0) & lax.broadcasted_iota(jnp.int32, (HEAD, HEAD), 1)
    inner = parity_signs(both, 7).astype(jnp.bfloat16)
    for k in range(count):
        there = pl.multiple_of(jnp.bitwise_xor(tensor_at, k) * columns, HEAD)
        flip = (1 - 2 * bits_ref[:, pl.ds(there, columns)]).astype(jnp.float32)
        for chunk in range(chunks):
            ref = block_refs[chunk * count + k]
            scale = None if k == 0 else scale_of(ref[:, width:])
            for head in range(per_chunk):
                block = ref[:, head * HEAD : (head + 1) * HEAD]
                if k:
                    block = decode(block, scale[:, head : head + 1])
                at = chunk * per_chunk + head
                block = block * cosine + pltpu.roll(block, HEAD // 2, 1) * sine
                block = block * flip[:, at * HEAD : (at + 1) * HEAD]
                stage[pl.ds((k * heads + at) * tok, tok), :] = block
    whole = stage[...]
    high = whole.astype(jnp.bfloat16)
    rest = whole - high.astype(jnp.float32)
    mid = rest.astype(jnp.bfloat16)
    low = (rest - mid.astype(jnp.float32)).astype(jnp.bfloat16)
    dot = functools.partial(jnp.dot, preferred_element_type=jnp.float32)
    stage[...] = dot(low, inner) + dot(mid, inner) + dot(high, inner)
    norm = 1.0 / float(HEAD * heads * count) ** 0.5
    for k in range(count):
        blocks = [stage[pl.ds((k * heads + head) * tok, tok), :] for head in range(heads)]
        for head, block in enumerate(butterflies(blocks)):
            stage[pl.ds((k * heads + head) * tok, tok), :] = block
    top = jnp.zeros((tok, HEAD), jnp.float32)
    for head in range(heads):
        blocks = [stage[pl.ds((k * heads + head) * tok, tok), :] for k in range(count)]
        for k, block in enumerate(butterflies(blocks)):
            block = block * norm
            stage[pl.ds((k * heads + head) * tok, tok), :] = block
            top = jnp.maximum(top, jnp.abs(block))
    top = jnp.max(top, axis=1, keepdims=True)
    row = lax.broadcasted_iota(jnp.int32, (tok, HEAD), 0)
    line = jnp.sum(jnp.where(row == lane_of(tok), top, 0.0), axis=0, keepdims=True)
    top_ref[...] = line[:, :tok]
    inverse = 1.0 / (top + 1e-06)
    for k in range(count):
        factor = inverse * parity_signs(jnp.bitwise_and(tensor_at, k), bits)
        for head in range(heads):
            block = stage[pl.ds((k * heads + head) * tok, tok), :] * factor
            out_ref[:, pl.ds((k * heads + head) * HEAD, HEAD)] = block.astype(jnp.bfloat16)


def swap(array, axis, count, offset):
    return lax.ppermute(array, axis, [(i, i ^ offset) for i in range(count)])


def gather(own, others, count):
    if count != 4:
        pieces = []
        for block in [own] + others:
            pieces += [block] + [swap(block, "tensor", count, k) for k in range(1, count)]
        return jnp.concatenate(pieces, axis=0)
    tok = own.shape[0]
    mine = jnp.concatenate([own] + others, axis=0)
    two = [swap(own, "tensor", count, 2), swap(mine[tok:], "tensor", count, 2)]
    two = jnp.concatenate(two, axis=0)
    one = swap(mine, "tensor", count, 1)
    near = lax.ppermute(mine, "tensor", [(1, 2), (2, 1)])
    far = lax.ppermute(two, "tensor", [(1, 0), (2, 3)])
    blocks = jnp.stack([mine, one, two, near + far])
    blocks = blocks.reshape(count, 1 + len(others), tok, own.shape[1])
    return jnp.swapaxes(blocks, 0, 1).reshape(-1, own.shape[1])


def per_device(hidden_rows, kv_weight, block_lengths, sign_bits):
    tok_dev, depth = hidden_rows.shape
    rows_dev, columns = kv_weight.shape[1:]
    which, tensor_at, seq_at = (lax.axis_index(name) for name in ("kv", "tensor", "seq"))
    cores, tensors, seqs = (lax.axis_size(name) for name in ("kv", "tensor", "seq"))
    weight = kv_weight[0]
    part = rows_dev // cores
    vmem = pl.BlockSpec(memory_space=pltpu.VMEM)
    chunks = 2 if columns >= 1024 else 1
    width = columns // chunks
    heads = columns // HEAD

    def local(kernel, outs, in_specs, limit, scratch=(), flops=0, moved=0):
        return pl.pallas_call(
            kernel,
            in_specs=in_specs,
            out_specs=jax.tree.map(lambda _: vmem, outs),
            out_shape=outs,
            scratch_shapes=scratch,
            compiler_params=pltpu.CompilerParams(vmem_limit_bytes=limit << 20),
            cost_estimate=pl.CostEstimate(flops=flops, bytes_accessed=moved, transcendentals=0),
        )

    index = jnp.arange(block_lengths.shape[0], dtype=jnp.int32)
    starts = jnp.sum(jnp.where(index[:, None] < index[None, :], block_lengths[:, None], 0), axis=0)
    glob = (tensor_at * seqs + seq_at) * tok_dev + jnp.arange(tok_dev, dtype=jnp.int32)
    hits = glob[:, None] >= starts[None, :]
    place = (glob - jnp.max(jnp.where(hits, starts[None, :], 0), axis=1)).astype(jnp.float32)
    freq = jnp.float32(1000000.0) ** (-2.0 * jnp.arange(HEAD // 2, dtype=jnp.float32) / HEAD)
    angle = place[:, None] * freq[None, :]
    cosine = jnp.where(which == 0, jnp.cos(angle), 1.0)
    sine = jnp.where(which == 0, jnp.sin(angle), 0.0)
    cosine = jnp.concatenate([cosine, cosine], axis=1)
    sine = jnp.concatenate([-sine, sine], axis=1)
    weight, cosine, sine = lax.optimization_barrier((weight, cosine, sine))

    halves = [
        local(
            functools.partial(load, offset, 8),
            pltpu.VMEM((part, columns), weight.dtype),
            [pl.BlockSpec(memory_space=pltpu.HBM)],
            4,
            [pltpu.SemaphoreType.DMA((8,))],
            moved=4 * part * columns,
        )(pltpu.with_memory_space_constraint(weight, pltpu.HBM))
        for offset in range(cores)
    ]

    def columns_for(seq):
        return lax.dynamic_slice_in_dim(hidden_rows, (seq * cores + which) * part, part, 1)

    others = [swap(columns_for(jnp.bitwise_xor(seq_at, j)), "seq", seqs, j) for j in range(1, seqs)]
    mine = gather(columns_for(seq_at), others, tensors)
    mine, *halves = lax.optimization_barrier((mine, *halves))
    other = swap(mine, "kv", cores, 1)
    rows = mine.shape[0]
    own = rows // seqs
    tile = min(256, width)
    limit = 8 if rows < 1024 else 24
    wide = width + LANES
    acc = local(
        functools.partial(first_half, tile),
        jax.ShapeDtypeStruct((rows, columns), jnp.float32),
        [vmem, vmem],
        limit,
        flops=2 * rows * part * columns,
        moved=4 * rows * columns,
    )(mine, pltpu.with_memory_space_constraint(halves[0], pltpu.VMEM))
    blocks = []
    for chunk in range(chunks):
        keep, send = local(
            functools.partial(second_half, chunk * width, tile),
            [
                jax.ShapeDtypeStruct((own, width), jnp.float32),
                jax.ShapeDtypeStruct((rows - own, wide), jnp.int16),
            ],
            [vmem, vmem, vmem],
            limit,
            flops=2 * rows * part * width,
            moved=8 * rows * width,
        )(other, pltpu.with_memory_space_constraint(halves[1], pltpu.VMEM), acc)
        got = [swap(send[(j - 1) * own : j * own], "seq", seqs, j) for j in range(1, seqs)]
        parts = local(
            functools.partial(middle, tok_dev, seqs),
            [jax.ShapeDtypeStruct((tok_dev, width), jnp.float32)]
            + [jax.ShapeDtypeStruct((tok_dev, wide), jnp.int16)] * (tensors - 1),
            [vmem] * seqs,
            limit,
            moved=8 * own * width,
        )(keep, *got)
        blocks += [parts[0]] + [swap(parts[k], "tensor", tensors, k) for k in range(1, tensors)]

    cache, top = local(
        functools.partial(final, tensors, chunks),
        [
            jax.ShapeDtypeStruct((tok_dev, depth), jnp.bfloat16),
            jax.ShapeDtypeStruct((1, tok_dev), jnp.float32),
        ],
        [vmem] * (tensors * chunks + 3),
        32,
        [pltpu.VMEM((tensors * heads * tok_dev, HEAD), jnp.float32)],
    )(*blocks, cosine, sine, sign_bits[None])
    return (cache[None], top)


def solution(mesh):
    return jax.shard_map(
        per_device,
        mesh=mesh,
        in_specs=(P(("groups", "tensor", "seq"), None), P("kv", "seq", "tensor"), P("groups"), P()),
        out_specs=(
            P("kv", ("groups", "tensor", "seq"), None),
            P("kv", ("groups", "tensor", "seq")),
        ),
        check_vma=False,
    )
```

time: 75 us -> 59.8 us (0.80)
  waiting for transfers between devices: 29.4 us -> 18.1 us
  Pallas kernels: 18.9 us -> 14.7 us
  starting transfers between devices: 20.4 us -> 23.9 us
  other arithmetic: 2.74 us -> 1.22 us
  local copies, waits for them, and re-layouts: 2.23 us -> 0.98 us
    ppermute x2 -> x1, waiting for transfers between devices: 11.4 us -> 0.01 us  [gather(): far = lax.ppermute(two, 'tensor', [(1, 0), (2, 3)])]
    ppermute x10 -> x13, starting transfers between devices: 16.5 us -> 21.9 us  [swap(): return lax.ppermute(array, axis, [(i, i ^ offset) for i in range(count)])]
    pallas_call x4 -> x8, Pallas kernels: 18.9 us -> 14.7 us  [the longest x2 6.96 us: per_device(): local(functools.partial(load, offset, 8), pltpu.VMEM((part, columns), wei...]
    ppermute x2 -> x1, starting transfers between devices: 2.58 us -> 1.29 us  [gather(): far = lax.ppermute(two, 'tensor', [(1, 0), (2, 3)])]
    unnamed x6 -> x3, local copies, waits for them, and re-layouts: 1.01 us -> 0.01 us
    dynamic_slice x0 -> x1, local copies, waits for them, and re-layouts: none -> 0.96 us  [columns_for(): lax.dynamic_slice_in_dim(hidden_rows, (seq * cores + which) * part, part, 1)]
    convert_element_type x3 -> x0, other arithmetic: 0.87 us -> none  [the longest x1 0.76 us: per_device(): (1 - 2 * sign_bits).astype(jnp.float32).reshape(tensors, columns)[order]]
    ppermute x10 -> x13, waiting for transfers between devices: 18 us -> 18.1 us  [swap(): return lax.ppermute(array, axis, [(i, i ^ offset) for i in range(count)])]
  transfers between devices with their start and end apart: 14 -> 15, of which waited for: 6 -> 7; matrix products, arithmetic and copies ran while one was open for 4% -> 2% of each run, Pallas kernels for 10% -> 19%
where the time goes in v2:
time: 59.8 us; the launch traced here: 59.6 us
  starting transfers between devices  23.9 us (40%)
  waiting for transfers between devices  18.1 us (30%)
  Pallas kernels  14.7 us (25%)
  other arithmetic  1.22 us (2%)
  local copies, waits for them, and re-layouts  0.98 us (2%)
  between operations  0.82 us (1%)
    ppermute x13, starting transfers between devices, swap(): return lax.ppermute(array, axis, [(i, i ^ offset) for i in range(count)])  21.9 us
    ppermute x13, waiting for transfers between devices, swap(): return lax.ppermute(array, axis, [(i, i ^ offset) for i in range(count)])  18.1 us
    pallas_call x2, Pallas kernels, per_device(): local(functools.partial(load, offset, 8), pltpu.VMEM((part, columns), wei...  6.96 us
    pallas_call x2, Pallas kernels, per_device(): local(functools.partial(second_half, chunk * width, tile), [jax.ShapeDtyp...  2.4 us
    pallas_call x1, Pallas kernels, per_device(): local(functools.partial(final, tensors, chunks), [jax.ShapeDtypeStruct((t...  2.04 us
    pallas_call x1, Pallas kernels, per_device(): local(functools.partial(first_half, tile), jax.ShapeDtypeStruct((rows, co...  1.84 us
    pallas_call x2, Pallas kernels, per_device(): local(functools.partial(middle, tok_dev, seqs), [jax.ShapeDtypeStruct((to...  1.41 us
    ppermute x1, starting transfers between devices, gather(): far = lax.ppermute(two, 'tensor', [(1, 0), (2, 3)])  1.29 us
  transfers between devices with their start and end apart: 15, of which 7 were waited for; matrix products, arithmetic and copies ran while one was open for 2% of the time, Pallas kernels for 19%

profile of v2, /device:TPU:0, one launch (start us, length us, event | category | flops | bytes accessed | tf_op | source)
XLA Modules:
  0.0 59.6 jit_solution(11642344461390971024)
XLA Ops:
  0.6 1.0 %constant_dynamic-slice_fusion.1 = (bf16[24,2048]{1,0:T(8,128)(2,1)S(1)}, bf16[24,2048]{1,0:T(8,128)(2,1)S(1)}) fusion(bf16[24,8192]{1,0:T(8,128)(2,1)} %param.4, s32[]{:T(128)S(6)} %select_n.26, s32[]{:T(128)S(6)} %select_n.27), kind=kLoop, calls=%fused_computation.18 | loop fusion | bytes 393224 | tf_op jit(solution)/shard_map/dynamic_slice | solution.py:245
  1.6 3.0 %collective-permute-start = (bf16[24,2048]{1,0:T(8,128)(2,1)S(1)}, bf16[24,2048]{1,0:T(8,128)(2,1)S(1)}, u32[]{:S(2)}, u32[]{:S(2)}) collective-permute-start(bf16[24,2048]{1,0:T(8,128)(2,1)S(1)} %get-tuple-element.43), channel_id=1, source_target_pairs={{0,2},{2,0},{1,3},{3,1},{4,6},{6,4},{5,7},{7,5},{8,10},{10,8},{9,1... | collective-permute-start | bytes 294920 | tf_op jit(solution)/shard_map/ppermute | solution.py:175
  4.6 2.6 %collective-permute-start.2 = (bf16[24,2048]{1,0:T(8,128)(2,1)S(1)}, bf16[24,2048]{1,0:T(8,128)(2,1)S(1)}, u32[]{:S(2)}, u32[]{:S(2)}) collective-permute-start(bf16[24,2048]{1,0:T(8,128)(2,1)S(1)} %get-tuple-element.42), channel_id=1, source_target_pairs={{0,8},{4,12},{8,0},{12,4},{1,9},{5,13},{9,1},{13,5},{2,10},{6,14},... | collective-permute-start | bytes 294920 | tf_op jit(solution)/shard_map/ppermute | solution.py:175
  7.2 0.7 %select_reduce_fusion.1 = s32[4]{0:T(128)S(1)} fusion(s32[4]{0:T(128)} %param.6), kind=kLoop, calls=%fused_computation.12 | loop fusion | flops 44 | bytes 32 | tf_op jit(solution)/shard_map/reduce_sum | solution.py:220
  7.9 0.1 select_reduce_fusion
  8.1 0.0 collective-permute-done
  8.1 0.7 %collective-permute-start.4 = (bf16[48,2048]{1,0:T(8,128)(2,1)S(1)}, bf16[48,2048]{1,0:T(8,128)(2,1)S(1)}, u32[]{:S(2)}, u32[]{:S(2)}) collective-permute-start(bf16[48,2048]{1,0:T(8,128)(2,1)S(1)} %pad_maximum_fusion.1), channel_id=1, source_target_pairs={{4,8},{8,4},{5,9},{9,5},{6,10},{10,6},{7,11},{11,7},{20,24},{24,20... | collective-permute-start | bytes 589832 | tf_op jit(solution)/shard_map/ppermute | solution.py:189
  8.8 4.1 %collective-permute-start.1 = (bf16[48,2048]{1,0:T(8,128)(2,1)S(1)}, bf16[48,2048]{1,0:T(8,128)(2,1)S(1)}, u32[]{:S(2)}, u32[]{:S(2)}) collective-permute-start(bf16[48,2048]{1,0:T(8,128)(2,1)S(1)} %pad_maximum_fusion.1), channel_id=1, source_target_pairs={{0,4},{4,0},{8,12},{12,8},{1,5},{5,1},{9,13},{13,9},{2,6},{6,2},{1... | collective-permute-start | bytes 589832 | tf_op jit(solution)/shard_map/ppermute | solution.py:175
  12.9 0.3 collective-permute-start.3
  13.2 0.0 collective-permute-done.2
  13.2 8.1 %collective-permute-done.3 = bf16[24,2048]{1,0:T(8,128)(2,1)S(1)} collective-permute-done((bf16[24,2048]{1,0:T(8,128)(2,1)S(1)}, bf16[24,2048]{1,0:T(8,128)(2,1)S(1)}, u32[]{:S(2)}, u32[]{:S(2)}) %collective-permute-start.3) | collective-permute-done | bytes 98336 | tf_op jit(solution)/shard_map/ppermute | solution.py:175
  21.3 1.3 %collective-permute-start.5 = (bf16[48,2048]{1,0:T(8,128)(2,1)S(1)}, bf16[48,2048]{1,0:T(8,128)(2,1)S(1)}, u32[]{:S(2)}, u32[]{:S(2)}) collective-permute-start(bf16[48,2048]{1,0:T(8,128)(2,1)S(1)} %constant_dynamic-update-slice_fusion), channel_id=1, source_target_pairs={{4,0},{8,12},{5,1},{9,13},{6,2},{10,14},{7,3},{11,15},{20,16},{24,... | collective-permute-start | bytes 589832 | tf_op jit(solution)/shard_map/ppermute | solution.py:190
  22.6 0.1 fusion.2
  22.7 0.1 pad_maximum_fusion.2
  22.8 3.5 %shard_map.60.w_ref = bf16[2048,2048]{1,0:T(8,128)(2,1)S(1)} custom-call(bf16[4096,2048]{1,0:T(8,128)(2,1)} %bitcast.21), custom_call_target="tpu_custom_call" | custom-call | bytes 16777216 | tf_op jit(solution)/shard_map/pallas_call | solution.py:233
  26.3 3.5 %shard_map.59.w_ref = bf16[2048,2048]{1,0:T(8,128)(2,1)S(1)} custom-call(bf16[4096,2048]{1,0:T(8,128)(2,1)} %bitcast.22), custom_call_target="tpu_custom_call" | custom-call | bytes 16777216 | tf_op jit(solution)/shard_map/pallas_call | solution.py:233
  29.8 0.0 collective-permute-done.4
  29.8 0.0 collective-permute-done.5
  29.9 0.0 collective-permute-done.1
  29.9 0.1 pad_maximum_fusion
  30.0 0.1 collective-permute-start.6
  30.1 1.8 %shard_map.61.acc_ref = f32[192,2048]{1,0:T(8,128)S(1)} custom-call(bf16[192,2048]{1,0:T(8,128)(2,1)S(1)} %bitcast.19, bf16[2048,2048]{1,0:T(8,128)(2,1)S(1)} %shard_map.59.w_ref), custom_call_target="tpu_custom_call" | custom-call | flops 1610612736 | bytes 1572864 | tf_op jit(solution)/shard_map/pallas_call | solution.py:256
  31.9 0.4 collective-permute-done.6.rows_ref
  32.3 1.2 %shard_map.64 = (f32[96,1024]{1,0:T(8,128)S(1)}, s16[96,1152]{1,0:T(8,128)(2,1)S(1)}) custom-call(bf16[192,2048]{1,0:T(8,128)(2,1)S(1)} %collective-permute-done.6.rows_ref, bf16[2048,2048]{1,0:T(8,128)(2,1)S(1)} %shard_map.60.w_ref, f32[192,2048]{1,0:T(8,128)S(1)} %shard_map.61.acc_ref), custom_call_target="tpu_custom_call" | custom-call | flops 805306368 | bytes 1572864 | tf_op jit(solution)/shard_map/pallas_call | solution.py:266
  33.6 0.0 copy-start
  33.6 0.8 %collective-permute-start.11 = (s16[96,1152]{1,0:T(8,128)(2,1)S(1)}, s16[96,1152]{1,0:T(8,128)(2,1)S(1)}, u32[]{:S(2)}, u32[]{:S(2)}) collective-permute-start(s16[96,1152]{1,0:T(8,128)(2,1)S(1)} %get-tuple-element.33), channel_id=1, source_target_pairs={{0,2},{2,0},{1,3},{3,1},{4,6},{6,4},{5,7},{7,5},{8,10},{10,8},{9,1... | collective-permute-start | bytes 663560 | tf_op jit(solution)/shard_map/ppermute | solution.py:175
  34.4 1.2 %shard_map.62 = (f32[96,1024]{1,0:T(8,128)S(1)}, s16[96,1152]{1,0:T(8,128)(2,1)S(1)}) custom-call(bf16[192,2048]{1,0:T(8,128)(2,1)S(1)} %collective-permute-done.6.rows_ref, bf16[2048,2048]{1,0:T(8,128)(2,1)S(1)} %shard_map.60.w_ref, f32[192,2048]{1,0:T(8,128)S(1)} %shard_map.61.acc_ref), custom_call_target="tpu_custom_call" | custom-call | flops 805306368 | bytes 1572864 | tf_op jit(solution)/shard_map/pallas_call | solution.py:266
  35.6 1.4 %collective-permute-start.7 = (s16[96,1152]{1,0:T(8,128)(2,1)S(1)}, s16[96,1152]{1,0:T(8,128)(2,1)S(1)}, u32[]{:S(2)}, u32[]{:S(2)}) collective-permute-start(s16[96,1152]{1,0:T(8,128)(2,1)S(1)} %get-tuple-element.27), channel_id=1, source_target_pairs={{0,2},{2,0},{1,3},{3,1},{4,6},{6,4},{5,7},{7,5},{8,10},{10,8},{9,1... | collective-permute-start | bytes 663560 | tf_op jit(solution)/shard_map/ppermute | solution.py:175
  36.9 5.0 %collective-permute-done.11.refs_1_ = s16[96,1152]{1,0:T(8,128)(2,1)S(1)} collective-permute-done((s16[96,1152]{1,0:T(8,128)(2,1)S(1)}, s16[96,1152]{1,0:T(8,128)(2,1)S(1)}, u32[]{:S(2)}, u32[]{:S(2)}) %collective-permute-start.11) | collective-permute-done | bytes 221216 | tf_op jit(solution)/shard_map/ppermute | solution.py:175
  41.9 0.7 %shard_map.65 = (f32[24,1024]{1,0:T(8,128)S(1)}, s16[24,1152]{1,0:T(8,128)(2,1)S(1)}, s16[24,1152]{1,0:T(8,128)(2,1)S(1)}, s16[24,1152]{1,0:T(8,128)(2,1)S(1)}) custom-call(f32[96,1024]{1,0:T(8,128)S(1)} %get-tuple-element.32.refs_0_, s16[96,1152]{1,0:T(8,128)(2,1)S(1)} %collective-permute-done.11.refs_1_), custom_call_target="tpu_custom_call" | custom-call | bytes 786432 | tf_op jit(solution)/shard_map/pallas_call | solution.py:278
  42.6 2.7 %collective-permute-start.12 = (s16[24,1152]{1,0:T(8,128)(2,1)S(1)}, s16[24,1152]{1,0:T(8,128)(2,1)S(1)}, u32[]{:S(2)}, u32[]{:S(2)}) collective-permute-start(s16[24,1152]{1,0:T(8,128)(2,1)S(1)} %get-tuple-element.35), channel_id=1, source_target_pairs={{0,4},{4,0},{8,12},{12,8},{1,5},{5,1},{9,13},{13,9},{2,6},{6,2},{1... | collective-permute-start | bytes 165896 | tf_op jit(solution)/shard_map/ppermute | solution.py:175
  45.3 1.1 %collective-permute-start.13 = (s16[24,1152]{1,0:T(8,128)(2,1)S(1)}, s16[24,1152]{1,0:T(8,128)(2,1)S(1)}, u32[]{:S(2)}, u32[]{:S(2)}) collective-permute-start(s16[24,1152]{1,0:T(8,128)(2,1)S(1)} %get-tuple-element.36), channel_id=1, source_target_pairs={{0,8},{4,12},{8,0},{12,4},{1,9},{5,13},{9,1},{13,5},{2,10},{6,14},... | collective-permute-start | bytes 165896 | tf_op jit(solution)/shard_map/ppermute | solution.py:175
  46.4 1.4 %collective-permute-start.14 = (s16[24,1152]{1,0:T(8,128)(2,1)S(1)}, s16[24,1152]{1,0:T(8,128)(2,1)S(1)}, u32[]{:S(2)}, u32[]{:S(2)}) collective-permute-start(s16[24,1152]{1,0:T(8,128)(2,1)S(1)} %get-tuple-element.37), channel_id=1, source_target_pairs={{0,12},{4,8},{8,4},{12,0},{1,13},{5,9},{9,5},{13,1},{2,14},{6,10},... | collective-permute-start | bytes 165896 | tf_op jit(solution)/shard_map/ppermute | solution.py:175
  47.8 0.0 collective-permute-done.7.refs_1_
  47.8 0.7 %shard_map.63 = (f32[24,1024]{1,0:T(8,128)S(1)}, s16[24,1152]{1,0:T(8,128)(2,1)S(1)}, s16[24,1152]{1,0:T(8,128)(2,1)S(1)}, s16[24,1152]{1,0:T(8,128)(2,1)S(1)}) custom-call(f32[96,1024]{1,0:T(8,128)S(1)} %get-tuple-element.26.refs_0_, s16[96,1152]{1,0:T(8,128)(2,1)S(1)} %collective-permute-done.7.refs_1_), custom_call_target="tpu_custom_call" | custom-call | bytes 786432 | tf_op jit(solution)/shard_map/pallas_call | solution.py:278
  48.5 1.1 %collective-permute-start.8 = (s16[24,1152]{1,0:T(8,128)(2,1)S(1)}, s16[24,1152]{1,0:T(8,128)(2,1)S(1)}, u32[]{:S(2)}, u32[]{:S(2)}) collective-permute-start(s16[24,1152]{1,0:T(8,128)(2,1)S(1)} %get-tuple-element.29), channel_id=1, source_target_pairs={{0,4},{4,0},{8,12},{12,8},{1,5},{5,1},{9,13},{13,9},{2,6},{6,2},{1... | collective-permute-start | bytes 165896 | tf_op jit(solution)/shard_map/ppermute | solution.py:175
  49.6 2.0 %collective-permute-start.9 = (s16[24,1152]{1,0:T(8,128)(2,1)S(1)}, s16[24,1152]{1,0:T(8,128)(2,1)S(1)}, u32[]{:S(2)}, u32[]{:S(2)}) collective-permute-start(s16[24,1152]{1,0:T(8,128)(2,1)S(1)} %get-tuple-element.30), channel_id=1, source_target_pairs={{0,8},{4,12},{8,0},{12,4},{1,9},{5,13},{9,1},{13,5},{2,10},{6,14},... | collective-permute-start | bytes 165896 | tf_op jit(solution)/shard_map/ppermute | solution.py:175
  51.6 0.0 collective-permute-done.12.refs_5_
  51.6 1.4 %collective-permute-start.10 = (s16[24,1152]{1,0:T(8,128)(2,1)S(1)}, s16[24,1152]{1,0:T(8,128)(2,1)S(1)}, u32[]{:S(2)}, u32[]{:S(2)}) collective-permute-start(s16[24,1152]{1,0:T(8,128)(2,1)S(1)} %get-tuple-element.31), channel_id=1, source_target_pairs={{0,12},{4,8},{8,4},{12,0},{1,13},{5,9},{9,5},{13,1},{2,14},{6,10},... | collective-permute-start | bytes 165896 | tf_op jit(solution)/shard_map/ppermute | solution.py:175
  53.0 0.0 collective-permute-done.13.refs_6_
  53.0 0.1 collective-permute-done.14.refs_7_
  53.1 0.3 collective-permute-done.8.refs_1_
  53.4 2.7 %collective-permute-done.9.refs_2_ = s16[24,1152]{1,0:T(8,128)(2,1)S(1)} collective-permute-done((s16[24,1152]{1,0:T(8,128)(2,1)S(1)}, s16[24,1152]{1,0:T(8,128)(2,1)S(1)}, u32[]{:S(2)}, u32[]{:S(2)}) %collective-permute-start.9) | collective-permute-done | bytes 55328 | tf_op jit(solution)/shard_map/ppermute | solution.py:175
  56.1 1.4 %collective-permute-done.10.refs_3_ = s16[24,1152]{1,0:T(8,128)(2,1)S(1)} collective-permute-done((s16[24,1152]{1,0:T(8,128)(2,1)S(1)}, s16[24,1152]{1,0:T(8,128)(2,1)S(1)}, u32[]{:S(2)}, u32[]{:S(2)}) %collective-permute-start.10) | collective-permute-done | bytes 55328 | tf_op jit(solution)/shard_map/ppermute | solution.py:175
  57.6 0.0 copy-done
  57.6 2.0 %shard_map.66 = (bf16[24,8192]{1,0:T(8,128)(2,1)}, f32[1,24]{1,0:T(1,128)}) custom-call(f32[24,1024]{1,0:T(8,128)S(1)} %get-tuple-element.28.refs_0_, s16[24,1152]{1,0:T(8,128)(2,1)S(1)} %collective-permute-done.8.refs_1_, s16[24,1152]{1,0:T(8,128)(2,1)S(1)} %collective-permute-done.9.refs_2_, s16[24,1152]{1,0:T(8,128)(2,1)S(1)} %collective-permute-done.10.refs_3_, ...), custom_call_target="tpu_custom_call" | custom-call | tf_op jit(solution)/shard_map/pallas_call | solution.py:288
  (7 shorter events, 0.1 us)
Async XLA Ops:
  1.6 6.5 %collective-permute-start = (bf16[24,2048]{1,0:T(8,128)(2,1)S(1)}, bf16[24,2048]{1,0:T(8,128)(2,1)S(1)}, u32[]{:S(2)}, u32[]{:S(2)}) collective-permute-start(bf16[24,2048]{1,0:T(8,128)(2,1)S(1)} %get-tuple-element.43), channel_id=1, source_target_pairs={{0,2},{2,0},{1,3},{3,1},{4,6},{6,4},{5,7},{7,5},{8,10},{10,8},{9,1... | collective-permute-start | bytes 294920 | tf_op jit(solution)/shard_map/ppermute | solution.py:175
  4.6 8.6 %collective-permute-start.2 = (bf16[24,2048]{1,0:T(8,128)(2,1)S(1)}, bf16[24,2048]{1,0:T(8,128)(2,1)S(1)}, u32[]{:S(2)}, u32[]{:S(2)}) collective-permute-start(bf16[24,2048]{1,0:T(8,128)(2,1)S(1)} %get-tuple-element.42), channel_id=1, source_target_pairs={{0,8},{4,12},{8,0},{12,4},{1,9},{5,13},{9,1},{13,5},{2,10},{6,14},... | collective-permute-start | bytes 294920 | tf_op jit(solution)/shard_map/ppermute | solution.py:175
  8.1 21.7 %collective-permute-start.4 = (bf16[48,2048]{1,0:T(8,128)(2,1)S(1)}, bf16[48,2048]{1,0:T(8,128)(2,1)S(1)}, u32[]{:S(2)}, u32[]{:S(2)}) collective-permute-start(bf16[48,2048]{1,0:T(8,128)(2,1)S(1)} %pad_maximum_fusion.1), channel_id=1, source_target_pairs={{4,8},{8,4},{5,9},{9,5},{6,10},{10,6},{7,11},{11,7},{20,24},{24,20... | collective-permute-start | bytes 589832 | tf_op jit(solution)/shard_map/ppermute | solution.py:189
  8.8 21.1 %collective-permute-start.1 = (bf16[48,2048]{1,0:T(8,128)(2,1)S(1)}, bf16[48,2048]{1,0:T(8,128)(2,1)S(1)}, u32[]{:S(2)}, u32[]{:S(2)}) collective-permute-start(bf16[48,2048]{1,0:T(8,128)(2,1)S(1)} %pad_maximum_fusion.1), channel_id=1, source_target_pairs={{0,4},{4,0},{8,12},{12,8},{1,5},{5,1},{9,13},{13,9},{2,6},{6,2},{1... | collective-permute-start | bytes 589832 | tf_op jit(solution)/shard_map/ppermute | solution.py:175
  12.9 8.4 %collective-permute-start.3 = (bf16[24,2048]{1,0:T(8,128)(2,1)S(1)}, bf16[24,2048]{1,0:T(8,128)(2,1)S(1)}, u32[]{:S(2)}, u32[]{:S(2)}) collective-permute-start(bf16[24,2048]{1,0:T(8,128)(2,1)S(1)} %collective-permute-done), channel_id=1, source_target_pairs={{0,8},{4,12},{8,0},{12,4},{1,9},{5,13},{9,1},{13,5},{2,10},{6,14},... | collective-permute-start | bytes 294920 | tf_op jit(solution)/shard_map/ppermute | solution.py:175
  21.3 8.5 %collective-permute-start.5 = (bf16[48,2048]{1,0:T(8,128)(2,1)S(1)}, bf16[48,2048]{1,0:T(8,128)(2,1)S(1)}, u32[]{:S(2)}, u32[]{:S(2)}) collective-permute-start(bf16[48,2048]{1,0:T(8,128)(2,1)S(1)} %constant_dynamic-update-slice_fusion), channel_id=1, source_target_pairs={{4,0},{8,12},{5,1},{9,13},{6,2},{10,14},{7,3},{11,15},{20,16},{24,... | collective-permute-start | bytes 589832 | tf_op jit(solution)/shard_map/ppermute | solution.py:190
  30.0 2.4 %collective-permute-start.6 = (bf16[192,2048]{1,0:T(8,128)(2,1)S(1)}, bf16[192,2048]{1,0:T(8,128)(2,1)S(1)}, u32[]{:S(2)}, u32[]{:S(2)}) collective-permute-start(bf16[192,2048]{1,0:T(8,128)(2,1)S(1)} %bitcast.18), channel_id=1, source_target_pairs={{0,1},{1,0},{2,3},{3,2},{4,5},{5,4},{6,7},{7,6},{8,9},{9,8},{10,11... | collective-permute-start | bytes 2359304 | tf_op jit(solution)/shard_map/ppermute | solution.py:175
  33.6 24.0 %copy-start = (s32[8192]{0:T(1024)S(1)}, s32[8192]{0:T(1024)}, u32[]{:S(2)}) copy-start(s32[8192]{0:T(1024)} %param.7) | copy-start | bytes 98308
  33.6 8.3 %collective-permute-start.11 = (s16[96,1152]{1,0:T(8,128)(2,1)S(1)}, s16[96,1152]{1,0:T(8,128)(2,1)S(1)}, u32[]{:S(2)}, u32[]{:S(2)}) collective-permute-start(s16[96,1152]{1,0:T(8,128)(2,1)S(1)} %get-tuple-element.33), channel_id=1, source_target_pairs={{0,2},{2,0},{1,3},{3,1},{4,6},{6,4},{5,7},{7,5},{8,10},{10,8},{9,1... | collective-permute-start | bytes 663560 | tf_op jit(solution)/shard_map/ppermute | solution.py:175
  35.6 12.3 %collective-permute-start.7 = (s16[96,1152]{1,0:T(8,128)(2,1)S(1)}, s16[96,1152]{1,0:T(8,128)(2,1)S(1)}, u32[]{:S(2)}, u32[]{:S(2)}) collective-permute-start(s16[96,1152]{1,0:T(8,128)(2,1)S(1)} %get-tuple-element.27), channel_id=1, source_target_pairs={{0,2},{2,0},{1,3},{3,1},{4,6},{6,4},{5,7},{7,5},{8,10},{10,8},{9,1... | collective-permute-start | bytes 663560 | tf_op jit(solution)/shard_map/ppermute | solution.py:175
  42.6 9.0 %collective-permute-start.12 = (s16[24,1152]{1,0:T(8,128)(2,1)S(1)}, s16[24,1152]{1,0:T(8,128)(2,1)S(1)}, u32[]{:S(2)}, u32[]{:S(2)}) collective-permute-start(s16[24,1152]{1,0:T(8,128)(2,1)S(1)} %get-tuple-element.35), channel_id=1, source_target_pairs={{0,4},{4,0},{8,12},{12,8},{1,5},{5,1},{9,13},{13,9},{2,6},{6,2},{1... | collective-permute-start | bytes 165896 | tf_op jit(solution)/shard_map/ppermute | solution.py:175
  45.3 7.7 %collective-permute-start.13 = (s16[24,1152]{1,0:T(8,128)(2,1)S(1)}, s16[24,1152]{1,0:T(8,128)(2,1)S(1)}, u32[]{:S(2)}, u32[]{:S(2)}) collective-permute-start(s16[24,1152]{1,0:T(8,128)(2,1)S(1)} %get-tuple-element.36), channel_id=1, source_target_pairs={{0,8},{4,12},{8,0},{12,4},{1,9},{5,13},{9,1},{13,5},{2,10},{6,14},... | collective-permute-start | bytes 165896 | tf_op jit(solution)/shard_map/ppermute | solution.py:175
  46.4 6.6 %collective-permute-start.14 = (s16[24,1152]{1,0:T(8,128)(2,1)S(1)}, s16[24,1152]{1,0:T(8,128)(2,1)S(1)}, u32[]{:S(2)}, u32[]{:S(2)}) collective-permute-start(s16[24,1152]{1,0:T(8,128)(2,1)S(1)} %get-tuple-element.37), channel_id=1, source_target_pairs={{0,12},{4,8},{8,4},{12,0},{1,13},{5,9},{9,5},{13,1},{2,14},{6,10},... | collective-permute-start | bytes 165896 | tf_op jit(solution)/shard_map/ppermute | solution.py:175
  48.5 4.8 %collective-permute-start.8 = (s16[24,1152]{1,0:T(8,128)(2,1)S(1)}, s16[24,1152]{1,0:T(8,128)(2,1)S(1)}, u32[]{:S(2)}, u32[]{:S(2)}) collective-permute-start(s16[24,1152]{1,0:T(8,128)(2,1)S(1)} %get-tuple-element.29), channel_id=1, source_target_pairs={{0,4},{4,0},{8,12},{12,8},{1,5},{5,1},{9,13},{13,9},{2,6},{6,2},{1... | collective-permute-start | bytes 165896 | tf_op jit(solution)/shard_map/ppermute | solution.py:175
  49.6 6.5 %collective-permute-start.9 = (s16[24,1152]{1,0:T(8,128)(2,1)S(1)}, s16[24,1152]{1,0:T(8,128)(2,1)S(1)}, u32[]{:S(2)}, u32[]{:S(2)}) collective-permute-start(s16[24,1152]{1,0:T(8,128)(2,1)S(1)} %get-tuple-element.30), channel_id=1, source_target_pairs={{0,8},{4,12},{8,0},{12,4},{1,9},{5,13},{9,1},{13,5},{2,10},{6,14},... | collective-permute-start | bytes 165896 | tf_op jit(solution)/shard_map/ppermute | solution.py:175
  51.6 6.0 %collective-permute-start.10 = (s16[24,1152]{1,0:T(8,128)(2,1)S(1)}, s16[24,1152]{1,0:T(8,128)(2,1)S(1)}, u32[]{:S(2)}, u32[]{:S(2)}) collective-permute-start(s16[24,1152]{1,0:T(8,128)(2,1)S(1)} %get-tuple-element.31), channel_id=1, source_target_pairs={{0,12},{4,8},{8,4},{12,0},{1,13},{5,9},{9,5},{13,1},{2,14},{6,10},... | collective-permute-start | bytes 165896 | tf_op jit(solution)/shard_map/ppermute | solution.py:175

commit v3 on v2

--- a/solution.py
+++ b/solution.py
@@ -43,6 +43,20 @@
         copies.append(
             pltpu.make_async_copy(w_ref.at[pl.ds(start, piece)], out_ref.at[pl.ds(i * piece, piece)], sems.at[i])
         )
+    for copy in copies:
+        copy.start()
+    for copy in copies:
+        copy.wait()
+
+
+def take(rows_ref, *refs):
+    out_refs, sems = refs[:-1], refs[-1]
+    part = out_refs[0].shape[1]
+    copies = []
+    for j, out_ref in enumerate(out_refs):
+        index = jnp.bitwise_xor(lax.axis_index("seq"), j) * lax.axis_size("kv") + lax.axis_index("kv")
+        at = pl.ds(pl.multiple_of(index * part, part), part)
+        copies.append(pltpu.make_async_copy(rows_ref.at[:, at], out_ref, sems.at[j]))
     for copy in copies:
         copy.start()
     for copy in copies:
@@ -175,22 +189,23 @@
     return lax.ppermute(array, axis, [(i, i ^ offset) for i in range(count)])
 
 
-def gather(own, others, count):
+def gather(own, others, half, count):
     if count != 4:
         pieces = []
         for block in [own] + others:
             pieces += [block] + [swap(block, "tensor", count, k) for k in range(1, count)]
-        return jnp.concatenate(pieces, axis=0)
+        return jnp.concatenate(pieces, axis=0), half
     tok = own.shape[0]
     mine = jnp.concatenate([own] + others, axis=0)
     two = [swap(own, "tensor", count, 2), swap(mine[tok:], "tensor", count, 2)]
     two = jnp.concatenate(two, axis=0)
     one = swap(mine, "tensor", count, 1)
+    mine, one, two, half = lax.optimization_barrier((mine, one, two, half))
     near = lax.ppermute(mine, "tensor", [(1, 2), (2, 1)])
     far = lax.ppermute(two, "tensor", [(1, 0), (2, 3)])
     blocks = jnp.stack([mine, one, two, near + far])
     blocks = blocks.reshape(count, 1 + len(others), tok, own.shape[1])
-    return jnp.swapaxes(blocks, 0, 1).reshape(-1, own.shape[1])
+    return jnp.swapaxes(blocks, 0, 1).reshape(-1, own.shape[1]), half
 
 
 def per_device(hidden_rows, kv_weight, block_lengths, sign_bits):
@@ -229,6 +244,16 @@
     sine = jnp.concatenate([-sine, sine], axis=1)
     weight, cosine, sine = lax.optimization_barrier((weight, cosine, sine))
 
+    slices = local(
+        take,
+        [pltpu.VMEM((tok_dev, part), hidden_rows.dtype)] * seqs,
+        [pl.BlockSpec(memory_space=pltpu.HBM)],
+        4,
+        [pltpu.SemaphoreType.DMA((seqs,))],
+    )(pltpu.with_memory_space_constraint(hidden_rows, pltpu.HBM))
+    others = [swap(slices[j], "seq", seqs, j) for j in range(1, seqs)]
+    weight = pltpu.with_memory_space_constraint(weight, pltpu.HBM)
+    weight, *others = lax.optimization_barrier((weight, *others))
     halves = [
         local(
             functools.partial(load, offset, 8),
@@ -237,15 +262,10 @@
             4,
             [pltpu.SemaphoreType.DMA((8,))],
             moved=4 * part * columns,
-        )(pltpu.with_memory_space_constraint(weight, pltpu.HBM))
+        )(weight)
         for offset in range(cores)
     ]
-
-    def columns_for(seq):
-        return lax.dynamic_slice_in_dim(hidden_rows, (seq * cores + which) * part, part, 1)
-
-    others = [swap(columns_for(jnp.bitwise_xor(seq_at, j)), "seq", seqs, j) for j in range(1, seqs)]
-    mine = gather(columns_for(seq_at), others, tensors)
+    mine, halves[0] = gather(slices[0], others, halves[0], tensors)
     mine, *halves = lax.optimization_barrier((mine, *halves))
     other = swap(mine, "kv", cores, 1)
     rows = mine.shape[0]
@@ -274,6 +294,8 @@
             flops=2 * rows * part * width,
             moved=8 * rows * width,
         )(other, pltpu.with_memory_space_constraint(halves[1], pltpu.VMEM), acc)
+        if blocks:
+            send, *got = lax.optimization_barrier((send, *got))
         got = [swap(send[(j - 1) * own : j * own], "seq", seqs, j) for j in range(1, seqs)]
         parts = local(
             functools.partial(middle, tok_dev, seqs),

time: 59.8 us -> 57.9 us (0.968)
  starting transfers between devices: 23.9 us -> 20.5 us
  waiting for transfers between devices: 18.1 us -> 19.5 us
  local copies, waits for them, and re-layouts: 0.98 us -> 0.02 us
  Pallas kernels: 14.7 us -> 15.6 us
    ppermute x1, waiting for transfers between devices: 0.01 us -> 4.07 us  [gather(): far = lax.ppermute(two, 'tensor', [(1, 0), (2, 3)])]
    ppermute x13, starting transfers between devices: 21.9 us -> 18.6 us  [swap(): return lax.ppermute(array, axis, [(i, i ^ offset) for i in range(count)])]
    ppermute x13, waiting for transfers between devices: 18.1 us -> 15.5 us  [swap(): return lax.ppermute(array, axis, [(i, i ^ offset) for i in range(count)])]
    pallas_call x0 -> x1, Pallas kernels: none -> 0.97 us  [per_device(): local(take, [pltpu.VMEM((tok_dev, part), hidden_rows.dtype)] * seqs, [pl....]
    dynamic_slice x1 -> x0, local copies, waits for them, and re-layouts: 0.96 us -> none  [columns_for(): lax.dynamic_slice_in_dim(hidden_rows, (seq * cores + which) * part, part, 1)]
  transfers between devices with their start and end apart: 15 -> 15, of which waited for: 7 -> 8; matrix products, arithmetic and copies ran while one was open for 2% -> 2% of each run, Pallas kernels for 19% -> 20%
where the time goes in v3:
time: 57.9 us; the launch traced here: 57.7 us
  starting transfers between devices  20.5 us (35%)
  waiting for transfers between devices  19.5 us (34%)
  Pallas kernels  15.6 us (27%)
  other arithmetic  1.22 us (2%)
  between operations  0.82 us (1%)
    ppermute x13, starting transfers between devices, swap(): return lax.ppermute(array, axis, [(i, i ^ offset) for i in range(count)])  18.6 us
    ppermute x13, waiting for transfers between devices, swap(): return lax.ppermute(array, axis, [(i, i ^ offset) for i in range(count)])  15.5 us
    pallas_call x2, Pallas kernels, per_device(): local(functools.partial(load, offset, 8), pltpu.VMEM((part, columns), wei...  6.96 us
    ppermute x1, waiting for transfers between devices, gather(): far = lax.ppermute(two, 'tensor', [(1, 0), (2, 3)])  4.07 us
    pallas_call x2, Pallas kernels, per_device(): local(functools.partial(second_half, chunk * width, tile), [jax.ShapeDtyp...  2.4 us
    pallas_call x1, Pallas kernels, per_device(): local(functools.partial(final, tensors, chunks), [jax.ShapeDtypeStruct((t...  2.04 us
    pallas_call x1, Pallas kernels, per_device(): local(functools.partial(first_half, tile), jax.ShapeDtypeStruct((rows, co...  1.84 us
    pallas_call x2, Pallas kernels, per_device(): local(functools.partial(middle, tok_dev, seqs), [jax.ShapeDtypeStruct((to...  1.41 us
  transfers between devices with their start and end apart: 15, of which 8 were waited for; matrix products, arithmetic and copies ran while one was open for 2% of the time, Pallas kernels for 20%

profile of v3, /device:TPU:0, one launch (start us, length us, event | category | flops | bytes accessed | tf_op | source)
XLA Modules:
  0.0 57.7 jit_solution(11555183680206408709)
XLA Ops:
  0.6 1.0 %shard_map.59 = (bf16[24,2048]{1,0:T(8,128)(2,1)S(1)}, bf16[24,2048]{1,0:T(8,128)(2,1)S(1)}) custom-call(bf16[24,8192]{1,0:T(8,128)(2,1)} %rows_ref.1), custom_call_target="tpu_custom_call" | custom-call | tf_op jit(solution)/shard_map/pallas_call | solution.py:247
  1.6 3.0 %collective-permute-start = (bf16[24,2048]{1,0:T(8,128)(2,1)S(1)}, bf16[24,2048]{1,0:T(8,128)(2,1)S(1)}, u32[]{:S(2)}, u32[]{:S(2)}) collective-permute-start(bf16[24,2048]{1,0:T(8,128)(2,1)S(1)} %get-tuple-element.33), channel_id=1, source_target_pairs={{0,2},{2,0},{1,3},{3,1},{4,6},{6,4},{5,7},{7,5},{8,10},{10,8},{9,1... | collective-permute-start | bytes 294920 | tf_op jit(solution)/shard_map/ppermute | solution.py:189
  4.6 2.6 %collective-permute-start.2 = (bf16[24,2048]{1,0:T(8,128)(2,1)S(1)}, bf16[24,2048]{1,0:T(8,128)(2,1)S(1)}, u32[]{:S(2)}, u32[]{:S(2)}) collective-permute-start(bf16[24,2048]{1,0:T(8,128)(2,1)S(1)} %get-tuple-element.31), channel_id=1, source_target_pairs={{0,8},{4,12},{8,0},{12,4},{1,9},{5,13},{9,1},{13,5},{2,10},{6,14},... | collective-permute-start | bytes 294920 | tf_op jit(solution)/shard_map/ppermute | solution.py:189
  7.2 0.7 %select_reduce_fusion.1 = s32[4]{0:T(128)S(1)} fusion(s32[4]{0:T(128)} %param.6), kind=kLoop, calls=%fused_computation.12 | loop fusion | flops 44 | bytes 32 | tf_op jit(solution)/shard_map/reduce_sum | solution.py:235
  8.0 0.1 select_reduce_fusion
  8.1 0.1 fusion.2
  8.2 0.1 pad_maximum_fusion.2
  8.3 0.0 collective-permute-done
  8.3 2.0 %collective-permute-start.3 = (bf16[24,2048]{1,0:T(8,128)(2,1)S(1)}, bf16[24,2048]{1,0:T(8,128)(2,1)S(1)}, u32[]{:S(2)}, u32[]{:S(2)}) collective-permute-start(bf16[24,2048]{1,0:T(8,128)(2,1)S(1)} %collective-permute-done), channel_id=1, source_target_pairs={{0,8},{4,12},{8,0},{12,4},{1,9},{5,13},{9,1},{13,5},{2,10},{6,14},... | collective-permute-start | bytes 294920 | tf_op jit(solution)/shard_map/ppermute | solution.py:189
  10.3 1.6 %collective-permute-start.1 = (bf16[48,2048]{1,0:T(8,128)(2,1)S(1)}, bf16[48,2048]{1,0:T(8,128)(2,1)S(1)}, u32[]{:S(2)}, u32[]{:S(2)}) collective-permute-start(bf16[48,2048]{1,0:T(8,128)(2,1)S(1)} %constant_dynamic-update-slice_fusion), channel_id=1, source_target_pairs={{0,4},{4,0},{8,12},{12,8},{1,5},{5,1},{9,13},{13,9},{2,6},{6,2},{1... | collective-permute-start | bytes 589832 | tf_op jit(solution)/shard_map/ppermute | solution.py:189
  12.0 3.5 %shard_map.60.w_ref = bf16[2048,2048]{1,0:T(8,128)(2,1)S(1)} custom-call(bf16[4096,2048]{1,0:T(8,128)(2,1)} %bitcast.21), custom_call_target="tpu_custom_call" | custom-call | bytes 16777216 | tf_op jit(solution)/shard_map/pallas_call | solution.py:258
  15.5 0.0 collective-permute-done.2
  15.5 0.6 %collective-permute-done.3 = bf16[24,2048]{1,0:T(8,128)(2,1)S(1)} collective-permute-done((bf16[24,2048]{1,0:T(8,128)(2,1)S(1)}, bf16[24,2048]{1,0:T(8,128)(2,1)S(1)}, u32[]{:S(2)}, u32[]{:S(2)}) %collective-permute-start.3) | collective-permute-done | bytes 98336 | tf_op jit(solution)/shard_map/ppermute | solution.py:189
  16.1 2.1 %collective-permute-done.1 = bf16[48,2048]{1,0:T(8,128)(2,1)S(1)} collective-permute-done((bf16[48,2048]{1,0:T(8,128)(2,1)S(1)}, bf16[48,2048]{1,0:T(8,128)(2,1)S(1)}, u32[]{:S(2)}, u32[]{:S(2)}) %collective-permute-start.1) | collective-permute-done | bytes 196640 | tf_op jit(solution)/shard_map/ppermute | solution.py:189
  18.2 0.7 %collective-permute-start.4 = (bf16[48,2048]{1,0:T(8,128)(2,1)S(1)}, bf16[48,2048]{1,0:T(8,128)(2,1)S(1)}, u32[]{:S(2)}, u32[]{:S(2)}) collective-permute-start(bf16[48,2048]{1,0:T(8,128)(2,1)S(1)} %constant_dynamic-update-slice_fusion), channel_id=1, source_target_pairs={{4,8},{8,4},{5,9},{9,5},{6,10},{10,6},{7,11},{11,7},{20,24},{24,20... | collective-permute-start | bytes 589832 | tf_op jit(solution)/shard_map/ppermute | solution.py:204
  18.9 1.3 %collective-permute-start.5 = (bf16[48,2048]{1,0:T(8,128)(2,1)S(1)}, bf16[48,2048]{1,0:T(8,128)(2,1)S(1)}, u32[]{:S(2)}, u32[]{:S(2)}) collective-permute-start(bf16[48,2048]{1,0:T(8,128)(2,1)S(1)} %pad_maximum_fusion.1), channel_id=1, source_target_pairs={{4,0},{8,12},{5,1},{9,13},{6,2},{10,14},{7,3},{11,15},{20,16},{24,... | collective-permute-start | bytes 589832 | tf_op jit(solution)/shard_map/ppermute | solution.py:205
  20.2 3.5 %shard_map.61.w_ref = bf16[2048,2048]{1,0:T(8,128)(2,1)S(1)} custom-call(bf16[4096,2048]{1,0:T(8,128)(2,1)} %bitcast.22), custom_call_target="tpu_custom_call" | custom-call | bytes 16777216 | tf_op jit(solution)/shard_map/pallas_call | solution.py:258
  23.7 0.0 collective-permute-done.4
  23.7 4.1 %collective-permute-done.5 = bf16[48,2048]{1,0:T(8,128)(2,1)S(1)} collective-permute-done((bf16[48,2048]{1,0:T(8,128)(2,1)S(1)}, bf16[48,2048]{1,0:T(8,128)(2,1)S(1)}, u32[]{:S(2)}, u32[]{:S(2)}) %collective-permute-start.5) | collective-permute-done | bytes 196640 | tf_op jit(solution)/shard_map/ppermute | solution.py:205
  27.8 0.1 pad_maximum_fusion
  27.9 0.1 collective-permute-start.6
  28.0 1.8 %shard_map.62.acc_ref = f32[192,2048]{1,0:T(8,128)S(1)} custom-call(bf16[192,2048]{1,0:T(8,128)(2,1)S(1)} %bitcast.19, bf16[2048,2048]{1,0:T(8,128)(2,1)S(1)} %shard_map.60.w_ref), custom_call_target="tpu_custom_call" | custom-call | flops 1610612736 | bytes 1572864 | tf_op jit(solution)/shard_map/pallas_call | solution.py:276
  29.8 0.4 collective-permute-done.6.rows_ref
  30.2 1.2 %shard_map.63 = (f32[96,1024]{1,0:T(8,128)S(1)}, s16[96,1152]{1,0:T(8,128)(2,1)S(1)}) custom-call(bf16[192,2048]{1,0:T(8,128)(2,1)S(1)} %collective-permute-done.6.rows_ref, bf16[2048,2048]{1,0:T(8,128)(2,1)S(1)} %shard_map.61.w_ref, f32[192,2048]{1,0:T(8,128)S(1)} %shard_map.62.acc_ref), custom_call_target="tpu_custom_call" | custom-call | flops 805306368 | bytes 1572864 | tf_op jit(solution)/shard_map/pallas_call | solution.py:286
  31.5 0.0 copy-start
  31.5 0.1 collective-permute-start.7
  31.5 1.2 %shard_map.65 = (f32[96,1024]{1,0:T(8,128)S(1)}, s16[96,1152]{1,0:T(8,128)(2,1)S(1)}) custom-call(bf16[192,2048]{1,0:T(8,128)(2,1)S(1)} %collective-permute-done.6.rows_ref, bf16[2048,2048]{1,0:T(8,128)(2,1)S(1)} %shard_map.61.w_ref, f32[192,2048]{1,0:T(8,128)S(1)} %shard_map.62.acc_ref), custom_call_target="tpu_custom_call" | custom-call | flops 805306368 | bytes 1572864 | tf_op jit(solution)/shard_map/pallas_call | solution.py:286
  32.8 6.3 %collective-permute-done.7.refs_1_ = s16[96,1152]{1,0:T(8,128)(2,1)S(1)} collective-permute-done((s16[96,1152]{1,0:T(8,128)(2,1)S(1)}, s16[96,1152]{1,0:T(8,128)(2,1)S(1)}, u32[]{:S(2)}, u32[]{:S(2)}) %collective-permute-start.7) | collective-permute-done | bytes 221216 | tf_op jit(solution)/shard_map/ppermute | solution.py:189
  39.0 0.3 collective-permute-start.11
  39.3 0.7 %shard_map.64 = (f32[24,1024]{1,0:T(8,128)S(1)}, s16[24,1152]{1,0:T(8,128)(2,1)S(1)}, s16[24,1152]{1,0:T(8,128)(2,1)S(1)}, s16[24,1152]{1,0:T(8,128)(2,1)S(1)}) custom-call(f32[96,1024]{1,0:T(8,128)S(1)} %get-tuple-element.43.refs_0_, s16[96,1152]{1,0:T(8,128)(2,1)S(1)} %collective-permute-done.7.refs_1_), custom_call_target="tpu_custom_call" | custom-call | bytes 786432 | tf_op jit(solution)/shard_map/pallas_call | solution.py:300
  40.0 0.1 collective-permute-start.8
  40.1 3.3 %collective-permute-start.9 = (s16[24,1152]{1,0:T(8,128)(2,1)S(1)}, s16[24,1152]{1,0:T(8,128)(2,1)S(1)}, u32[]{:S(2)}, u32[]{:S(2)}) collective-permute-start(s16[24,1152]{1,0:T(8,128)(2,1)S(1)} %get-tuple-element.47), channel_id=1, source_target_pairs={{0,8},{4,12},{8,0},{12,4},{1,9},{5,13},{9,1},{13,5},{2,10},{6,14},... | collective-permute-start | bytes 165896 | tf_op jit(solution)/shard_map/ppermute | solution.py:189
  43.4 1.1 %collective-permute-start.10 = (s16[24,1152]{1,0:T(8,128)(2,1)S(1)}, s16[24,1152]{1,0:T(8,128)(2,1)S(1)}, u32[]{:S(2)}, u32[]{:S(2)}) collective-permute-start(s16[24,1152]{1,0:T(8,128)(2,1)S(1)} %get-tuple-element.48), channel_id=1, source_target_pairs={{0,12},{4,8},{8,4},{12,0},{1,13},{5,9},{9,5},{13,1},{2,14},{6,10},... | collective-permute-start | bytes 165896 | tf_op jit(solution)/shard_map/ppermute | solution.py:189
  44.5 1.2 %collective-permute-done.11.refs_1_ = s16[96,1152]{1,0:T(8,128)(2,1)S(1)} collective-permute-done((s16[96,1152]{1,0:T(8,128)(2,1)S(1)}, s16[96,1152]{1,0:T(8,128)(2,1)S(1)}, u32[]{:S(2)}, u32[]{:S(2)}) %collective-permute-start.11) | collective-permute-done | bytes 221216 | tf_op jit(solution)/shard_map/ppermute | solution.py:189
  45.6 0.7 %shard_map.66 = (f32[24,1024]{1,0:T(8,128)S(1)}, s16[24,1152]{1,0:T(8,128)(2,1)S(1)}, s16[24,1152]{1,0:T(8,128)(2,1)S(1)}, s16[24,1152]{1,0:T(8,128)(2,1)S(1)}) custom-call(f32[96,1024]{1,0:T(8,128)S(1)} %get-tuple-element.49.refs_0_, s16[96,1152]{1,0:T(8,128)(2,1)S(1)} %collective-permute-done.11.refs_1_), custom_call_target="tpu_custom_call" | custom-call | bytes 786432 | tf_op jit(solution)/shard_map/pallas_call | solution.py:300
  46.4 0.1 collective-permute-start.12
  46.4 3.3 %collective-permute-start.13 = (s16[24,1152]{1,0:T(8,128)(2,1)S(1)}, s16[24,1152]{1,0:T(8,128)(2,1)S(1)}, u32[]{:S(2)}, u32[]{:S(2)}) collective-permute-start(s16[24,1152]{1,0:T(8,128)(2,1)S(1)} %get-tuple-element.54), channel_id=1, source_target_pairs={{0,8},{4,12},{8,0},{12,4},{1,9},{5,13},{9,1},{13,5},{2,10},{6,14},... | collective-permute-start | bytes 165896 | tf_op jit(solution)/shard_map/ppermute | solution.py:189
  49.7 0.0 collective-permute-done.8.refs_1_
  49.7 1.1 %collective-permute-start.14 = (s16[24,1152]{1,0:T(8,128)(2,1)S(1)}, s16[24,1152]{1,0:T(8,128)(2,1)S(1)}, u32[]{:S(2)}, u32[]{:S(2)}) collective-permute-start(s16[24,1152]{1,0:T(8,128)(2,1)S(1)} %get-tuple-element.55), channel_id=1, source_target_pairs={{0,12},{4,8},{8,4},{12,0},{1,13},{5,9},{9,5},{13,1},{2,14},{6,10},... | collective-permute-start | bytes 165896 | tf_op jit(solution)/shard_map/ppermute | solution.py:189
  50.8 0.0 collective-permute-done.9.refs_2_
  50.8 0.0 collective-permute-done.10.refs_3_
  50.8 0.0 collective-permute-done.12.refs_5_
  50.8 1.0 %collective-permute-done.13.refs_6_ = s16[24,1152]{1,0:T(8,128)(2,1)S(1)} collective-permute-done((s16[24,1152]{1,0:T(8,128)(2,1)S(1)}, s16[24,1152]{1,0:T(8,128)(2,1)S(1)}, u32[]{:S(2)}, u32[]{:S(2)}) %collective-permute-start.13) | collective-permute-done | bytes 55328 | tf_op jit(solution)/shard_map/ppermute | solution.py:189
  51.9 3.8 %collective-permute-done.14.refs_7_ = s16[24,1152]{1,0:T(8,128)(2,1)S(1)} collective-permute-done((s16[24,1152]{1,0:T(8,128)(2,1)S(1)}, s16[24,1152]{1,0:T(8,128)(2,1)S(1)}, u32[]{:S(2)}, u32[]{:S(2)}) %collective-permute-start.14) | collective-permute-done | bytes 55328 | tf_op jit(solution)/shard_map/ppermute | solution.py:189
  55.7 0.0 copy-done
  55.7 2.0 %shard_map.67 = (bf16[24,8192]{1,0:T(8,128)(2,1)}, f32[1,24]{1,0:T(1,128)}) custom-call(f32[24,1024]{1,0:T(8,128)S(1)} %get-tuple-element.45.refs_0_, s16[24,1152]{1,0:T(8,128)(2,1)S(1)} %collective-permute-done.8.refs_1_, s16[24,1152]{1,0:T(8,128)(2,1)S(1)} %collective-permute-done.9.refs_2_, s16[24,1152]{1,0:T(8,128)(2,1)S(1)} %collective-permute-done.10.refs_3_, ...), custom_call_target="tpu_custom_call" | custom-call | tf_op jit(solution)/shard_map/pallas_call | solution.py:310
  (7 shorter events, 0.1 us)
Async XLA Ops:
  1.6 6.7 %collective-permute-start = (bf16[24,2048]{1,0:T(8,128)(2,1)S(1)}, bf16[24,2048]{1,0:T(8,128)(2,1)S(1)}, u32[]{:S(2)}, u32[]{:S(2)}) collective-permute-start(bf16[24,2048]{1,0:T(8,128)(2,1)S(1)} %get-tuple-element.33), channel_id=1, source_target_pairs={{0,2},{2,0},{1,3},{3,1},{4,6},{6,4},{5,7},{7,5},{8,10},{10,8},{9,1... | collective-permute-start | bytes 294920 | tf_op jit(solution)/shard_map/ppermute | solution.py:189
  4.6 10.8 %collective-permute-start.2 = (bf16[24,2048]{1,0:T(8,128)(2,1)S(1)}, bf16[24,2048]{1,0:T(8,128)(2,1)S(1)}, u32[]{:S(2)}, u32[]{:S(2)}) collective-permute-start(bf16[24,2048]{1,0:T(8,128)(2,1)S(1)} %get-tuple-element.31), channel_id=1, source_target_pairs={{0,8},{4,12},{8,0},{12,4},{1,9},{5,13},{9,1},{13,5},{2,10},{6,14},... | collective-permute-start | bytes 294920 | tf_op jit(solution)/shard_map/ppermute | solution.py:189
  8.3 7.8 %collective-permute-start.3 = (bf16[24,2048]{1,0:T(8,128)(2,1)S(1)}, bf16[24,2048]{1,0:T(8,128)(2,1)S(1)}, u32[]{:S(2)}, u32[]{:S(2)}) collective-permute-start(bf16[24,2048]{1,0:T(8,128)(2,1)S(1)} %collective-permute-done), channel_id=1, source_target_pairs={{0,8},{4,12},{8,0},{12,4},{1,9},{5,13},{9,1},{13,5},{2,10},{6,14},... | collective-permute-start | bytes 294920 | tf_op jit(solution)/shard_map/ppermute | solution.py:189
  10.3 7.9 %collective-permute-start.1 = (bf16[48,2048]{1,0:T(8,128)(2,1)S(1)}, bf16[48,2048]{1,0:T(8,128)(2,1)S(1)}, u32[]{:S(2)}, u32[]{:S(2)}) collective-permute-start(bf16[48,2048]{1,0:T(8,128)(2,1)S(1)} %constant_dynamic-update-slice_fusion), channel_id=1, source_target_pairs={{0,4},{4,0},{8,12},{12,8},{1,5},{5,1},{9,13},{13,9},{2,6},{6,2},{1... | collective-permute-start | bytes 589832 | tf_op jit(solution)/shard_map/ppermute | solution.py:189
  18.2 5.5 %collective-permute-start.4 = (bf16[48,2048]{1,0:T(8,128)(2,1)S(1)}, bf16[48,2048]{1,0:T(8,128)(2,1)S(1)}, u32[]{:S(2)}, u32[]{:S(2)}) collective-permute-start(bf16[48,2048]{1,0:T(8,128)(2,1)S(1)} %constant_dynamic-update-slice_fusion), channel_id=1, source_target_pairs={{4,8},{8,4},{5,9},{9,5},{6,10},{10,6},{7,11},{11,7},{20,24},{24,20... | collective-permute-start | bytes 589832 | tf_op jit(solution)/shard_map/ppermute | solution.py:204
  18.9 8.9 %collective-permute-start.5 = (bf16[48,2048]{1,0:T(8,128)(2,1)S(1)}, bf16[48,2048]{1,0:T(8,128)(2,1)S(1)}, u32[]{:S(2)}, u32[]{:S(2)}) collective-permute-start(bf16[48,2048]{1,0:T(8,128)(2,1)S(1)} %pad_maximum_fusion.1), channel_id=1, source_target_pairs={{4,0},{8,12},{5,1},{9,13},{6,2},{10,14},{7,3},{11,15},{20,16},{24,... | collective-permute-start | bytes 589832 | tf_op jit(solution)/shard_map/ppermute | solution.py:205
  27.9 2.4 %collective-permute-start.6 = (bf16[192,2048]{1,0:T(8,128)(2,1)S(1)}, bf16[192,2048]{1,0:T(8,128)(2,1)S(1)}, u32[]{:S(2)}, u32[]{:S(2)}) collective-permute-start(bf16[192,2048]{1,0:T(8,128)(2,1)S(1)} %bitcast.18), channel_id=1, source_target_pairs={{0,1},{1,0},{2,3},{3,2},{4,5},{5,4},{6,7},{7,6},{8,9},{9,8},{10,11... | collective-permute-start | bytes 2359304 | tf_op jit(solution)/shard_map/ppermute | solution.py:189
  31.5 24.3 %copy-start = (s32[8192]{0:T(1024)S(1)}, s32[8192]{0:T(1024)}, u32[]{:S(2)}) copy-start(s32[8192]{0:T(1024)} %param.7) | copy-start | bytes 98308
  31.5 7.5 %collective-permute-start.7 = (s16[96,1152]{1,0:T(8,128)(2,1)S(1)}, s16[96,1152]{1,0:T(8,128)(2,1)S(1)}, u32[]{:S(2)}, u32[]{:S(2)}) collective-permute-start(s16[96,1152]{1,0:T(8,128)(2,1)S(1)} %get-tuple-element.44), channel_id=1, source_target_pairs={{0,2},{2,0},{1,3},{3,1},{4,6},{6,4},{5,7},{7,5},{8,10},{10,8},{9,1... | collective-permute-start | bytes 663560 | tf_op jit(solution)/shard_map/ppermute | solution.py:189
  39.0 6.6 %collective-permute-start.11 = (s16[96,1152]{1,0:T(8,128)(2,1)S(1)}, s16[96,1152]{1,0:T(8,128)(2,1)S(1)}, u32[]{:S(2)}, u32[]{:S(2)}) collective-permute-start(s16[96,1152]{1,0:T(8,128)(2,1)S(1)} %get-tuple-element.51), channel_id=1, source_target_pairs={{0,2},{2,0},{1,3},{3,1},{4,6},{6,4},{5,7},{7,5},{8,10},{10,8},{9,1... | collective-permute-start | bytes 663560 | tf_op jit(solution)/shard_map/ppermute | solution.py:189
  40.0 9.7 %collective-permute-start.8 = (s16[24,1152]{1,0:T(8,128)(2,1)S(1)}, s16[24,1152]{1,0:T(8,128)(2,1)S(1)}, u32[]{:S(2)}, u32[]{:S(2)}) collective-permute-start(s16[24,1152]{1,0:T(8,128)(2,1)S(1)} %get-tuple-element.46), channel_id=1, source_target_pairs={{0,4},{4,0},{8,12},{12,8},{1,5},{5,1},{9,13},{13,9},{2,6},{6,2},{1... | collective-permute-start | bytes 165896 | tf_op jit(solution)/shard_map/ppermute | solution.py:189
  40.1 10.7 %collective-permute-start.9 = (s16[24,1152]{1,0:T(8,128)(2,1)S(1)}, s16[24,1152]{1,0:T(8,128)(2,1)S(1)}, u32[]{:S(2)}, u32[]{:S(2)}) collective-permute-start(s16[24,1152]{1,0:T(8,128)(2,1)S(1)} %get-tuple-element.47), channel_id=1, source_target_pairs={{0,8},{4,12},{8,0},{12,4},{1,9},{5,13},{9,1},{13,5},{2,10},{6,14},... | collective-permute-start | bytes 165896 | tf_op jit(solution)/shard_map/ppermute | solution.py:189
  43.4 7.4 %collective-permute-start.10 = (s16[24,1152]{1,0:T(8,128)(2,1)S(1)}, s16[24,1152]{1,0:T(8,128)(2,1)S(1)}, u32[]{:S(2)}, u32[]{:S(2)}) collective-permute-start(s16[24,1152]{1,0:T(8,128)(2,1)S(1)} %get-tuple-element.48), channel_id=1, source_target_pairs={{0,12},{4,8},{8,4},{12,0},{1,13},{5,9},{9,5},{13,1},{2,14},{6,10},... | collective-permute-start | bytes 165896 | tf_op jit(solution)/shard_map/ppermute | solution.py:189
  46.4 4.5 %collective-permute-start.12 = (s16[24,1152]{1,0:T(8,128)(2,1)S(1)}, s16[24,1152]{1,0:T(8,128)(2,1)S(1)}, u32[]{:S(2)}, u32[]{:S(2)}) collective-permute-start(s16[24,1152]{1,0:T(8,128)(2,1)S(1)} %get-tuple-element.53), channel_id=1, source_target_pairs={{0,4},{4,0},{8,12},{12,8},{1,5},{5,1},{9,13},{13,9},{2,6},{6,2},{1... | collective-permute-start | bytes 165896 | tf_op jit(solution)/shard_map/ppermute | solution.py:189
  46.4 5.4 %collective-permute-start.13 = (s16[24,1152]{1,0:T(8,128)(2,1)S(1)}, s16[24,1152]{1,0:T(8,128)(2,1)S(1)}, u32[]{:S(2)}, u32[]{:S(2)}) collective-permute-start(s16[24,1152]{1,0:T(8,128)(2,1)S(1)} %get-tuple-element.54), channel_id=1, source_target_pairs={{0,8},{4,12},{8,0},{12,4},{1,9},{5,13},{9,1},{13,5},{2,10},{6,14},... | collective-permute-start | bytes 165896 | tf_op jit(solution)/shard_map/ppermute | solution.py:189
  49.7 6.0 %collective-permute-start.14 = (s16[24,1152]{1,0:T(8,128)(2,1)S(1)}, s16[24,1152]{1,0:T(8,128)(2,1)S(1)}, u32[]{:S(2)}, u32[]{:S(2)}) collective-permute-start(s16[24,1152]{1,0:T(8,128)(2,1)S(1)} %get-tuple-element.55), channel_id=1, source_target_pairs={{0,12},{4,8},{8,4},{12,0},{1,13},{5,9},{9,5},{13,1},{2,14},{6,10},... | collective-permute-start | bytes 165896 | tf_op jit(solution)/shard_map/ppermute | solution.py:189

commit v4 on v3

v4 whole, which is shorter than its diff:
```python
import functools

import jax
import jax.numpy as jnp
from jax import lax
from jax.experimental import pallas as pl
from jax.experimental.pallas import tpu as pltpu
from jax.sharding import PartitionSpec as P

HEAD = 128
LANES = 128
FULL = 32000.0
STEPS = 64.0
TINY = 1e-30


def encode(block):
    top = jnp.max(jnp.abs(block), axis=1, keepdims=True)
    code = jnp.ceil(jnp.log2(jnp.maximum(top, TINY)) * STEPS)
    coded = jnp.round(block * (jnp.exp2(code * (-1.0 / STEPS)) * FULL))
    return coded.astype(jnp.int32).astype(jnp.int16), code


def scale_of(codes):
    return jnp.exp2(codes.astype(jnp.int32).astype(jnp.float32) * (1.0 / STEPS)) * (1.0 / FULL)


def decode(coded, scale):
    return coded.astype(jnp.int32).astype(jnp.float32) * scale


def lane_of(rows):
    return lax.broadcasted_iota(jnp.int32, (rows, LANES), 1)


def load(offset, piece, copies, w_ref, out_ref, sems):
    rows = out_ref.shape[0]
    cores = lax.axis_size("kv")
    index = lax.rem(lax.axis_index("kv") + offset, cores)
    base = index * (w_ref.shape[0] // cores) + piece * rows
    step = rows // copies
    started = []
    for i in range(copies):
        start = pl.multiple_of(base + i * step, step)
        started.append(
            pltpu.make_async_copy(w_ref.at[pl.ds(start, step)], out_ref.at[pl.ds(i * step, step)], sems.at[i])
        )
    for copy in started:
        copy.start()
    for copy in started:
        copy.wait()


def take(rows_ref, *refs):
    out_refs, sems = refs[:-1], refs[-1]
    part = out_refs[0].shape[1]
    copies = []
    for j, out_ref in enumerate(out_refs):
        index = jnp.bitwise_xor(lax.axis_index("seq"), j) * lax.axis_size("kv") + lax.axis_index("kv")
        at = pl.ds(pl.multiple_of(index * part, part), part)
        copies.append(pltpu.make_async_copy(rows_ref.at[:, at], out_ref, sems.at[j]))
    for copy in copies:
        copy.start()
    for copy in copies:
        copy.wait()


def first_half(tile, rows_ref, w_ref, acc_ref):
    for first in range(0, acc_ref.shape[1], tile):
        at = slice(first, first + tile)
        acc_ref[:, at] = jnp.dot(rows_ref[...], w_ref[:, at], preferred_element_type=jnp.float32)


def second_half(row, rows, column, tile, rows_ref, w_ref, acc_ref, keep_ref, *send_refs):
    kept, width = keep_ref.shape
    size = send_refs[0].shape[0]
    codes = jnp.zeros((rows - kept, LANES), jnp.float32)
    lane = lane_of(rows - kept)
    for first in range(0, width, tile):
        at = slice(column + first, column + first + tile)
        total = acc_ref[row : row + rows, at]
        total = total + jnp.dot(rows_ref[row : row + rows, :], w_ref[:, at], preferred_element_type=jnp.float32)
        keep_ref[:, first : first + tile] = total[:kept]
        for begin in range(0, tile, HEAD):
            coded, code = encode(total[kept:, begin : begin + HEAD])
            head = (first + begin) // HEAD
            for i, ref in enumerate(send_refs):
                ref[:, head * HEAD : (head + 1) * HEAD] = coded[i * size : (i + 1) * size]
            codes = jnp.where(lane == head, code, codes)
    codes = codes.astype(jnp.int32).astype(jnp.int16)
    for i, ref in enumerate(send_refs):
        ref[:, width:] = codes[i * size : (i + 1) * size]


def middle(seqs, keep_ref, *refs):
    got_refs, out_refs = refs[: seqs - 1], refs[seqs - 1 :]
    rows, columns = keep_ref.shape
    tok = out_refs[0].shape[0]
    scales = [scale_of(ref[:, columns:]) for ref in got_refs]
    codes = jnp.zeros((rows, LANES), jnp.float32)
    lane = lane_of(rows)
    for head in range(columns // HEAD):
        at = slice(head * HEAD, (head + 1) * HEAD)
        total = keep_ref[:, at]
        for ref, scale in zip(got_refs, scales):
            total = total + decode(ref[:, at], scale[:, head : head + 1])
        coded, code = encode(total)
        codes = jnp.where(lane == head, code, codes)
        for k, ref in enumerate(out_refs):
            ref[:, at] = coded[k * tok : (k + 1) * tok]
    codes = codes.astype(jnp.int32).astype(jnp.int16)
    for k, ref in enumerate(out_refs):
        ref[:, columns:] = codes[k * tok : (k + 1) * tok]


def butterflies(blocks):
    blocks = list(blocks)
    span = 1
    while span < len(blocks):
        for i in range(len(blocks)):
            if not i & span:
                a, b = blocks[i], blocks[i + span]
                blocks[i], blocks[i + span] = a + b, a - b
        span *= 2
    return blocks


def parity_signs(both, bits):
    parity = jnp.zeros_like(both)
    for bit in range(bits):
        parity = parity + jnp.bitwise_and(jnp.right_shift(both, bit), 1)
    return (1 - 2 * jnp.bitwise_and(parity, 1)).astype(jnp.float32)


def local_part(first, chunks, groups, tok, cos_ref, sin_ref, bits_ref, stage):
    cosine, sine = cos_ref[...], sin_ref[...]
    both = lax.broadcasted_iota(jnp.int32, (HEAD, HEAD), 0) & lax.broadcasted_iota(jnp.int32, (HEAD, HEAD), 1)
    inner = parity_signs(both, 7).astype(jnp.bfloat16)
    heads = stage.shape[0] // tok // len(groups)
    columns, width = heads * HEAD, heads * HEAD // chunks
    for i, group in enumerate(groups):
        there = jnp.bitwise_xor(lax.axis_index("tensor"), first + i)
        flip = (1 - 2 * bits_ref[:, pl.ds(pl.multiple_of(there * columns, HEAD), columns)]).astype(jnp.float32)
        scales = [[scale_of(ref[:, width:]) if ref.shape[1] > width else None for ref in refs] for refs in group]
        for head in range(heads):
            chunk, inside = divmod(head, heads // chunks)
            at = slice(inside * HEAD, (inside + 1) * HEAD)
            block = None
            for ref, scale in zip(group[chunk], scales[chunk]):
                term = ref[:, at] if scale is None else decode(ref[:, at], scale[:, inside : inside + 1])
                block = term if block is None else block + term
            block = block * cosine + pltpu.roll(block, HEAD // 2, 1) * sine
            stage[pl.ds((i * heads + head) * tok, tok), :] = block * flip[:, head * HEAD : (head + 1) * HEAD]
    whole = stage[...]
    high = whole.astype(jnp.bfloat16)
    rest = whole - high.astype(jnp.float32)
    mid = rest.astype(jnp.bfloat16)
    low = (rest - mid.astype(jnp.float32)).astype(jnp.bfloat16)
    dot = functools.partial(jnp.dot, preferred_element_type=jnp.float32)
    stage[...] = dot(low, inner) + dot(mid, inner) + dot(high, inner)
    for i in range(len(groups)):
        blocks = [stage[pl.ds((i * heads + head) * tok, tok), :] for head in range(heads)]
        for head, block in enumerate(butterflies(blocks)):
            stage[pl.ds((i * heads + head) * tok, tok), :] = block


def early(near, tok, *refs):
    *block_refs, cos_ref, sin_ref, bits_ref, stage = refs
    groups = [[block_refs[k::near]] for k in range(near)]
    local_part(0, 1, groups, tok, cos_ref, sin_ref, bits_ref, stage)


def final(near, chunks, tok, near_ref, *refs):
    *block_refs, cos_ref, sin_ref, bits_ref, out_ref, top_ref, stage, whole = refs
    far = len(block_refs) // chunks
    count = near + far
    groups = [[[block_refs[chunk * far + k]] for chunk in range(chunks)] for k in range(far)]
    local_part(near, chunks, groups, tok, cos_ref, sin_ref, bits_ref, stage)
    heads = stage.shape[0] // tok // far
    norm = 1.0 / float(HEAD * heads * count) ** 0.5

    def place(k, head):
        ref, k = (near_ref, k) if k < near else (stage, k - near)
        return ref[pl.ds((k * heads + head) * tok, tok), :]

    top = jnp.zeros((tok, HEAD), jnp.float32)
    for head in range(heads):
        for k, block in enumerate(butterflies([place(k, head) for k in range(count)])):
            block = block * norm
            whole[pl.ds((k * heads + head) * tok, tok), :] = block
            top = jnp.maximum(top, jnp.abs(block))
    top = jnp.max(top, axis=1, keepdims=True)
    row = lax.broadcasted_iota(jnp.int32, (tok, HEAD), 0)
    line = jnp.sum(jnp.where(row == lane_of(tok), top, 0.0), axis=0, keepdims=True)
    top_ref[...] = line[:, :tok]
    inverse = 1.0 / (top + 1e-06)
    bits = (count - 1).bit_length()
    for k in range(count):
        factor = inverse * parity_signs(jnp.bitwise_and(lax.axis_index("tensor"), k), bits)
        for head in range(heads):
            at = pl.ds((k * heads + head) * HEAD, HEAD)
            out_ref[:, at] = (whole[pl.ds((k * heads + head) * tok, tok), :] * factor).astype(jnp.bfloat16)


def swap(array, axis, count, offset):
    return lax.ppermute(array, axis, [(i, i ^ offset) for i in range(count)])


def cross(array, seqs, tensors, j, k):
    pairs = [(i, (i // seqs ^ k) * seqs + (i % seqs ^ j)) for i in range(seqs * tensors)]
    return lax.ppermute(array, ("tensor", "seq"), pairs)


def per_device(hidden_rows, kv_weight, block_lengths, sign_bits):
    tok, depth = hidden_rows.shape
    rows_dev, columns = kv_weight.shape[1:]
    which, tensor_at, seq_at = (lax.axis_index(name) for name in ("kv", "tensor", "seq"))
    cores, tensors, seqs = (lax.axis_size(name) for name in ("kv", "tensor", "seq"))
    weight = pltpu.with_memory_space_constraint(kv_weight[0], pltpu.HBM)
    part = rows_dev // cores
    vmem = pl.BlockSpec(memory_space=pltpu.VMEM)
    hbm = pl.BlockSpec(memory_space=pltpu.HBM)
    chunks = 2 if columns >= 1024 else 1
    width = columns // chunks
    near = min(2, tensors)
    order = [(j, k) for j in range(seqs) for k in range(near)]
    order += [(j, k) for j in range(seqs) for k in range(near, tensors)]

    def local(kernel, outs, in_specs, limit, scratch=(), flops=0, moved=0):
        return pl.pallas_call(
            kernel,
            in_specs=in_specs,
            out_specs=jax.tree.map(lambda _: vmem, outs),
            out_shape=outs,
            scratch_shapes=scratch,
            compiler_params=pltpu.CompilerParams(vmem_limit_bytes=limit << 20),
            cost_estimate=pl.CostEstimate(flops=flops, bytes_accessed=moved, transcendentals=0),
        )

    def loaded(weight, offset):
        return local(
            functools.partial(load, offset, 0, 8),
            pltpu.VMEM((part, columns), weight.dtype),
            [hbm],
            4,
            [pltpu.SemaphoreType.DMA((8,))],
            moved=4 * part * columns,
        )(weight)

    index = jnp.arange(block_lengths.shape[0], dtype=jnp.int32)
    starts = jnp.sum(jnp.where(index[:, None] < index[None, :], block_lengths[:, None], 0), axis=0)
    glob = (tensor_at * seqs + seq_at) * tok + jnp.arange(tok, dtype=jnp.int32)
    hits = glob[:, None] >= starts[None, :]
    place = (glob - jnp.max(jnp.where(hits, starts[None, :], 0), axis=1)).astype(jnp.float32)
    freq = jnp.float32(1000000.0) ** (-2.0 * jnp.arange(HEAD // 2, dtype=jnp.float32) / HEAD)
    angle = place[:, None] * freq[None, :]
    cosine = jnp.where(which == 0, jnp.cos(angle), 1.0)
    sine = jnp.where(which == 0, jnp.sin(angle), 0.0)
    cosine = jnp.concatenate([cosine, cosine], axis=1)
    sine = jnp.concatenate([-sine, sine], axis=1)

    slices = local(
        take,
        [pltpu.VMEM((tok, part), hidden_rows.dtype)] * seqs,
        [hbm],
        4,
        [pltpu.SemaphoreType.DMA((seqs,))],
    )(pltpu.with_memory_space_constraint(hidden_rows, pltpu.HBM))
    blocks = {(0, 0): slices[0]}
    for j in range(1, seqs):
        blocks[j, 0] = cross(slices[j], seqs, tensors, j, 0)
    for k in range(near, tensors):
        for j in range(seqs):
            blocks[j, k] = cross(slices[j], seqs, tensors, j, k)
    pair = jnp.concatenate([blocks[j, 0] for j in range(seqs)], axis=0)
    for k in range(1, near):
        got = cross(pair, seqs, tensors, 0, k)
        for j in range(seqs):
            blocks[j, k] = got[j * tok : (j + 1) * tok]
    weight, cosine, sine, blocks[1, 0] = lax.optimization_barrier((weight, cosine, sine, blocks[1, 0]))
    halves = [loaded(weight, offset) for offset in range(cores)]
    mine = jnp.concatenate([blocks[at] for at in order], axis=0)
    mine, *halves = lax.optimization_barrier((mine, *halves))
    other = swap(mine, "kv", cores, 1)
    rows = mine.shape[0]
    tile = min(256, width)
    limit = 8 if rows < 1024 else 24
    acc = local(
        functools.partial(first_half, tile),
        jax.ShapeDtypeStruct((rows, columns), jnp.float32),
        [vmem] * 2,
        limit,
        flops=2 * rows * part * columns,
        moved=4 * rows * columns,
    )(mine, halves[0])

    def second(row, count, kept, column, width, sends):
        size = (count - kept) // sends
        return local(
            functools.partial(second_half, row, count, column, tile),
            [jax.ShapeDtypeStruct((kept, width), jnp.float32)]
            + [jax.ShapeDtypeStruct((size, width + LANES), jnp.int16)] * sends,
            [vmem] * 3,
            limit,
            flops=2 * count * part * width,
            moved=8 * count * width,
        )(other, halves[1], acc)

    begin = seqs * near * tok
    away = (tensors - near) * tok
    far = []
    for chunk in range(chunks):
        keep, *sends = second(begin, rows - begin, away, chunk * width, width, seqs - 1)
        got = [cross(send, seqs, tensors, j, 0) for j, send in enumerate(sends, 1)]
        parts = local(
            functools.partial(middle, seqs),
            [jax.ShapeDtypeStruct((tok, width + LANES), jnp.int16)] * (tensors - near),
            [vmem] * seqs,
            limit,
            moved=8 * away * width,
        )(keep, *got)
        far += [cross(array, seqs, tensors, 0, k) for k, array in enumerate(parts, near)]
    keep, *sends = second(0, begin, tok, 0, columns, seqs * near - 1)
    direct = [keep] + [cross(send, seqs, tensors, *order[i]) for i, send in enumerate(sends, 1)]

    tables = cosine, sine, sign_bits[None]
    heads = columns // HEAD
    size = heads * tok * HEAD
    ready = local(
        functools.partial(early, near, tok),
        jax.ShapeDtypeStruct((near * heads * tok, HEAD), jnp.float32),
        [vmem] * (seqs * near + 3),
        16,
        flops=6 * near * size * HEAD,
        moved=8 * near * size,
    )(*direct, *tables)
    cache, top = local(
        functools.partial(final, near, chunks, tok),
        [
            jax.ShapeDtypeStruct((tok, depth), jnp.bfloat16),
            jax.ShapeDtypeStruct((1, tok), jnp.float32),
        ],
        [vmem] * ((tensors - near) * chunks + 4),
        16,
        [pltpu.VMEM((count * heads * tok, HEAD), jnp.float32) for count in (tensors - near, tensors)],
        moved=8 * tensors * size,
    )(ready, *far, *tables)
    return (cache[None], top)


def solution(mesh):
    return jax.shard_map(
        per_device,
        mesh=mesh,
        in_specs=(P(("groups", "tensor", "seq"), None), P("kv", "seq", "tensor"), P("groups"), P()),
        out_specs=(
            P("kv", ("groups", "tensor", "seq"), None),
            P("kv", ("groups", "tensor", "seq")),
        ),
        check_vma=False,
    )
```

time: 57.9 us -> 50 us (0.86)
  waiting for transfers between devices: 19.5 us -> 7.02 us
  starting transfers between devices: 20.5 us -> 24.1 us
  Pallas kernels: 15.6 us -> 16.8 us
    ppermute x2 -> x15, starting transfers between devices: 1.95 us -> 24 us  [cross(): return lax.ppermute(array, ('tensor', 'seq'), pairs)]
    ppermute x13 -> x1, starting transfers between devices: 18.6 us -> 0.07 us  [swap(): return lax.ppermute(array, axis, [(i, i ^ offset) for i in range(count)])]
    ppermute x13 -> x1, waiting for transfers between devices: 15.5 us -> 0.42 us  [swap(): return lax.ppermute(array, axis, [(i, i ^ offset) for i in range(count)])]
    ppermute x2 -> x15, waiting for transfers between devices: 4.07 us -> 6.6 us  [cross(): return lax.ppermute(array, ('tensor', 'seq'), pairs)]
    pallas_call x8 -> x10, Pallas kernels: 13.8 us -> 14.9 us  [the longest x2 6.97 us: loaded(): local(functools.partial(load, offset, 0, 8), pltpu.VMEM((part, columns),...]
  transfers between devices with their start and end apart: 15 -> 16, of which waited for: 8 -> 5; matrix products, arithmetic and copies ran while one was open for 2% -> 2% of each run, Pallas kernels for 20% -> 26%
where the time goes in v4:
time: 50 us; the launch traced here: 49.9 us
  starting transfers between devices  24.1 us (48%)
  Pallas kernels  16.8 us (34%)
  waiting for transfers between devices  7.02 us (14%)
  other arithmetic  1.08 us (2%)
  between operations  0.84 us (2%)
    ppermute x15, starting transfers between devices, cross(): return lax.ppermute(array, ('tensor', 'seq'), pairs)  24 us
    pallas_call x2, Pallas kernels, loaded(): local(functools.partial(load, offset, 0, 8), pltpu.VMEM((part, columns),...  6.97 us
    ppermute x15, waiting for transfers between devices, cross(): return lax.ppermute(array, ('tensor', 'seq'), pairs)  6.6 us
    pallas_call x3, Pallas kernels, second(): local(functools.partial(second_half, row, count, column, tile), [jax.Shap...  3.57 us
    pallas_call x1, Pallas kernels, per_device(): local(functools.partial(first_half, tile), jax.ShapeDtypeStruct((rows, co...  1.84 us
    pallas_call x1, Pallas kernels, per_device(): local(functools.partial(final, near, chunks, tok), [jax.ShapeDtypeStruct(...  1.69 us
    pallas_call x2, Pallas kernels, per_device(): local(functools.partial(middle, seqs), [jax.ShapeDtypeStruct((tok, width...  1.12 us
  transfers between devices with their start and end apart: 16, of which 5 were waited for; matrix products, arithmetic and copies ran while one was open for 2% of the time, Pallas kernels for 26%

profile of v4, /device:TPU:0, one launch (start us, length us, event | category | flops | bytes accessed | tf_op | source)
XLA Modules:
  0.0 49.9 jit_solution(1680811690022675081)
XLA Ops:
  0.6 1.0 %shard_map.59 = (bf16[24,2048]{1,0:T(8,128)(2,1)S(1)}, bf16[24,2048]{1,0:T(8,128)(2,1)S(1)}) custom-call(bf16[24,8192]{1,0:T(8,128)(2,1)} %rows_ref.1), custom_call_target="tpu_custom_call" | custom-call | tf_op jit(solution)/shard_map/pallas_call | solution.py:262
  1.6 6.0 %collective-permute-start.5 = (bf16[24,2048]{1,0:T(8,128)(2,1)S(1)}, bf16[24,2048]{1,0:T(8,128)(2,1)S(1)}, u32[]{:S(2)}, u32[]{:S(2)}) collective-permute-start(bf16[24,2048]{1,0:T(8,128)(2,1)S(1)} %get-tuple-element.26), channel_id=1, source_target_pairs={{0,14},{2,12},{4,10},{6,8},{8,6},{10,4},{12,2},{14,0},{1,15},{3,13... | collective-permute-start | bytes 294920 | tf_op jit(solution)/shard_map/ppermute | solution.py:211
  7.6 0.0 collective-permute-start.4
  7.7 0.9 %collective-permute-start = (bf16[24,2048]{1,0:T(8,128)(2,1)S(1)}, bf16[24,2048]{1,0:T(8,128)(2,1)S(1)}, u32[]{:S(2)}, u32[]{:S(2)}) collective-permute-start(bf16[24,2048]{1,0:T(8,128)(2,1)S(1)} %get-tuple-element.26), channel_id=1, source_target_pairs={{0,2},{2,0},{4,6},{6,4},{8,10},{10,8},{12,14},{14,12},{1,3},{3,1},... | collective-permute-start | bytes 294920 | tf_op jit(solution)/shard_map/ppermute | solution.py:211
  8.5 2.5 %collective-permute-start.3 = (bf16[24,2048]{1,0:T(8,128)(2,1)S(1)}, bf16[24,2048]{1,0:T(8,128)(2,1)S(1)}, u32[]{:S(2)}, u32[]{:S(2)}) collective-permute-start(bf16[24,2048]{1,0:T(8,128)(2,1)S(1)} %get-tuple-element.25), channel_id=1, source_target_pairs={{0,12},{2,14},{4,8},{6,10},{8,4},{10,6},{12,0},{14,2},{1,13},{3,15... | collective-permute-start | bytes 294920 | tf_op jit(solution)/shard_map/ppermute | solution.py:211
  11.0 1.0 %collective-permute-start.2 = (bf16[24,2048]{1,0:T(8,128)(2,1)S(1)}, bf16[24,2048]{1,0:T(8,128)(2,1)S(1)}, u32[]{:S(2)}, u32[]{:S(2)}) collective-permute-start(bf16[24,2048]{1,0:T(8,128)(2,1)S(1)} %get-tuple-element.25), channel_id=1, source_target_pairs={{0,8},{2,10},{4,12},{6,14},{8,0},{10,2},{12,4},{14,6},{1,9},{3,11}... | collective-permute-start | bytes 294920 | tf_op jit(solution)/shard_map/ppermute | solution.py:211
  12.1 0.7 %select_reduce_fusion.1 = s32[4]{0:T(128)S(1)} fusion(s32[4]{0:T(128)} %param.6), kind=kLoop, calls=%fused_computation.17 | loop fusion | flops 44 | bytes 32 | tf_op jit(solution)/shard_map/reduce_sum | solution.py:251
  12.8 0.1 select_reduce_fusion
  12.9 0.1 fusion.2
  13.0 0.1 pad_maximum_fusion.1
  13.1 0.0 collective-permute-done
  13.1 1.9 %collective-permute-start.1 = (bf16[48,2048]{1,0:T(8,128)(2,1)S(1)}, bf16[48,2048]{1,0:T(8,128)(2,1)S(1)}, u32[]{:S(2)}, u32[]{:S(2)}) collective-permute-start(bf16[48,2048]{1,0:T(8,128)(2,1)S(1)} %pad_maximum_fusion), channel_id=1, source_target_pairs={{0,4},{2,6},{4,0},{6,2},{8,12},{10,14},{12,8},{14,10},{1,5},{3,7},... | collective-permute-start | bytes 589832 | tf_op jit(solution)/shard_map/ppermute | solution.py:211
  15.1 3.5 %shard_map.61.w_ref = bf16[2048,2048]{1,0:T(8,128)(2,1)S(1)} custom-call(bf16[4096,2048]{1,0:T(8,128)(2,1)} %bitcast.5), custom_call_target="tpu_custom_call" | custom-call | bytes 16777216 | tf_op jit(solution)/shard_map/pallas_call | solution.py:241
  18.5 3.5 %shard_map.60.w_ref = bf16[2048,2048]{1,0:T(8,128)(2,1)S(1)} custom-call(bf16[4096,2048]{1,0:T(8,128)(2,1)} %bitcast.6), custom_call_target="tpu_custom_call" | custom-call | bytes 16777216 | tf_op jit(solution)/shard_map/pallas_call | solution.py:241
  22.0 0.1 collective-permute-done.1
  22.2 2.2 %collective-permute-done.2 = bf16[24,2048]{1,0:T(8,128)(2,1)S(1)} collective-permute-done((bf16[24,2048]{1,0:T(8,128)(2,1)S(1)}, bf16[24,2048]{1,0:T(8,128)(2,1)S(1)}, u32[]{:S(2)}, u32[]{:S(2)}) %collective-permute-start.2) | collective-permute-done | bytes 98336 | tf_op jit(solution)/shard_map/ppermute | solution.py:211
  24.4 0.0 collective-permute-done.3
  24.4 0.0 collective-permute-done.4
  24.4 0.0 collective-permute-done.5
  24.4 0.1 collective-permute-start.6
  24.5 1.8 %shard_map.62.acc_ref = f32[192,2048]{1,0:T(8,128)S(1)} custom-call(bf16[192,2048]{1,0:T(8,128)(2,1)S(1)} %constant_dynamic-update-slice_fusion.rows_ref, bf16[2048,2048]{1,0:T(8,128)(2,1)S(1)} %shard_map.60.w_ref), custom_call_target="tpu_custom_call" | custom-call | flops 1610612736 | bytes 1572864 | tf_op jit(solution)/shard_map/pallas_call | solution.py:288
  26.4 0.4 collective-permute-done.6.rows_ref
  26.8 0.9 %shard_map.67 = (f32[48,1024]{1,0:T(8,128)S(1)}, s16[48,1152]{1,0:T(8,128)(2,1)S(1)}) custom-call(bf16[192,2048]{1,0:T(8,128)(2,1)S(1)} %collective-permute-done.6.rows_ref, bf16[2048,2048]{1,0:T(8,128)(2,1)S(1)} %shard_map.61.w_ref, f32[192,2048]{1,0:T(8,128)S(1)} %shard_map.62.acc_ref), custom_call_target="tpu_custom_call" | custom-call | flops 402653184 | bytes 786432 | tf_op jit(solution)/shard_map/pallas_call | solution.py:299
  27.7 0.0 copy-start
  27.7 0.8 %collective-permute-start.13 = (s16[48,1152]{1,0:T(8,128)(2,1)S(1)}, s16[48,1152]{1,0:T(8,128)(2,1)S(1)}, u32[]{:S(2)}, u32[]{:S(2)}) collective-permute-start(s16[48,1152]{1,0:T(8,128)(2,1)S(1)} %get-tuple-element.43), channel_id=1, source_target_pairs={{0,2},{2,0},{4,6},{6,4},{8,10},{10,8},{12,14},{14,12},{1,3},{3,1},... | collective-permute-start | bytes 331784 | tf_op jit(solution)/shard_map/ppermute | solution.py:211
  28.5 0.9 %shard_map.65 = (f32[48,1024]{1,0:T(8,128)S(1)}, s16[48,1152]{1,0:T(8,128)(2,1)S(1)}) custom-call(bf16[192,2048]{1,0:T(8,128)(2,1)S(1)} %collective-permute-done.6.rows_ref, bf16[2048,2048]{1,0:T(8,128)(2,1)S(1)} %shard_map.61.w_ref, f32[192,2048]{1,0:T(8,128)S(1)} %shard_map.62.acc_ref), custom_call_target="tpu_custom_call" | custom-call | flops 402653184 | bytes 786432 | tf_op jit(solution)/shard_map/pallas_call | solution.py:299
  29.5 1.4 %collective-permute-start.10 = (s16[48,1152]{1,0:T(8,128)(2,1)S(1)}, s16[48,1152]{1,0:T(8,128)(2,1)S(1)}, u32[]{:S(2)}, u32[]{:S(2)}) collective-permute-start(s16[48,1152]{1,0:T(8,128)(2,1)S(1)} %get-tuple-element.39), channel_id=1, source_target_pairs={{0,2},{2,0},{4,6},{6,4},{8,10},{10,8},{12,14},{14,12},{1,3},{3,1},... | collective-permute-start | bytes 331784 | tf_op jit(solution)/shard_map/ppermute | solution.py:211
  30.9 1.7 %shard_map.63 = (f32[24,2048]{1,0:T(8,128)S(1)}, s16[24,2176]{1,0:T(8,128)(2,1)S(1)}, s16[24,2176]{1,0:T(8,128)(2,1)S(1)}, s16[24,2176]{1,0:T(8,128)(2,1)S(1)}) custom-call(bf16[192,2048]{1,0:T(8,128)(2,1)S(1)} %collective-permute-done.6.rows_ref, bf16[2048,2048]{1,0:T(8,128)(2,1)S(1)} %shard_map.61.w_ref, f32[192,2048]{1,0:T(8,128)S(1)} %shard_map.62.acc_ref), custom_call_target="tpu_custom_call" | custom-call | flops 805306368 | bytes 1572864 | tf_op jit(solution)/shard_map/pallas_call | solution.py:299
  32.5 0.1 collective-permute-start.7
  32.6 0.8 %collective-permute-start.8 = (s16[24,2176]{1,0:T(8,128)(2,1)S(1)}, s16[24,2176]{1,0:T(8,128)(2,1)S(1)}, u32[]{:S(2)}, u32[]{:S(2)}) collective-permute-start(s16[24,2176]{1,0:T(8,128)(2,1)S(1)} %get-tuple-element.34), channel_id=1, source_target_pairs={{0,2},{2,0},{4,6},{6,4},{8,10},{10,8},{12,14},{14,12},{1,3},{3,1},... | collective-permute-start | bytes 313352 | tf_op jit(solution)/shard_map/ppermute | solution.py:211
  33.4 2.7 %collective-permute-start.9 = (s16[24,2176]{1,0:T(8,128)(2,1)S(1)}, s16[24,2176]{1,0:T(8,128)(2,1)S(1)}, u32[]{:S(2)}, u32[]{:S(2)}) collective-permute-start(s16[24,2176]{1,0:T(8,128)(2,1)S(1)} %get-tuple-element.35), channel_id=1, source_target_pairs={{0,6},{2,4},{4,2},{6,0},{8,14},{10,12},{12,10},{14,8},{1,7},{3,5},... | collective-permute-start | bytes 313352 | tf_op jit(solution)/shard_map/ppermute | solution.py:211
  36.1 0.0 collective-permute-done.13.refs_0_
  36.1 0.6 %shard_map.68 = (s16[24,1152]{1,0:T(8,128)(2,1)S(1)}, s16[24,1152]{1,0:T(8,128)(2,1)S(1)}) custom-call(f32[48,1024]{1,0:T(8,128)S(1)} %get-tuple-element.42.keep_ref, s16[48,1152]{1,0:T(8,128)(2,1)S(1)} %collective-permute-done.13.refs_0_), custom_call_target="tpu_custom_call" | custom-call | bytes 393216 | tf_op jit(solution)/shard_map/pallas_call | solution.py:315
  36.7 1.2 %collective-permute-start.14 = (s16[24,1152]{1,0:T(8,128)(2,1)S(1)}, s16[24,1152]{1,0:T(8,128)(2,1)S(1)}, u32[]{:S(2)}, u32[]{:S(2)}) collective-permute-start(s16[24,1152]{1,0:T(8,128)(2,1)S(1)} %get-tuple-element.44), channel_id=1, source_target_pairs={{0,8},{2,10},{4,12},{6,14},{8,0},{10,2},{12,4},{14,6},{1,9},{3,11}... | collective-permute-start | bytes 165896 | tf_op jit(solution)/shard_map/ppermute | solution.py:211
  37.9 0.0 collective-permute-done.10.refs_0_
  37.9 1.5 %collective-permute-start.15 = (s16[24,1152]{1,0:T(8,128)(2,1)S(1)}, s16[24,1152]{1,0:T(8,128)(2,1)S(1)}, u32[]{:S(2)}, u32[]{:S(2)}) collective-permute-start(s16[24,1152]{1,0:T(8,128)(2,1)S(1)} %get-tuple-element.45), channel_id=1, source_target_pairs={{0,12},{2,14},{4,8},{6,10},{8,4},{10,6},{12,0},{14,2},{1,13},{3,15... | collective-permute-start | bytes 165896 | tf_op jit(solution)/shard_map/ppermute | solution.py:211
  39.3 0.6 %shard_map.66 = (s16[24,1152]{1,0:T(8,128)(2,1)S(1)}, s16[24,1152]{1,0:T(8,128)(2,1)S(1)}) custom-call(f32[48,1024]{1,0:T(8,128)S(1)} %get-tuple-element.38.keep_ref, s16[48,1152]{1,0:T(8,128)(2,1)S(1)} %collective-permute-done.10.refs_0_), custom_call_target="tpu_custom_call" | custom-call | bytes 393216 | tf_op jit(solution)/shard_map/pallas_call | solution.py:315
  39.9 0.0 collective-permute-done.7.refs_1_
  39.9 2.0 %collective-permute-start.11 = (s16[24,1152]{1,0:T(8,128)(2,1)S(1)}, s16[24,1152]{1,0:T(8,128)(2,1)S(1)}, u32[]{:S(2)}, u32[]{:S(2)}) collective-permute-start(s16[24,1152]{1,0:T(8,128)(2,1)S(1)} %get-tuple-element.40), channel_id=1, source_target_pairs={{0,8},{2,10},{4,12},{6,14},{8,0},{10,2},{12,4},{14,6},{1,9},{3,11}... | collective-permute-start | bytes 165896 | tf_op jit(solution)/shard_map/ppermute | solution.py:211
  41.9 0.0 collective-permute-done.8.refs_2_
  41.9 1.3 %collective-permute-start.12 = (s16[24,1152]{1,0:T(8,128)(2,1)S(1)}, s16[24,1152]{1,0:T(8,128)(2,1)S(1)}, u32[]{:S(2)}, u32[]{:S(2)}) collective-permute-start(s16[24,1152]{1,0:T(8,128)(2,1)S(1)} %get-tuple-element.41), channel_id=1, source_target_pairs={{0,12},{2,14},{4,8},{6,10},{8,4},{10,6},{12,0},{14,2},{1,13},{3,15... | collective-permute-start | bytes 165896 | tf_op jit(solution)/shard_map/ppermute | solution.py:211
  43.2 0.0 collective-permute-done.9.refs_3_
  43.2 0.6 %shard_map.64.near_ref = f32[768,128]{1,0:T(8,128)S(1)} custom-call(f32[24,2048]{1,0:T(8,128)S(1)} %get-tuple-element.32.refs_0_, s16[24,2176]{1,0:T(8,128)(2,1)S(1)} %collective-permute-done.7.refs_1_, s16[24,2176]{1,0:T(8,128)(2,1)S(1)} %collective-permute-done.8.refs_2_, s16[24,2176]{1,0:T(8,128)(2,1)S(1)} %collective-permute-done.9.refs_3_, ...), custom_call_target="tpu_custom_call" | custom-call | flops 75497472 | bytes 786432 | tf_op jit(solution)/shard_map/pallas_call | solution.py:329
  43.9 1.6 %collective-permute-done.14.refs_2_ = s16[24,1152]{1,0:T(8,128)(2,1)S(1)} collective-permute-done((s16[24,1152]{1,0:T(8,128)(2,1)S(1)}, s16[24,1152]{1,0:T(8,128)(2,1)S(1)}, u32[]{:S(2)}, u32[]{:S(2)}) %collective-permute-start.14) | collective-permute-done | bytes 55328 | tf_op jit(solution)/shard_map/ppermute | solution.py:211
  45.5 0.0 collective-permute-done.15.refs_3_
  45.5 2.7 %collective-permute-done.11.refs_0_ = s16[24,1152]{1,0:T(8,128)(2,1)S(1)} collective-permute-done((s16[24,1152]{1,0:T(8,128)(2,1)S(1)}, s16[24,1152]{1,0:T(8,128)(2,1)S(1)}, u32[]{:S(2)}, u32[]{:S(2)}) %collective-permute-start.11) | collective-permute-done | bytes 55328 | tf_op jit(solution)/shard_map/ppermute | solution.py:211
  48.2 0.0 collective-permute-done.12.refs_1_
  48.2 1.7 %shard_map.69 = (bf16[24,8192]{1,0:T(8,128)(2,1)}, f32[1,24]{1,0:T(1,128)}) custom-call(f32[768,128]{1,0:T(8,128)S(1)} %shard_map.64.near_ref, s16[24,1152]{1,0:T(8,128)(2,1)S(1)} %collective-permute-done.11.refs_0_, s16[24,1152]{1,0:T(8,128)(2,1)S(1)} %collective-permute-done.12.refs_1_, s16[24,1152]{1,0:T(8,128)(2,1)S(1)} %collective-permute-done.14.refs_2_, ...), custom_call_target="tpu_custom_call" | custom-call | bytes 1572864 | tf_op jit(solution)/shard_map/pallas_call | solution.py:337
  (13 shorter events, 0.1 us)
Async XLA Ops:
  1.6 22.8 %collective-permute-start.5 = (bf16[24,2048]{1,0:T(8,128)(2,1)S(1)}, bf16[24,2048]{1,0:T(8,128)(2,1)S(1)}, u32[]{:S(2)}, u32[]{:S(2)}) collective-permute-start(bf16[24,2048]{1,0:T(8,128)(2,1)S(1)} %get-tuple-element.26), channel_id=1, source_target_pairs={{0,14},{2,12},{4,10},{6,8},{8,6},{10,4},{12,2},{14,0},{1,15},{3,13... | collective-permute-start | bytes 294920 | tf_op jit(solution)/shard_map/ppermute | solution.py:211
  7.6 16.7 %collective-permute-start.4 = (bf16[24,2048]{1,0:T(8,128)(2,1)S(1)}, bf16[24,2048]{1,0:T(8,128)(2,1)S(1)}, u32[]{:S(2)}, u32[]{:S(2)}) collective-permute-start(bf16[24,2048]{1,0:T(8,128)(2,1)S(1)} %get-tuple-element.26), channel_id=1, source_target_pairs={{0,10},{2,8},{4,14},{6,12},{8,2},{10,0},{12,6},{14,4},{1,11},{3,9}... | collective-permute-start | bytes 294920 | tf_op jit(solution)/shard_map/ppermute | solution.py:211
  7.7 5.5 %collective-permute-start = (bf16[24,2048]{1,0:T(8,128)(2,1)S(1)}, bf16[24,2048]{1,0:T(8,128)(2,1)S(1)}, u32[]{:S(2)}, u32[]{:S(2)}) collective-permute-start(bf16[24,2048]{1,0:T(8,128)(2,1)S(1)} %get-tuple-element.26), channel_id=1, source_target_pairs={{0,2},{2,0},{4,6},{6,4},{8,10},{10,8},{12,14},{14,12},{1,3},{3,1},... | collective-permute-start | bytes 294920 | tf_op jit(solution)/shard_map/ppermute | solution.py:211
  8.5 15.8 %collective-permute-start.3 = (bf16[24,2048]{1,0:T(8,128)(2,1)S(1)}, bf16[24,2048]{1,0:T(8,128)(2,1)S(1)}, u32[]{:S(2)}, u32[]{:S(2)}) collective-permute-start(bf16[24,2048]{1,0:T(8,128)(2,1)S(1)} %get-tuple-element.25), channel_id=1, source_target_pairs={{0,12},{2,14},{4,8},{6,10},{8,4},{10,6},{12,0},{14,2},{1,13},{3,15... | collective-permute-start | bytes 294920 | tf_op jit(solution)/shard_map/ppermute | solution.py:211
  11.0 13.3 %collective-permute-start.2 = (bf16[24,2048]{1,0:T(8,128)(2,1)S(1)}, bf16[24,2048]{1,0:T(8,128)(2,1)S(1)}, u32[]{:S(2)}, u32[]{:S(2)}) collective-permute-start(bf16[24,2048]{1,0:T(8,128)(2,1)S(1)} %get-tuple-element.25), channel_id=1, source_target_pairs={{0,8},{2,10},{4,12},{6,14},{8,0},{10,2},{12,4},{14,6},{1,9},{3,11}... | collective-permute-start | bytes 294920 | tf_op jit(solution)/shard_map/ppermute | solution.py:211
  13.1 9.0 %collective-permute-start.1 = (bf16[48,2048]{1,0:T(8,128)(2,1)S(1)}, bf16[48,2048]{1,0:T(8,128)(2,1)S(1)}, u32[]{:S(2)}, u32[]{:S(2)}) collective-permute-start(bf16[48,2048]{1,0:T(8,128)(2,1)S(1)} %pad_maximum_fusion), channel_id=1, source_target_pairs={{0,4},{2,6},{4,0},{6,2},{8,12},{10,14},{12,8},{14,10},{1,5},{3,7},... | collective-permute-start | bytes 589832 | tf_op jit(solution)/shard_map/ppermute | solution.py:211
  24.4 2.4 %collective-permute-start.6 = (bf16[192,2048]{1,0:T(8,128)(2,1)S(1)}, bf16[192,2048]{1,0:T(8,128)(2,1)S(1)}, u32[]{:S(2)}, u32[]{:S(2)}) collective-permute-start(bf16[192,2048]{1,0:T(8,128)(2,1)S(1)} %constant_dynamic-update-slice_fusion.rows_ref), channel_id=1, source_target_pairs={{0,1},{1,0},{2,3},{3,2},{4,5},{5,4},{6,7},{7,6},{8,9},{9,8},{10,11... | collective-permute-start | bytes 2359304 | tf_op jit(solution)/shard_map/ppermute | solution.py:206
  27.7 15.5 %copy-start = (s32[8192]{0:T(1024)S(1)}, s32[8192]{0:T(1024)}, u32[]{:S(2)}) copy-start(s32[8192]{0:T(1024)} %param.7) | copy-start | bytes 98308
  27.7 8.4 %collective-permute-start.13 = (s16[48,1152]{1,0:T(8,128)(2,1)S(1)}, s16[48,1152]{1,0:T(8,128)(2,1)S(1)}, u32[]{:S(2)}, u32[]{:S(2)}) collective-permute-start(s16[48,1152]{1,0:T(8,128)(2,1)S(1)} %get-tuple-element.43), channel_id=1, source_target_pairs={{0,2},{2,0},{4,6},{6,4},{8,10},{10,8},{12,14},{14,12},{1,3},{3,1},... | collective-permute-start | bytes 331784 | tf_op jit(solution)/shard_map/ppermute | solution.py:211
  29.5 8.4 %collective-permute-start.10 = (s16[48,1152]{1,0:T(8,128)(2,1)S(1)}, s16[48,1152]{1,0:T(8,128)(2,1)S(1)}, u32[]{:S(2)}, u32[]{:S(2)}) collective-permute-start(s16[48,1152]{1,0:T(8,128)(2,1)S(1)} %get-tuple-element.39), channel_id=1, source_target_pairs={{0,2},{2,0},{4,6},{6,4},{8,10},{10,8},{12,14},{14,12},{1,3},{3,1},... | collective-permute-start | bytes 331784 | tf_op jit(solution)/shard_map/ppermute | solution.py:211
  32.5 7.4 %collective-permute-start.7 = (s16[24,2176]{1,0:T(8,128)(2,1)S(1)}, s16[24,2176]{1,0:T(8,128)(2,1)S(1)}, u32[]{:S(2)}, u32[]{:S(2)}) collective-permute-start(s16[24,2176]{1,0:T(8,128)(2,1)S(1)} %get-tuple-element.33), channel_id=1, source_target_pairs={{0,4},{2,6},{4,0},{6,2},{8,12},{10,14},{12,8},{14,10},{1,5},{3,7},... | collective-permute-start | bytes 313352 | tf_op jit(solution)/shard_map/ppermute | solution.py:211
  32.6 9.3 %collective-permute-start.8 = (s16[24,2176]{1,0:T(8,128)(2,1)S(1)}, s16[24,2176]{1,0:T(8,128)(2,1)S(1)}, u32[]{:S(2)}, u32[]{:S(2)}) collective-permute-start(s16[24,2176]{1,0:T(8,128)(2,1)S(1)} %get-tuple-element.34), channel_id=1, source_target_pairs={{0,2},{2,0},{4,6},{6,4},{8,10},{10,8},{12,14},{14,12},{1,3},{3,1},... | collective-permute-start | bytes 313352 | tf_op jit(solution)/shard_map/ppermute | solution.py:211
  33.4 9.9 %collective-permute-start.9 = (s16[24,2176]{1,0:T(8,128)(2,1)S(1)}, s16[24,2176]{1,0:T(8,128)(2,1)S(1)}, u32[]{:S(2)}, u32[]{:S(2)}) collective-permute-start(s16[24,2176]{1,0:T(8,128)(2,1)S(1)} %get-tuple-element.35), channel_id=1, source_target_pairs={{0,6},{2,4},{4,2},{6,0},{8,14},{10,12},{12,10},{14,8},{1,7},{3,5},... | collective-permute-start | bytes 313352 | tf_op jit(solution)/shard_map/ppermute | solution.py:211
  36.7 8.9 %collective-permute-start.14 = (s16[24,1152]{1,0:T(8,128)(2,1)S(1)}, s16[24,1152]{1,0:T(8,128)(2,1)S(1)}, u32[]{:S(2)}, u32[]{:S(2)}) collective-permute-start(s16[24,1152]{1,0:T(8,128)(2,1)S(1)} %get-tuple-element.44), channel_id=1, source_target_pairs={{0,8},{2,10},{4,12},{6,14},{8,0},{10,2},{12,4},{14,6},{1,9},{3,11}... | collective-permute-start | bytes 165896 | tf_op jit(solution)/shard_map/ppermute | solution.py:211
  37.9 7.7 %collective-permute-start.15 = (s16[24,1152]{1,0:T(8,128)(2,1)S(1)}, s16[24,1152]{1,0:T(8,128)(2,1)S(1)}, u32[]{:S(2)}, u32[]{:S(2)}) collective-permute-start(s16[24,1152]{1,0:T(8,128)(2,1)S(1)} %get-tuple-element.45), channel_id=1, source_target_pairs={{0,12},{2,14},{4,8},{6,10},{8,4},{10,6},{12,0},{14,2},{1,13},{3,15... | collective-permute-start | bytes 165896 | tf_op jit(solution)/shard_map/ppermute | solution.py:211
  39.9 8.3 %collective-permute-start.11 = (s16[24,1152]{1,0:T(8,128)(2,1)S(1)}, s16[24,1152]{1,0:T(8,128)(2,1)S(1)}, u32[]{:S(2)}, u32[]{:S(2)}) collective-permute-start(s16[24,1152]{1,0:T(8,128)(2,1)S(1)} %get-tuple-element.40), channel_id=1, source_target_pairs={{0,8},{2,10},{4,12},{6,14},{8,0},{10,2},{12,4},{14,6},{1,9},{3,11}... | collective-permute-start | bytes 165896 | tf_op jit(solution)/shard_map/ppermute | solution.py:211
  41.9 6.3 %collective-permute-start.12 = (s16[24,1152]{1,0:T(8,128)(2,1)S(1)}, s16[24,1152]{1,0:T(8,128)(2,1)S(1)}, u32[]{:S(2)}, u32[]{:S(2)}) collective-permute-start(s16[24,1152]{1,0:T(8,128)(2,1)S(1)} %get-tuple-element.41), channel_id=1, source_target_pairs={{0,12},{2,14},{4,8},{6,10},{8,4},{10,6},{12,0},{14,2},{1,13},{3,15... | collective-permute-start | bytes 165896 | tf_op jit(solution)/shard_map/ppermute | solution.py:211

commit v5 on v4

--- a/solution.py
+++ b/solution.py
@@ -65,10 +65,10 @@
         copy.wait()
 
 
-def first_half(tile, rows_ref, w_ref, acc_ref):
+def first_half(row, rows, tile, rows_ref, w_ref, acc_ref):
     for first in range(0, acc_ref.shape[1], tile):
         at = slice(first, first + tile)
-        acc_ref[:, at] = jnp.dot(rows_ref[...], w_ref[:, at], preferred_element_type=jnp.float32)
+        acc_ref[:, at] = jnp.dot(rows_ref[row : row + rows, :], w_ref[:, at], preferred_element_type=jnp.float32)
 
 
 def second_half(row, rows, column, tile, rows_ref, w_ref, acc_ref, keep_ref, *send_refs):
@@ -220,8 +220,7 @@
     part = rows_dev // cores
     vmem = pl.BlockSpec(memory_space=pltpu.VMEM)
     hbm = pl.BlockSpec(memory_space=pltpu.HBM)
-    chunks = 2 if columns >= 1024 else 1
-    width = columns // chunks
+    chunks = 1
     near = min(2, tensors)
     order = [(j, k) for j in range(seqs) for k in range(near)]
     order += [(j, k) for j in range(seqs) for k in range(near, tensors)]
@@ -279,48 +278,46 @@
             blocks[j, k] = got[j * tok : (j + 1) * tok]
     weight, cosine, sine, blocks[1, 0] = lax.optimization_barrier((weight, cosine, sine, blocks[1, 0]))
     halves = [loaded(weight, offset) for offset in range(cores)]
+    begin = seqs * near * tok
     mine = jnp.concatenate([blocks[at] for at in order], axis=0)
     mine, *halves = lax.optimization_barrier((mine, *halves))
-    other = swap(mine, "kv", cores, 1)
-    rows = mine.shape[0]
-    tile = min(256, width)
-    limit = 8 if rows < 1024 else 24
-    acc = local(
-        functools.partial(first_half, tile),
-        jax.ShapeDtypeStruct((rows, columns), jnp.float32),
-        [vmem] * 2,
-        limit,
-        flops=2 * rows * part * columns,
-        moved=4 * rows * columns,
-    )(mine, halves[0])
-
-    def second(row, count, kept, column, width, sends):
-        size = (count - kept) // sends
+    tile = min(256, columns)
+    limit = 8 if mine.shape[0] < 1024 else 24
+    wide = columns + LANES
+
+    def projected(mine, other, row, kept, sends):
+        rows = other.shape[0]
+        cost = dict(flops=2 * rows * part * columns, moved=4 * rows * columns)
+        acc = local(
+            functools.partial(first_half, row, rows, tile),
+            jax.ShapeDtypeStruct((rows, columns), jnp.float32),
+            [vmem] * 2,
+            limit,
+            **cost,
+        )(mine, halves[0])
         return local(
-            functools.partial(second_half, row, count, column, tile),
-            [jax.ShapeDtypeStruct((kept, width), jnp.float32)]
-            + [jax.ShapeDtypeStruct((size, width + LANES), jnp.int16)] * sends,
+            functools.partial(second_half, 0, rows, 0, tile),
+            [jax.ShapeDtypeStruct((kept, columns), jnp.float32)]
+            + [jax.ShapeDtypeStruct(((rows - kept) // sends, wide), jnp.int16)] * sends,
             [vmem] * 3,
             limit,
-            flops=2 * count * part * width,
-            moved=8 * count * width,
+            **cost,
         )(other, halves[1], acc)
 
-    begin = seqs * near * tok
     away = (tensors - near) * tok
-    far = []
-    for chunk in range(chunks):
-        keep, *sends = second(begin, rows - begin, away, chunk * width, width, seqs - 1)
-        got = [cross(send, seqs, tensors, j, 0) for j, send in enumerate(sends, 1)]
-        parts = local(
-            functools.partial(middle, seqs),
-            [jax.ShapeDtypeStruct((tok, width + LANES), jnp.int16)] * (tensors - near),
-            [vmem] * seqs,
-            limit,
-            moved=8 * away * width,
-        )(keep, *got)
-        far += [cross(array, seqs, tensors, 0, k) for k, array in enumerate(parts, near)]
-    keep, *sends = second(0, begin, tok, 0, columns, seqs * near - 1)
+    keep, *sends = projected(mine, swap(mine[begin:], "kv", cores, 1), begin, away, seqs - 1)
+    got = [cross(send, seqs, tensors, j, 0) for j, send in enumerate(sends, 1)]
+    parts = local(
+        functools.partial(middle, seqs),
+        [jax.ShapeDtypeStruct((tok, wide), jnp.int16)] * (tensors - near),
+        [vmem] * seqs,
+        limit,
+        moved=8 * away * columns,
+    )(keep, *got)
+    far = [cross(array, seqs, tensors, 0, k) for k, array in enumerate(parts, near)]
+    other = swap(mine[:begin], "kv", cores, 1)
+    mine, sends = lax.optimization_barrier((mine, sends))
+    keep, *sends = projected(mine, other, 0, tok, seqs * near - 1)
     direct = [keep] + [cross(send, seqs, tensors, *order[i]) for i, send in enumerate(sends, 1)]
 
     tables = cosine, sine, sign_bits[None]

time: 50 us -> 49.2 us (0.984)
  starting transfers between devices: 24.1 us -> 20.2 us
  waiting for transfers between devices: 7.02 us -> 9.01 us
  Pallas kernels: 16.8 us -> 17.8 us
    ppermute x15 -> x12, starting transfers between devices: 24 us -> 19.6 us  [cross(): return lax.ppermute(array, ('tensor', 'seq'), pairs)]
    ppermute x15 -> x12, waiting for transfers between devices: 6.6 us -> 9 us  [cross(): return lax.ppermute(array, ('tensor', 'seq'), pairs)]
    pallas_call x6 -> x5, Pallas kernels: 6.53 us -> 7.55 us  [the longest x2 3.34 us: projected(): local(functools.partial(second_half, 0, rows, 0, tile), [jax.ShapeDtypeSt...]
  transfers between devices with their start and end apart: 16 -> 14, of which waited for: 5 -> 4; matrix products, arithmetic and copies ran while one was open for 2% -> 2% of each run, Pallas kernels for 26% -> 31%
where the time goes in v5:
time: 49.2 us; the launch traced here: 49 us
  starting transfers between devices  20.2 us (41%)
  Pallas kernels  17.8 us (36%)
  waiting for transfers between devices  9.01 us (18%)
  other arithmetic  1.08 us (2%)
  between operations  0.84 us (2%)
    ppermute x12, starting transfers between devices, cross(): return lax.ppermute(array, ('tensor', 'seq'), pairs)  19.6 us
    ppermute x12, waiting for transfers between devices, cross(): return lax.ppermute(array, ('tensor', 'seq'), pairs)  9 us
    pallas_call x2, Pallas kernels, loaded(): local(functools.partial(load, offset, 0, 8), pltpu.VMEM((part, columns),...  6.97 us
    pallas_call x2, Pallas kernels, projected(): local(functools.partial(second_half, 0, rows, 0, tile), [jax.ShapeDtypeSt...  3.34 us
    pallas_call x2, Pallas kernels, projected(): local(functools.partial(first_half, row, rows, tile), jax.ShapeDtypeStruc...  2.95 us
    pallas_call x1, Pallas kernels, per_device(): local(functools.partial(final, near, chunks, tok), [jax.ShapeDtypeStruct(...  1.64 us
    pallas_call x1, Pallas kernels, per_device(): local(functools.partial(middle, seqs), [jax.ShapeDtypeStruct((tok, wide),...  1.26 us
  transfers between devices with their start and end apart: 14, of which 4 were waited for; matrix products, arithmetic and copies ran while one was open for 2% of the time, Pallas kernels for 31%

profile of v5, /device:TPU:0, one launch (start us, length us, event | category | flops | bytes accessed | tf_op | source)
XLA Modules:
  0.0 49.0 jit_solution(10832808989225782830)
XLA Ops:
  0.6 1.0 %shard_map.59 = (bf16[24,2048]{1,0:T(8,128)(2,1)S(1)}, bf16[24,2048]{1,0:T(8,128)(2,1)S(1)}) custom-call(bf16[24,8192]{1,0:T(8,128)(2,1)} %rows_ref.1), custom_call_target="tpu_custom_call" | custom-call | tf_op jit(solution)/shard_map/pallas_call | solution.py:261
  1.6 6.0 %collective-permute-start.5 = (bf16[24,2048]{1,0:T(8,128)(2,1)S(1)}, bf16[24,2048]{1,0:T(8,128)(2,1)S(1)}, u32[]{:S(2)}, u32[]{:S(2)}) collective-permute-start(bf16[24,2048]{1,0:T(8,128)(2,1)S(1)} %get-tuple-element.23), channel_id=1, source_target_pairs={{0,14},{2,12},{4,10},{6,8},{8,6},{10,4},{12,2},{14,0},{1,15},{3,13... | collective-permute-start | bytes 294920 | tf_op jit(solution)/shard_map/ppermute | solution.py:211
  7.6 0.0 collective-permute-start.4
  7.7 0.9 %collective-permute-start = (bf16[24,2048]{1,0:T(8,128)(2,1)S(1)}, bf16[24,2048]{1,0:T(8,128)(2,1)S(1)}, u32[]{:S(2)}, u32[]{:S(2)}) collective-permute-start(bf16[24,2048]{1,0:T(8,128)(2,1)S(1)} %get-tuple-element.23), channel_id=1, source_target_pairs={{0,2},{2,0},{4,6},{6,4},{8,10},{10,8},{12,14},{14,12},{1,3},{3,1},... | collective-permute-start | bytes 294920 | tf_op jit(solution)/shard_map/ppermute | solution.py:211
  8.5 2.5 %collective-permute-start.3 = (bf16[24,2048]{1,0:T(8,128)(2,1)S(1)}, bf16[24,2048]{1,0:T(8,128)(2,1)S(1)}, u32[]{:S(2)}, u32[]{:S(2)}) collective-permute-start(bf16[24,2048]{1,0:T(8,128)(2,1)S(1)} %get-tuple-element.22), channel_id=1, source_target_pairs={{0,12},{2,14},{4,8},{6,10},{8,4},{10,6},{12,0},{14,2},{1,13},{3,15... | collective-permute-start | bytes 294920 | tf_op jit(solution)/shard_map/ppermute | solution.py:211
  11.0 1.0 %collective-permute-start.2 = (bf16[24,2048]{1,0:T(8,128)(2,1)S(1)}, bf16[24,2048]{1,0:T(8,128)(2,1)S(1)}, u32[]{:S(2)}, u32[]{:S(2)}) collective-permute-start(bf16[24,2048]{1,0:T(8,128)(2,1)S(1)} %get-tuple-element.22), channel_id=1, source_target_pairs={{0,8},{2,10},{4,12},{6,14},{8,0},{10,2},{12,4},{14,6},{1,9},{3,11}... | collective-permute-start | bytes 294920 | tf_op jit(solution)/shard_map/ppermute | solution.py:211
  12.1 0.7 %select_reduce_fusion.1 = s32[4]{0:T(128)S(1)} fusion(s32[4]{0:T(128)} %param.6), kind=kLoop, calls=%fused_computation.17 | loop fusion | flops 44 | bytes 32 | tf_op jit(solution)/shard_map/reduce_sum | solution.py:250
  12.8 0.1 select_reduce_fusion
  12.9 0.1 fusion.2
  13.0 0.1 pad_maximum_fusion.1
  13.1 0.0 collective-permute-done
  13.1 1.9 %collective-permute-start.1 = (bf16[48,2048]{1,0:T(8,128)(2,1)S(1)}, bf16[48,2048]{1,0:T(8,128)(2,1)S(1)}, u32[]{:S(2)}, u32[]{:S(2)}) collective-permute-start(bf16[48,2048]{1,0:T(8,128)(2,1)S(1)} %pad_maximum_fusion), channel_id=1, source_target_pairs={{0,4},{2,6},{4,0},{6,2},{8,12},{10,14},{12,8},{14,10},{1,5},{3,7},... | collective-permute-start | bytes 589832 | tf_op jit(solution)/shard_map/ppermute | solution.py:211
  15.1 3.5 %shard_map.61.w_ref = bf16[2048,2048]{1,0:T(8,128)(2,1)S(1)} custom-call(bf16[4096,2048]{1,0:T(8,128)(2,1)} %bitcast.5), custom_call_target="tpu_custom_call" | custom-call | bytes 16777216 | tf_op jit(solution)/shard_map/pallas_call | solution.py:240
  18.5 3.5 %shard_map.60.w_ref = bf16[2048,2048]{1,0:T(8,128)(2,1)S(1)} custom-call(bf16[4096,2048]{1,0:T(8,128)(2,1)} %bitcast.6), custom_call_target="tpu_custom_call" | custom-call | bytes 16777216 | tf_op jit(solution)/shard_map/pallas_call | solution.py:240
  22.0 0.1 collective-permute-done.1
  22.2 2.2 %collective-permute-done.2 = bf16[24,2048]{1,0:T(8,128)(2,1)S(1)} collective-permute-done((bf16[24,2048]{1,0:T(8,128)(2,1)S(1)}, bf16[24,2048]{1,0:T(8,128)(2,1)S(1)}, u32[]{:S(2)}, u32[]{:S(2)}) %collective-permute-start.2) | collective-permute-done | bytes 98336 | tf_op jit(solution)/shard_map/ppermute | solution.py:211
  24.4 0.0 collective-permute-done.3
  24.4 0.0 collective-permute-done.4
  24.4 0.0 collective-permute-done.5
  24.4 0.1 fusion.3
  24.5 0.1 collective-permute-start.7
  24.6 0.5 %collective-permute-start.6 = (bf16[96,2048]{1,0:T(8,128)(2,1)S(1)}, bf16[96,2048]{1,0:T(8,128)(2,1)S(1)}, u32[]{:S(2)}, u32[]{:S(2)}) collective-permute-start(bf16[96,2048]{1,0:T(8,128)(2,1)S(1)} %get-tuple-element.43), channel_id=1, source_target_pairs={{0,1},{1,0},{2,3},{3,2},{4,5},{5,4},{6,7},{7,6},{8,9},{9,8},{10,11... | collective-permute-start | bytes 1179656 | tf_op jit(solution)/shard_map/ppermute | solution.py:206
  25.1 1.5 %shard_map.62.acc_ref = f32[96,2048]{1,0:T(8,128)S(1)} custom-call(bf16[192,2048]{1,0:T(8,128)(2,1)S(1)} %constant_dynamic-update-slice_fusion.rows_ref, bf16[2048,2048]{1,0:T(8,128)(2,1)S(1)} %shard_map.60.w_ref), custom_call_target="tpu_custom_call" | custom-call | flops 805306368 | bytes 786432 | tf_op jit(solution)/shard_map/pallas_call | solution.py:291
  26.6 0.0 collective-permute-done.7.rows_ref
  26.6 1.6 %shard_map.63 = (f32[48,2048]{1,0:T(8,128)S(1)}, s16[48,2176]{1,0:T(8,128)(2,1)S(1)}) custom-call(bf16[96,2048]{1,0:T(8,128)(2,1)S(1)} %collective-permute-done.7.rows_ref, bf16[2048,2048]{1,0:T(8,128)(2,1)S(1)} %shard_map.61.w_ref, f32[96,2048]{1,0:T(8,128)S(1)} %shard_map.62.acc_ref), custom_call_target="tpu_custom_call" | custom-call | flops 805306368 | bytes 786432 | tf_op jit(solution)/shard_map/pallas_call | solution.py:298
  28.2 0.0 copy-start
  28.2 0.8 %collective-permute-start.11 = (s16[48,2176]{1,0:T(8,128)(2,1)S(1)}, s16[48,2176]{1,0:T(8,128)(2,1)S(1)}, u32[]{:S(2)}, u32[]{:S(2)}) collective-permute-start(s16[48,2176]{1,0:T(8,128)(2,1)S(1)} %get-tuple-element.29), channel_id=1, source_target_pairs={{0,2},{2,0},{4,6},{6,4},{8,10},{10,8},{12,14},{14,12},{1,3},{3,1},... | collective-permute-start | bytes 626696 | tf_op jit(solution)/shard_map/ppermute | solution.py:211
  29.0 1.5 %shard_map.64.acc_ref = f32[96,2048]{1,0:T(8,128)S(1)} custom-call(bf16[192,2048]{1,0:T(8,128)(2,1)S(1)} %constant_dynamic-update-slice_fusion.rows_ref, bf16[2048,2048]{1,0:T(8,128)(2,1)S(1)} %shard_map.60.w_ref), custom_call_target="tpu_custom_call" | custom-call | flops 805306368 | bytes 786432 | tf_op jit(solution)/shard_map/pallas_call | solution.py:291
  30.5 0.0 collective-permute-done.6.rows_ref
  30.5 1.7 %shard_map.65 = (f32[24,2048]{1,0:T(8,128)S(1)}, s16[24,2176]{1,0:T(8,128)(2,1)S(1)}, s16[24,2176]{1,0:T(8,128)(2,1)S(1)}, s16[24,2176]{1,0:T(8,128)(2,1)S(1)}) custom-call(bf16[96,2048]{1,0:T(8,128)(2,1)S(1)} %collective-permute-done.6.rows_ref, bf16[2048,2048]{1,0:T(8,128)(2,1)S(1)} %shard_map.61.w_ref, f32[96,2048]{1,0:T(8,128)S(1)} %shard_map.64.acc_ref), custom_call_target="tpu_custom_call" | custom-call | flops 805306368 | bytes 786432 | tf_op jit(solution)/shard_map/pallas_call | solution.py:298
  32.2 0.1 collective-permute-start.8
  32.3 1.4 %collective-permute-start.9 = (s16[24,2176]{1,0:T(8,128)(2,1)S(1)}, s16[24,2176]{1,0:T(8,128)(2,1)S(1)}, u32[]{:S(2)}, u32[]{:S(2)}) collective-permute-start(s16[24,2176]{1,0:T(8,128)(2,1)S(1)} %get-tuple-element.33), channel_id=1, source_target_pairs={{0,2},{2,0},{4,6},{6,4},{8,10},{10,8},{12,14},{14,12},{1,3},{3,1},... | collective-permute-start | bytes 313352 | tf_op jit(solution)/shard_map/ppermute | solution.py:211
  33.7 2.1 %collective-permute-start.10 = (s16[24,2176]{1,0:T(8,128)(2,1)S(1)}, s16[24,2176]{1,0:T(8,128)(2,1)S(1)}, u32[]{:S(2)}, u32[]{:S(2)}) collective-permute-start(s16[24,2176]{1,0:T(8,128)(2,1)S(1)} %get-tuple-element.34), channel_id=1, source_target_pairs={{0,6},{2,4},{4,2},{6,0},{8,14},{10,12},{12,10},{14,8},{1,7},{3,5},... | collective-permute-start | bytes 313352 | tf_op jit(solution)/shard_map/ppermute | solution.py:211
  35.7 0.4 collective-permute-done.11.refs_0_
  36.1 1.3 %shard_map.67 = (s16[24,2176]{1,0:T(8,128)(2,1)S(1)}, s16[24,2176]{1,0:T(8,128)(2,1)S(1)}) custom-call(f32[48,2048]{1,0:T(8,128)S(1)} %get-tuple-element.37.keep_ref, s16[48,2176]{1,0:T(8,128)(2,1)S(1)} %collective-permute-done.11.refs_0_), custom_call_target="tpu_custom_call" | custom-call | bytes 786432 | tf_op jit(solution)/shard_map/pallas_call | solution.py:310
  37.4 1.5 %collective-permute-start.12 = (s16[24,2176]{1,0:T(8,128)(2,1)S(1)}, s16[24,2176]{1,0:T(8,128)(2,1)S(1)}, u32[]{:S(2)}, u32[]{:S(2)}) collective-permute-start(s16[24,2176]{1,0:T(8,128)(2,1)S(1)} %get-tuple-element.38), channel_id=1, source_target_pairs={{0,8},{2,10},{4,12},{6,14},{8,0},{10,2},{12,4},{14,6},{1,9},{3,11}... | collective-permute-start | bytes 313352 | tf_op jit(solution)/shard_map/ppermute | solution.py:211
  38.9 1.5 %collective-permute-start.13 = (s16[24,2176]{1,0:T(8,128)(2,1)S(1)}, s16[24,2176]{1,0:T(8,128)(2,1)S(1)}, u32[]{:S(2)}, u32[]{:S(2)}) collective-permute-start(s16[24,2176]{1,0:T(8,128)(2,1)S(1)} %get-tuple-element.39), channel_id=1, source_target_pairs={{0,12},{2,14},{4,8},{6,10},{8,4},{10,6},{12,0},{14,2},{1,13},{3,15... | collective-permute-start | bytes 313352 | tf_op jit(solution)/shard_map/ppermute | solution.py:211
  40.4 0.0 collective-permute-done.8.refs_1_
  40.4 0.0 collective-permute-done.9.refs_2_
  40.4 0.0 collective-permute-done.10.refs_3_
  40.4 0.0 copy-done
  40.4 0.6 %shard_map.66.near_ref = f32[768,128]{1,0:T(8,128)S(1)} custom-call(f32[24,2048]{1,0:T(8,128)S(1)} %get-tuple-element.31.refs_0_, s16[24,2176]{1,0:T(8,128)(2,1)S(1)} %collective-permute-done.8.refs_1_, s16[24,2176]{1,0:T(8,128)(2,1)S(1)} %collective-permute-done.9.refs_2_, s16[24,2176]{1,0:T(8,128)(2,1)S(1)} %collective-permute-done.10.refs_3_, ...), custom_call_target="tpu_custom_call" | custom-call | flops 75497472 | bytes 786432 | tf_op jit(solution)/shard_map/pallas_call | solution.py:326
  41.0 6.4 %collective-permute-done.12.refs_0_ = s16[24,2176]{1,0:T(8,128)(2,1)S(1)} collective-permute-done((s16[24,2176]{1,0:T(8,128)(2,1)S(1)}, s16[24,2176]{1,0:T(8,128)(2,1)S(1)}, u32[]{:S(2)}, u32[]{:S(2)}) %collective-permute-start.12) | collective-permute-done | bytes 104480 | tf_op jit(solution)/shard_map/ppermute | solution.py:211
  47.4 0.0 collective-permute-done.13.refs_1_
  47.4 1.6 %shard_map.68 = (bf16[24,8192]{1,0:T(8,128)(2,1)}, f32[1,24]{1,0:T(1,128)}) custom-call(f32[768,128]{1,0:T(8,128)S(1)} %shard_map.66.near_ref, s16[24,2176]{1,0:T(8,128)(2,1)S(1)} %collective-permute-done.12.refs_0_, s16[24,2176]{1,0:T(8,128)(2,1)S(1)} %collective-permute-done.13.refs_1_, f32[24,128]{1,0:T(8,128)S(1)} %get-tuple-element.35.refs_4_.refs_2_, ...), custom_call_target="tpu_custom_call" | custom-call | bytes 1572864 | tf_op jit(solution)/shard_map/pallas_call | solution.py:334
  (12 shorter events, 0.1 us)
Async XLA Ops:
  1.6 22.8 %collective-permute-start.5 = (bf16[24,2048]{1,0:T(8,128)(2,1)S(1)}, bf16[24,2048]{1,0:T(8,128)(2,1)S(1)}, u32[]{:S(2)}, u32[]{:S(2)}) collective-permute-start(bf16[24,2048]{1,0:T(8,128)(2,1)S(1)} %get-tuple-element.23), channel_id=1, source_target_pairs={{0,14},{2,12},{4,10},{6,8},{8,6},{10,4},{12,2},{14,0},{1,15},{3,13... | collective-permute-start | bytes 294920 | tf_op jit(solution)/shard_map/ppermute | solution.py:211
  7.6 16.7 %collective-permute-start.4 = (bf16[24,2048]{1,0:T(8,128)(2,1)S(1)}, bf16[24,2048]{1,0:T(8,128)(2,1)S(1)}, u32[]{:S(2)}, u32[]{:S(2)}) collective-permute-start(bf16[24,2048]{1,0:T(8,128)(2,1)S(1)} %get-tuple-element.23), channel_id=1, source_target_pairs={{0,10},{2,8},{4,14},{6,12},{8,2},{10,0},{12,6},{14,4},{1,11},{3,9}... | collective-permute-start | bytes 294920 | tf_op jit(solution)/shard_map/ppermute | solution.py:211
  7.7 5.5 %collective-permute-start = (bf16[24,2048]{1,0:T(8,128)(2,1)S(1)}, bf16[24,2048]{1,0:T(8,128)(2,1)S(1)}, u32[]{:S(2)}, u32[]{:S(2)}) collective-permute-start(bf16[24,2048]{1,0:T(8,128)(2,1)S(1)} %get-tuple-element.23), channel_id=1, source_target_pairs={{0,2},{2,0},{4,6},{6,4},{8,10},{10,8},{12,14},{14,12},{1,3},{3,1},... | collective-permute-start | bytes 294920 | tf_op jit(solution)/shard_map/ppermute | solution.py:211
  8.5 15.8 %collective-permute-start.3 = (bf16[24,2048]{1,0:T(8,128)(2,1)S(1)}, bf16[24,2048]{1,0:T(8,128)(2,1)S(1)}, u32[]{:S(2)}, u32[]{:S(2)}) collective-permute-start(bf16[24,2048]{1,0:T(8,128)(2,1)S(1)} %get-tuple-element.22), channel_id=1, source_target_pairs={{0,12},{2,14},{4,8},{6,10},{8,4},{10,6},{12,0},{14,2},{1,13},{3,15... | collective-permute-start | bytes 294920 | tf_op jit(solution)/shard_map/ppermute | solution.py:211
  11.0 13.3 %collective-permute-start.2 = (bf16[24,2048]{1,0:T(8,128)(2,1)S(1)}, bf16[24,2048]{1,0:T(8,128)(2,1)S(1)}, u32[]{:S(2)}, u32[]{:S(2)}) collective-permute-start(bf16[24,2048]{1,0:T(8,128)(2,1)S(1)} %get-tuple-element.22), channel_id=1, source_target_pairs={{0,8},{2,10},{4,12},{6,14},{8,0},{10,2},{12,4},{14,6},{1,9},{3,11}... | collective-permute-start | bytes 294920 | tf_op jit(solution)/shard_map/ppermute | solution.py:211
  13.1 9.0 %collective-permute-start.1 = (bf16[48,2048]{1,0:T(8,128)(2,1)S(1)}, bf16[48,2048]{1,0:T(8,128)(2,1)S(1)}, u32[]{:S(2)}, u32[]{:S(2)}) collective-permute-start(bf16[48,2048]{1,0:T(8,128)(2,1)S(1)} %pad_maximum_fusion), channel_id=1, source_target_pairs={{0,4},{2,6},{4,0},{6,2},{8,12},{10,14},{12,8},{14,10},{1,5},{3,7},... | collective-permute-start | bytes 589832 | tf_op jit(solution)/shard_map/ppermute | solution.py:211
  24.5 2.1 %collective-permute-start.7 = (bf16[96,2048]{1,0:T(8,128)(2,1)S(1)}, bf16[96,2048]{1,0:T(8,128)(2,1)S(1)}, u32[]{:S(2)}, u32[]{:S(2)}) collective-permute-start(bf16[96,2048]{1,0:T(8,128)(2,1)S(1)} %get-tuple-element.42), channel_id=1, source_target_pairs={{0,1},{1,0},{2,3},{3,2},{4,5},{5,4},{6,7},{7,6},{8,9},{9,8},{10,11... | collective-permute-start | bytes 1179656 | tf_op jit(solution)/shard_map/ppermute | solution.py:206
  24.6 5.9 %collective-permute-start.6 = (bf16[96,2048]{1,0:T(8,128)(2,1)S(1)}, bf16[96,2048]{1,0:T(8,128)(2,1)S(1)}, u32[]{:S(2)}, u32[]{:S(2)}) collective-permute-start(bf16[96,2048]{1,0:T(8,128)(2,1)S(1)} %get-tuple-element.43), channel_id=1, source_target_pairs={{0,1},{1,0},{2,3},{3,2},{4,5},{5,4},{6,7},{7,6},{8,9},{9,8},{10,11... | collective-permute-start | bytes 1179656 | tf_op jit(solution)/shard_map/ppermute | solution.py:206
  28.2 12.2 %copy-start = (s32[8192]{0:T(1024)S(1)}, s32[8192]{0:T(1024)}, u32[]{:S(2)}) copy-start(s32[8192]{0:T(1024)} %param.7) | copy-start | bytes 98308
  28.2 7.9 %collective-permute-start.11 = (s16[48,2176]{1,0:T(8,128)(2,1)S(1)}, s16[48,2176]{1,0:T(8,128)(2,1)S(1)}, u32[]{:S(2)}, u32[]{:S(2)}) collective-permute-start(s16[48,2176]{1,0:T(8,128)(2,1)S(1)} %get-tuple-element.29), channel_id=1, source_target_pairs={{0,2},{2,0},{4,6},{6,4},{8,10},{10,8},{12,14},{14,12},{1,3},{3,1},... | collective-permute-start | bytes 626696 | tf_op jit(solution)/shard_map/ppermute | solution.py:211
  32.2 8.2 %collective-permute-start.8 = (s16[24,2176]{1,0:T(8,128)(2,1)S(1)}, s16[24,2176]{1,0:T(8,128)(2,1)S(1)}, u32[]{:S(2)}, u32[]{:S(2)}) collective-permute-start(s16[24,2176]{1,0:T(8,128)(2,1)S(1)} %get-tuple-element.32), channel_id=1, source_target_pairs={{0,4},{2,6},{4,0},{6,2},{8,12},{10,14},{12,8},{14,10},{1,5},{3,7},... | collective-permute-start | bytes 313352 | tf_op jit(solution)/shard_map/ppermute | solution.py:211
  32.3 8.1 %collective-permute-start.9 = (s16[24,2176]{1,0:T(8,128)(2,1)S(1)}, s16[24,2176]{1,0:T(8,128)(2,1)S(1)}, u32[]{:S(2)}, u32[]{:S(2)}) collective-permute-start(s16[24,2176]{1,0:T(8,128)(2,1)S(1)} %get-tuple-element.33), channel_id=1, source_target_pairs={{0,2},{2,0},{4,6},{6,4},{8,10},{10,8},{12,14},{14,12},{1,3},{3,1},... | collective-permute-start | bytes 313352 | tf_op jit(solution)/shard_map/ppermute | solution.py:211
  33.7 6.7 %collective-permute-start.10 = (s16[24,2176]{1,0:T(8,128)(2,1)S(1)}, s16[24,2176]{1,0:T(8,128)(2,1)S(1)}, u32[]{:S(2)}, u32[]{:S(2)}) collective-permute-start(s16[24,2176]{1,0:T(8,128)(2,1)S(1)} %get-tuple-element.34), channel_id=1, source_target_pairs={{0,6},{2,4},{4,2},{6,0},{8,14},{10,12},{12,10},{14,8},{1,7},{3,5},... | collective-permute-start | bytes 313352 | tf_op jit(solution)/shard_map/ppermute | solution.py:211
  37.4 10.0 %collective-permute-start.12 = (s16[24,2176]{1,0:T(8,128)(2,1)S(1)}, s16[24,2176]{1,0:T(8,128)(2,1)S(1)}, u32[]{:S(2)}, u32[]{:S(2)}) collective-permute-start(s16[24,2176]{1,0:T(8,128)(2,1)S(1)} %get-tuple-element.38), channel_id=1, source_target_pairs={{0,8},{2,10},{4,12},{6,14},{8,0},{10,2},{12,4},{14,6},{1,9},{3,11}... | collective-permute-start | bytes 313352 | tf_op jit(solution)/shard_map/ppermute | solution.py:211
  38.9 8.5 %collective-permute-start.13 = (s16[24,2176]{1,0:T(8,128)(2,1)S(1)}, s16[24,2176]{1,0:T(8,128)(2,1)S(1)}, u32[]{:S(2)}, u32[]{:S(2)}) collective-permute-start(s16[24,2176]{1,0:T(8,128)(2,1)S(1)} %get-tuple-element.39), channel_id=1, source_target_pairs={{0,12},{2,14},{4,8},{6,10},{8,4},{10,6},{12,0},{14,2},{1,13},{3,15... | collective-permute-start | bytes 313352 | tf_op jit(solution)/shard_map/ppermute | solution.py:211

commit v6 on v5

--- a/solution.py
+++ b/solution.py
@@ -33,21 +33,21 @@
     return lax.broadcasted_iota(jnp.int32, (rows, LANES), 1)
 
 
-def load(offset, piece, copies, w_ref, out_ref, sems):
-    rows = out_ref.shape[0]
-    cores = lax.axis_size("kv")
-    index = lax.rem(lax.axis_index("kv") + offset, cores)
-    base = index * (w_ref.shape[0] // cores) + piece * rows
-    step = rows // copies
-    started = []
-    for i in range(copies):
-        start = pl.multiple_of(base + i * step, step)
-        started.append(
-            pltpu.make_async_copy(w_ref.at[pl.ds(start, step)], out_ref.at[pl.ds(i * step, step)], sems.at[i])
-        )
-    for copy in started:
+def load(w_ref, *refs):
+    *out_refs, sems = refs
+    rows = out_refs[0].shape[0]
+    pieces = sems.shape[1]
+    step = rows // pieces
+    copies = []
+    for offset, out_ref in enumerate(out_refs):
+        index = lax.rem(lax.axis_index("kv") + offset, len(out_refs))
+        for i in range(pieces):
+            start = pl.multiple_of(index * rows + i * step, step)
+            source, target = w_ref.at[pl.ds(start, step)], out_ref.at[pl.ds(i * step, step)]
+            copies.append(pltpu.make_async_copy(source, target, sems.at[offset, i]))
+    for copy in copies:
         copy.start()
-    for copy in started:
+    for copy in copies:
         copy.wait()
 
 
@@ -65,22 +65,26 @@
         copy.wait()
 
 
-def first_half(row, rows, tile, rows_ref, w_ref, acc_ref):
+def first_half(tile, rows_ref, w_ref, acc_ref):
     for first in range(0, acc_ref.shape[1], tile):
         at = slice(first, first + tile)
-        acc_ref[:, at] = jnp.dot(rows_ref[row : row + rows, :], w_ref[:, at], preferred_element_type=jnp.float32)
-
-
-def second_half(row, rows, column, tile, rows_ref, w_ref, acc_ref, keep_ref, *send_refs):
-    kept, width = keep_ref.shape
+        acc_ref[:, at] = jnp.dot(rows_ref[...], w_ref[:, at], preferred_element_type=jnp.float32)
+
+
+def second_half(keeps, tile, rows_ref, w_ref, acc_ref, *refs):
+    keep_refs, send_refs = refs[:keeps], refs[keeps:]
+    rows, columns = acc_ref.shape
+    kept = sum(ref.shape[0] for ref in keep_refs)
     size = send_refs[0].shape[0]
     codes = jnp.zeros((rows - kept, LANES), jnp.float32)
     lane = lane_of(rows - kept)
-    for first in range(0, width, tile):
-        at = slice(column + first, column + first + tile)
-        total = acc_ref[row : row + rows, at]
-        total = total + jnp.dot(rows_ref[row : row + rows, :], w_ref[:, at], preferred_element_type=jnp.float32)
-        keep_ref[:, first : first + tile] = total[:kept]
+    for first in range(0, columns, tile):
+        at = slice(first, first + tile)
+        total = acc_ref[:, at] + jnp.dot(rows_ref[...], w_ref[:, at], preferred_element_type=jnp.float32)
+        begin = 0
+        for ref in keep_refs:
+            ref[:, at] = total[begin : begin + ref.shape[0]]
+            begin += ref.shape[0]
         for begin in range(0, tile, HEAD):
             coded, code = encode(total[kept:, begin : begin + HEAD])
             head = (first + begin) // HEAD
@@ -89,7 +93,7 @@
             codes = jnp.where(lane == head, code, codes)
     codes = codes.astype(jnp.int32).astype(jnp.int16)
     for i, ref in enumerate(send_refs):
-        ref[:, width:] = codes[i * size : (i + 1) * size]
+        ref[:, columns:] = codes[i * size : (i + 1) * size]
 
 
 def middle(seqs, keep_ref, *refs):
@@ -222,8 +226,6 @@
     hbm = pl.BlockSpec(memory_space=pltpu.HBM)
     chunks = 1
     near = min(2, tensors)
-    order = [(j, k) for j in range(seqs) for k in range(near)]
-    order += [(j, k) for j in range(seqs) for k in range(near, tensors)]
 
     def local(kernel, outs, in_specs, limit, scratch=(), flops=0, moved=0):
         return pl.pallas_call(
@@ -236,14 +238,14 @@
             cost_estimate=pl.CostEstimate(flops=flops, bytes_accessed=moved, transcendentals=0),
         )
 
-    def loaded(weight, offset):
+    def loaded(weight):
         return local(
-            functools.partial(load, offset, 0, 8),
-            pltpu.VMEM((part, columns), weight.dtype),
+            load,
+            [pltpu.VMEM((part, columns), weight.dtype)] * cores,
             [hbm],
             4,
-            [pltpu.SemaphoreType.DMA((8,))],
-            moved=4 * part * columns,
+            [pltpu.SemaphoreType.DMA((cores, 8))],
+            moved=4 * rows_dev * columns,
         )(weight)
 
     index = jnp.arange(block_lengths.shape[0], dtype=jnp.int32)
@@ -268,45 +270,53 @@
     blocks = {(0, 0): slices[0]}
     for j in range(1, seqs):
         blocks[j, 0] = cross(slices[j], seqs, tensors, j, 0)
+        for k in range(near, tensors):
+            blocks[j, k] = cross(slices[j], seqs, tensors, j, k)
+    own = slices[0]
     for k in range(near, tensors):
-        for j in range(seqs):
-            blocks[j, k] = cross(slices[j], seqs, tensors, j, k)
+        blocks[0, k] = cross(own, seqs, tensors, 0, k)
     pair = jnp.concatenate([blocks[j, 0] for j in range(seqs)], axis=0)
     for k in range(1, near):
         got = cross(pair, seqs, tensors, 0, k)
         for j in range(seqs):
             blocks[j, k] = got[j * tok : (j + 1) * tok]
+    remote = jnp.concatenate([blocks[j, k] for j in range(1, seqs) for k in range(near, tensors)], axis=0)
+    order = [(0, k) for k in range(near, tensors)] + [(j, k) for j in range(seqs) for k in range(near)]
     weight, cosine, sine, blocks[1, 0] = lax.optimization_barrier((weight, cosine, sine, blocks[1, 0]))
-    halves = [loaded(weight, offset) for offset in range(cores)]
-    begin = seqs * near * tok
-    mine = jnp.concatenate([blocks[at] for at in order], axis=0)
-    mine, *halves = lax.optimization_barrier((mine, *halves))
+    halves = loaded(weight)
+    remote, *halves = lax.optimization_barrier((remote, *halves))
     tile = min(256, columns)
-    limit = 8 if mine.shape[0] < 1024 else 24
+    limit = 8 if remote.shape[0] < 1024 else 24
     wide = columns + LANES
 
-    def projected(mine, other, row, kept, sends):
-        rows = other.shape[0]
+    def projected(mine, other, keeps, sends):
+        rows = mine.shape[0]
+        size = (rows - sum(keeps)) // sends
         cost = dict(flops=2 * rows * part * columns, moved=4 * rows * columns)
         acc = local(
-            functools.partial(first_half, row, rows, tile),
+            functools.partial(first_half, tile),
             jax.ShapeDtypeStruct((rows, columns), jnp.float32),
             [vmem] * 2,
             limit,
             **cost,
         )(mine, halves[0])
-        return local(
-            functools.partial(second_half, 0, rows, 0, tile),
-            [jax.ShapeDtypeStruct((kept, columns), jnp.float32)]
-            + [jax.ShapeDtypeStruct(((rows - kept) // sends, wide), jnp.int16)] * sends,
+        outs = local(
+            functools.partial(second_half, len(keeps), tile),
+            [jax.ShapeDtypeStruct((keep, columns), jnp.float32) for keep in keeps]
+            + [jax.ShapeDtypeStruct((size, wide), jnp.int16)] * sends,
             [vmem] * 3,
             limit,
             **cost,
         )(other, halves[1], acc)
+        return outs[: len(keeps)], outs[len(keeps) :]
 
     away = (tensors - near) * tok
-    keep, *sends = projected(mine, swap(mine[begin:], "kv", cores, 1), begin, away, seqs - 1)
+    _, sends = projected(remote, swap(remote, "kv", cores, 1), [], seqs - 1)
     got = [cross(send, seqs, tensors, j, 0) for j, send in enumerate(sends, 1)]
+    late, sends = lax.optimization_barrier(([blocks[at] for at in order], sends))
+    mine = jnp.concatenate(late, axis=0)
+    other = swap(mine, "kv", cores, 1)
+    (keep, first), sends = projected(mine, other, [away, tok], seqs * near - 1)
     parts = local(
         functools.partial(middle, seqs),
         [jax.ShapeDtypeStruct((tok, wide), jnp.int16)] * (tensors - near),
@@ -315,10 +325,8 @@
         moved=8 * away * columns,
     )(keep, *got)
     far = [cross(array, seqs, tensors, 0, k) for k, array in enumerate(parts, near)]
-    other = swap(mine[:begin], "kv", cores, 1)
-    mine, sends = lax.optimization_barrier((mine, sends))
-    keep, *sends = projected(mine, other, 0, tok, seqs * near - 1)
-    direct = [keep] + [cross(send, seqs, tensors, *order[i]) for i, send in enumerate(sends, 1)]
+    close = [(j, k) for j in range(seqs) for k in range(near)]
+    direct = [first] + [cross(send, seqs, tensors, *close[i]) for i, send in enumerate(sends, 1)]
 
     tables = cosine, sine, sign_bits[None]
     heads = columns // HEAD

time: 49.2 us -> 47.3 us (0.961)
  waiting for transfers between devices: 9.01 us -> 6.71 us
  starting transfers between devices: 20.2 us -> 21.6 us
  Pallas kernels: 17.8 us -> 16.8 us
    ppermute x12, waiting for transfers between devices: 9 us -> 6.71 us  [cross(): return lax.ppermute(array, ('tensor', 'seq'), pairs)]
    ppermute x12, starting transfers between devices: 19.6 us -> 21 us  [cross(): return lax.ppermute(array, ('tensor', 'seq'), pairs)]
    pallas_call x6 -> x5, Pallas kernels: 13.3 us -> 12.3 us  [the longest x1 5.93 us: loaded(): local(load, [pltpu.VMEM((part, columns), weight.dtype)] * cores, [hbm], 4...]
  transfers between devices with their start and end apart: 14 -> 14, of which waited for: 4 -> 2; matrix products, arithmetic and copies ran while one was open for 2% -> 2% of each run, Pallas kernels for 31% -> 30%
where the time goes in v6:
time: 47.3 us; the launch traced here: 47.1 us
  starting transfers between devices  21.6 us (46%)
  Pallas kernels  16.8 us (36%)
  waiting for transfers between devices  6.71 us (14%)
  other arithmetic  1.09 us (2%)
  between operations  0.85 us (2%)
    ppermute x12, starting transfers between devices, cross(): return lax.ppermute(array, ('tensor', 'seq'), pairs)  21 us
    ppermute x12, waiting for transfers between devices, cross(): return lax.ppermute(array, ('tensor', 'seq'), pairs)  6.71 us
    pallas_call x1, Pallas kernels, loaded(): local(load, [pltpu.VMEM((part, columns), weight.dtype)] * cores, [hbm], 4...  5.93 us
    pallas_call x2, Pallas kernels, projected(): local(functools.partial(second_half, len(keeps), tile), [jax.ShapeDtypeSt...  3.38 us
    pallas_call x2, Pallas kernels, projected(): local(functools.partial(first_half, tile), jax.ShapeDtypeStruct((rows, co...  2.98 us
    pallas_call x1, Pallas kernels, per_device(): local(functools.partial(final, near, chunks, tok), [jax.ShapeDtypeStruct(...  1.64 us
    pallas_call x1, Pallas kernels, per_device(): local(functools.partial(middle, seqs), [jax.ShapeDtypeStruct((tok, wide),...  1.26 us
    pallas_call x1, Pallas kernels, per_device(): local(take, [pltpu.VMEM((tok, part), hidden_rows.dtype)] * seqs, [hbm], 4...  0.97 us
  transfers between devices with their start and end apart: 14, of which 2 were waited for; matrix products, arithmetic and copies ran while one was open for 2% of the time, Pallas kernels for 30%

profile of v6, /device:TPU:0, one launch (start us, length us, event | category | flops | bytes accessed | tf_op | source)
XLA Modules:
  0.0 47.1 jit_solution(6165216679581340921)
XLA Ops:
  0.6 1.0 %shard_map.59 = (bf16[24,2048]{1,0:T(8,128)(2,1)S(1)}, bf16[24,2048]{1,0:T(8,128)(2,1)S(1)}) custom-call(bf16[24,8192]{1,0:T(8,128)(2,1)} %rows_ref.1), custom_call_target="tpu_custom_call" | custom-call | tf_op jit(solution)/shard_map/pallas_call | solution.py:263
  1.6 6.0 %collective-permute-start.5 = (bf16[24,2048]{1,0:T(8,128)(2,1)S(1)}, bf16[24,2048]{1,0:T(8,128)(2,1)S(1)}, u32[]{:S(2)}, u32[]{:S(2)}) collective-permute-start(bf16[24,2048]{1,0:T(8,128)(2,1)S(1)} %get-tuple-element.29), channel_id=1, source_target_pairs={{0,14},{2,12},{4,10},{6,8},{8,6},{10,4},{12,2},{14,0},{1,15},{3,13... | collective-permute-start | bytes 294920 | tf_op jit(solution)/shard_map/ppermute | solution.py:215
  7.6 0.0 collective-permute-start.4
  7.7 0.9 %collective-permute-start.2 = (bf16[24,2048]{1,0:T(8,128)(2,1)S(1)}, bf16[24,2048]{1,0:T(8,128)(2,1)S(1)}, u32[]{:S(2)}, u32[]{:S(2)}) collective-permute-start(bf16[24,2048]{1,0:T(8,128)(2,1)S(1)} %get-tuple-element.29), channel_id=1, source_target_pairs={{0,2},{2,0},{4,6},{6,4},{8,10},{10,8},{12,14},{14,12},{1,3},{3,1},... | collective-permute-start | bytes 294920 | tf_op jit(solution)/shard_map/ppermute | solution.py:215
  8.5 2.5 %collective-permute-start.1 = (bf16[24,2048]{1,0:T(8,128)(2,1)S(1)}, bf16[24,2048]{1,0:T(8,128)(2,1)S(1)}, u32[]{:S(2)}, u32[]{:S(2)}) collective-permute-start(bf16[24,2048]{1,0:T(8,128)(2,1)S(1)} %get-tuple-element.39), channel_id=1, source_target_pairs={{0,12},{2,14},{4,8},{6,10},{8,4},{10,6},{12,0},{14,2},{1,13},{3,15... | collective-permute-start | bytes 294920 | tf_op jit(solution)/shard_map/ppermute | solution.py:215
  11.0 1.0 %collective-permute-start = (bf16[24,2048]{1,0:T(8,128)(2,1)S(1)}, bf16[24,2048]{1,0:T(8,128)(2,1)S(1)}, u32[]{:S(2)}, u32[]{:S(2)}) collective-permute-start(bf16[24,2048]{1,0:T(8,128)(2,1)S(1)} %get-tuple-element.39), channel_id=1, source_target_pairs={{0,8},{2,10},{4,12},{6,14},{8,0},{10,2},{12,4},{14,6},{1,9},{3,11}... | collective-permute-start | bytes 294920 | tf_op jit(solution)/shard_map/ppermute | solution.py:215
  12.1 0.7 %select_reduce_fusion.1 = s32[4]{0:T(128)S(1)} fusion(s32[4]{0:T(128)} %param.6), kind=kLoop, calls=%fused_computation.16 | loop fusion | flops 44 | bytes 32 | tf_op jit(solution)/shard_map/reduce_sum | solution.py:252
  12.8 0.1 select_reduce_fusion
  12.9 0.1 fusion.2
  13.0 0.1 pad_maximum_fusion.2
  13.1 0.0 collective-permute-done.2
  13.1 1.9 %collective-permute-start.3 = (bf16[48,2048]{1,0:T(8,128)(2,1)S(1)}, bf16[48,2048]{1,0:T(8,128)(2,1)S(1)}, u32[]{:S(2)}, u32[]{:S(2)}) collective-permute-start(bf16[48,2048]{1,0:T(8,128)(2,1)S(1)} %pad_maximum_fusion), channel_id=1, source_target_pairs={{0,4},{2,6},{4,0},{6,2},{8,12},{10,14},{12,8},{14,10},{1,5},{3,7},... | collective-permute-start | bytes 589832 | tf_op jit(solution)/shard_map/ppermute | solution.py:215
  15.0 5.9 %shard_map.60 = (bf16[2048,2048]{1,0:T(8,128)(2,1)S(1)}, bf16[2048,2048]{1,0:T(8,128)(2,1)S(1)}) custom-call(bf16[4096,2048]{1,0:T(8,128)(2,1)} %bitcast.5), custom_call_target="tpu_custom_call" | custom-call | bytes 33554432 | tf_op jit(solution)/shard_map/pallas_call | solution.py:242
  21.0 0.0 collective-permute-done.5
  21.0 0.1 collective-permute-done.4
  21.1 0.1 collective-permute-start.6
  21.2 1.6 %shard_map.61.acc_ref = f32[48,2048]{1,0:T(8,128)S(1)} custom-call(bf16[48,2048]{1,0:T(8,128)(2,1)S(1)} %pad_maximum_fusion.1.rows_ref, bf16[2048,2048]{1,0:T(8,128)(2,1)S(1)} %get-tuple-element.36.w_ref), custom_call_target="tpu_custom_call" | custom-call | flops 402653184 | bytes 393216 | tf_op jit(solution)/shard_map/pallas_call | solution.py:296
  22.8 0.0 collective-permute-done.3
  22.8 0.0 collective-permute-done.6.rows_ref
  22.8 1.7 %shard_map.62 = s16[48,2176]{1,0:T(8,128)(2,1)S(1)} custom-call(bf16[48,2048]{1,0:T(8,128)(2,1)S(1)} %collective-permute-done.6.rows_ref, bf16[2048,2048]{1,0:T(8,128)(2,1)S(1)} %get-tuple-element.35.w_ref, f32[48,2048]{1,0:T(8,128)S(1)} %shard_map.61.acc_ref), custom_call_target="tpu_custom_call" | custom-call | flops 402653184 | bytes 393216 | tf_op jit(solution)/shard_map/pallas_call | solution.py:303
  24.6 0.0 collective-permute-done.1
  24.6 0.0 collective-permute-done
  24.7 0.0 copy-start
  24.7 0.6 %collective-permute-start.7 = (bf16[144,2048]{1,0:T(8,128)(2,1)S(1)}, bf16[144,2048]{1,0:T(8,128)(2,1)S(1)}, u32[]{:S(2)}, u32[]{:S(2)}) collective-permute-start(bf16[144,2048]{1,0:T(8,128)(2,1)S(1)} %constant_dynamic-update-slice_fusion.rows_ref), channel_id=1, source_target_pairs={{0,1},{1,0},{2,3},{3,2},{4,5},{5,4},{6,7},{7,6},{8,9},{9,8},{10,11... | collective-permute-start | bytes 1769480 | tf_op jit(solution)/shard_map/ppermute | solution.py:210
  25.3 1.7 %collective-permute-start.11 = (s16[48,2176]{1,0:T(8,128)(2,1)S(1)}, s16[48,2176]{1,0:T(8,128)(2,1)S(1)}, u32[]{:S(2)}, u32[]{:S(2)}) collective-permute-start(s16[48,2176]{1,0:T(8,128)(2,1)S(1)} %shard_map.62), channel_id=1, source_target_pairs={{0,2},{2,0},{4,6},{6,4},{8,10},{10,8},{12,14},{14,12},{1,3},{3,1},... | collective-permute-start | bytes 626696 | tf_op jit(solution)/shard_map/ppermute | solution.py:215
  27.0 1.4 %shard_map.63.acc_ref = f32[144,2048]{1,0:T(8,128)S(1)} custom-call(bf16[144,2048]{1,0:T(8,128)(2,1)S(1)} %constant_dynamic-update-slice_fusion.rows_ref, bf16[2048,2048]{1,0:T(8,128)(2,1)S(1)} %get-tuple-element.36.w_ref), custom_call_target="tpu_custom_call" | custom-call | flops 1207959552 | bytes 1179648 | tf_op jit(solution)/shard_map/pallas_call | solution.py:296
  28.5 0.0 collective-permute-done.7.rows_ref
  28.5 1.6 %shard_map.64 = (f32[48,2048]{1,0:T(8,128)S(1)}, f32[24,2048]{1,0:T(8,128)S(1)}, s16[24,2176]{1,0:T(8,128)(2,1)S(1)}, s16[24,2176]{1,0:T(8,128)(2,1)S(1)}, s16[24,2176]{1,0:T(8,128)(2,1)S(1)}) custom-call(bf16[144,2048]{1,0:T(8,128)(2,1)S(1)} %collective-permute-done.7.rows_ref, bf16[2048,2048]{1,0:T(8,128)(2,1)S(1)} %get-tuple-element.35.w_ref, ...), custom_call_target="tpu_custom_call" | custom-call | flops 1207959552 | bytes 1179648 | tf_op jit(solution)/shard_map/pallas_call | solution.py:303
  30.1 0.1 collective-permute-start.8
  30.2 0.5 %collective-permute-start.9 = (s16[24,2176]{1,0:T(8,128)(2,1)S(1)}, s16[24,2176]{1,0:T(8,128)(2,1)S(1)}, u32[]{:S(2)}, u32[]{:S(2)}) collective-permute-start(s16[24,2176]{1,0:T(8,128)(2,1)S(1)} %get-tuple-element.45), channel_id=1, source_target_pairs={{0,2},{2,0},{4,6},{6,4},{8,10},{10,8},{12,14},{14,12},{1,3},{3,1},... | collective-permute-start | bytes 313352 | tf_op jit(solution)/shard_map/ppermute | solution.py:215
  30.7 2.9 %collective-permute-start.10 = (s16[24,2176]{1,0:T(8,128)(2,1)S(1)}, s16[24,2176]{1,0:T(8,128)(2,1)S(1)}, u32[]{:S(2)}, u32[]{:S(2)}) collective-permute-start(s16[24,2176]{1,0:T(8,128)(2,1)S(1)} %get-tuple-element.46), channel_id=1, source_target_pairs={{0,6},{2,4},{4,2},{6,0},{8,14},{10,12},{12,10},{14,8},{1,7},{3,5},... | collective-permute-start | bytes 313352 | tf_op jit(solution)/shard_map/ppermute | solution.py:215
  33.7 0.0 collective-permute-done.11.refs_0_
  33.7 1.3 %shard_map.66 = (s16[24,2176]{1,0:T(8,128)(2,1)S(1)}, s16[24,2176]{1,0:T(8,128)(2,1)S(1)}) custom-call(f32[48,2048]{1,0:T(8,128)S(1)} %get-tuple-element.49.keep_ref, s16[48,2176]{1,0:T(8,128)(2,1)S(1)} %collective-permute-done.11.refs_0_), custom_call_target="tpu_custom_call" | custom-call | bytes 786432 | tf_op jit(solution)/shard_map/pallas_call | solution.py:320
  34.9 1.9 %collective-permute-start.12 = (s16[24,2176]{1,0:T(8,128)(2,1)S(1)}, s16[24,2176]{1,0:T(8,128)(2,1)S(1)}, u32[]{:S(2)}, u32[]{:S(2)}) collective-permute-start(s16[24,2176]{1,0:T(8,128)(2,1)S(1)} %get-tuple-element.50), channel_id=1, source_target_pairs={{0,8},{2,10},{4,12},{6,14},{8,0},{10,2},{12,4},{14,6},{1,9},{3,11}... | collective-permute-start | bytes 313352 | tf_op jit(solution)/shard_map/ppermute | solution.py:215
  36.8 1.5 %collective-permute-start.13 = (s16[24,2176]{1,0:T(8,128)(2,1)S(1)}, s16[24,2176]{1,0:T(8,128)(2,1)S(1)}, u32[]{:S(2)}, u32[]{:S(2)}) collective-permute-start(s16[24,2176]{1,0:T(8,128)(2,1)S(1)} %get-tuple-element.51), channel_id=1, source_target_pairs={{0,12},{2,14},{4,8},{6,10},{8,4},{10,6},{12,0},{14,2},{1,13},{3,15... | collective-permute-start | bytes 313352 | tf_op jit(solution)/shard_map/ppermute | solution.py:215
  38.3 0.0 collective-permute-done.8.refs_1_
  38.3 0.0 collective-permute-done.9.refs_2_
  38.3 0.0 collective-permute-done.10.refs_3_
  38.3 0.0 copy-done
  38.3 0.6 %shard_map.65.near_ref = f32[768,128]{1,0:T(8,128)S(1)} custom-call(f32[24,2048]{1,0:T(8,128)S(1)} %get-tuple-element.43.refs_0_, s16[24,2176]{1,0:T(8,128)(2,1)S(1)} %collective-permute-done.8.refs_1_, s16[24,2176]{1,0:T(8,128)(2,1)S(1)} %collective-permute-done.9.refs_2_, s16[24,2176]{1,0:T(8,128)(2,1)S(1)} %collective-permute-done.10.refs_3_, ...), custom_call_target="tpu_custom_call" | custom-call | flops 75497472 | bytes 786432 | tf_op jit(solution)/shard_map/pallas_call | solution.py:334
  39.0 6.5 %collective-permute-done.12.refs_0_ = s16[24,2176]{1,0:T(8,128)(2,1)S(1)} collective-permute-done((s16[24,2176]{1,0:T(8,128)(2,1)S(1)}, s16[24,2176]{1,0:T(8,128)(2,1)S(1)}, u32[]{:S(2)}, u32[]{:S(2)}) %collective-permute-start.12) | collective-permute-done | bytes 104480 | tf_op jit(solution)/shard_map/ppermute | solution.py:215
  45.5 0.0 collective-permute-done.13.refs_1_
  45.5 1.6 %shard_map.67 = (bf16[24,8192]{1,0:T(8,128)(2,1)}, f32[1,24]{1,0:T(1,128)}) custom-call(f32[768,128]{1,0:T(8,128)S(1)} %shard_map.65.near_ref, s16[24,2176]{1,0:T(8,128)(2,1)S(1)} %collective-permute-done.12.refs_0_, s16[24,2176]{1,0:T(8,128)(2,1)S(1)} %collective-permute-done.13.refs_1_, f32[24,128]{1,0:T(8,128)S(1)} %get-tuple-element.47.refs_4_.refs_2_, ...), custom_call_target="tpu_custom_call" | custom-call | bytes 1572864 | tf_op jit(solution)/shard_map/pallas_call | solution.py:342
  (12 shorter events, 0.1 us)
Async XLA Ops:
  1.6 19.4 %collective-permute-start.5 = (bf16[24,2048]{1,0:T(8,128)(2,1)S(1)}, bf16[24,2048]{1,0:T(8,128)(2,1)S(1)}, u32[]{:S(2)}, u32[]{:S(2)}) collective-permute-start(bf16[24,2048]{1,0:T(8,128)(2,1)S(1)} %get-tuple-element.29), channel_id=1, source_target_pairs={{0,14},{2,12},{4,10},{6,8},{8,6},{10,4},{12,2},{14,0},{1,15},{3,13... | collective-permute-start | bytes 294920 | tf_op jit(solution)/shard_map/ppermute | solution.py:215
  7.6 13.5 %collective-permute-start.4 = (bf16[24,2048]{1,0:T(8,128)(2,1)S(1)}, bf16[24,2048]{1,0:T(8,128)(2,1)S(1)}, u32[]{:S(2)}, u32[]{:S(2)}) collective-permute-start(bf16[24,2048]{1,0:T(8,128)(2,1)S(1)} %get-tuple-element.29), channel_id=1, source_target_pairs={{0,10},{2,8},{4,14},{6,12},{8,2},{10,0},{12,6},{14,4},{1,11},{3,9}... | collective-permute-start | bytes 294920 | tf_op jit(solution)/shard_map/ppermute | solution.py:215
  7.7 5.5 %collective-permute-start.2 = (bf16[24,2048]{1,0:T(8,128)(2,1)S(1)}, bf16[24,2048]{1,0:T(8,128)(2,1)S(1)}, u32[]{:S(2)}, u32[]{:S(2)}) collective-permute-start(bf16[24,2048]{1,0:T(8,128)(2,1)S(1)} %get-tuple-element.29), channel_id=1, source_target_pairs={{0,2},{2,0},{4,6},{6,4},{8,10},{10,8},{12,14},{14,12},{1,3},{3,1},... | collective-permute-start | bytes 294920 | tf_op jit(solution)/shard_map/ppermute | solution.py:215
  8.5 16.0 %collective-permute-start.1 = (bf16[24,2048]{1,0:T(8,128)(2,1)S(1)}, bf16[24,2048]{1,0:T(8,128)(2,1)S(1)}, u32[]{:S(2)}, u32[]{:S(2)}) collective-permute-start(bf16[24,2048]{1,0:T(8,128)(2,1)S(1)} %get-tuple-element.39), channel_id=1, source_target_pairs={{0,12},{2,14},{4,8},{6,10},{8,4},{10,6},{12,0},{14,2},{1,13},{3,15... | collective-permute-start | bytes 294920 | tf_op jit(solution)/shard_map/ppermute | solution.py:215
  11.0 13.6 %collective-permute-start = (bf16[24,2048]{1,0:T(8,128)(2,1)S(1)}, bf16[24,2048]{1,0:T(8,128)(2,1)S(1)}, u32[]{:S(2)}, u32[]{:S(2)}) collective-permute-start(bf16[24,2048]{1,0:T(8,128)(2,1)S(1)} %get-tuple-element.39), channel_id=1, source_target_pairs={{0,8},{2,10},{4,12},{6,14},{8,0},{10,2},{12,4},{14,6},{1,9},{3,11}... | collective-permute-start | bytes 294920 | tf_op jit(solution)/shard_map/ppermute | solution.py:215
  13.1 9.7 %collective-permute-start.3 = (bf16[48,2048]{1,0:T(8,128)(2,1)S(1)}, bf16[48,2048]{1,0:T(8,128)(2,1)S(1)}, u32[]{:S(2)}, u32[]{:S(2)}) collective-permute-start(bf16[48,2048]{1,0:T(8,128)(2,1)S(1)} %pad_maximum_fusion), channel_id=1, source_target_pairs={{0,4},{2,6},{4,0},{6,2},{8,12},{10,14},{12,8},{14,10},{1,5},{3,7},... | collective-permute-start | bytes 589832 | tf_op jit(solution)/shard_map/ppermute | solution.py:215
  21.1 1.7 %collective-permute-start.6 = (bf16[48,2048]{1,0:T(8,128)(2,1)S(1)}, bf16[48,2048]{1,0:T(8,128)(2,1)S(1)}, u32[]{:S(2)}, u32[]{:S(2)}) collective-permute-start(bf16[48,2048]{1,0:T(8,128)(2,1)S(1)} %pad_maximum_fusion.1.rows_ref), channel_id=1, source_target_pairs={{0,1},{1,0},{2,3},{3,2},{4,5},{5,4},{6,7},{7,6},{8,9},{9,8},{10,11... | collective-permute-start | bytes 589832 | tf_op jit(solution)/shard_map/ppermute | solution.py:210
  24.7 13.6 %copy-start = (s32[8192]{0:T(1024)S(1)}, s32[8192]{0:T(1024)}, u32[]{:S(2)}) copy-start(s32[8192]{0:T(1024)} %param.7) | copy-start | bytes 98308
  24.7 3.7 %collective-permute-start.7 = (bf16[144,2048]{1,0:T(8,128)(2,1)S(1)}, bf16[144,2048]{1,0:T(8,128)(2,1)S(1)}, u32[]{:S(2)}, u32[]{:S(2)}) collective-permute-start(bf16[144,2048]{1,0:T(8,128)(2,1)S(1)} %constant_dynamic-update-slice_fusion.rows_ref), channel_id=1, source_target_pairs={{0,1},{1,0},{2,3},{3,2},{4,5},{5,4},{6,7},{7,6},{8,9},{9,8},{10,11... | collective-permute-start | bytes 1769480 | tf_op jit(solution)/shard_map/ppermute | solution.py:210
  25.3 8.4 %collective-permute-start.11 = (s16[48,2176]{1,0:T(8,128)(2,1)S(1)}, s16[48,2176]{1,0:T(8,128)(2,1)S(1)}, u32[]{:S(2)}, u32[]{:S(2)}) collective-permute-start(s16[48,2176]{1,0:T(8,128)(2,1)S(1)} %shard_map.62), channel_id=1, source_target_pairs={{0,2},{2,0},{4,6},{6,4},{8,10},{10,8},{12,14},{14,12},{1,3},{3,1},... | collective-permute-start | bytes 626696 | tf_op jit(solution)/shard_map/ppermute | solution.py:215
  30.1 8.2 %collective-permute-start.8 = (s16[24,2176]{1,0:T(8,128)(2,1)S(1)}, s16[24,2176]{1,0:T(8,128)(2,1)S(1)}, u32[]{:S(2)}, u32[]{:S(2)}) collective-permute-start(s16[24,2176]{1,0:T(8,128)(2,1)S(1)} %get-tuple-element.44), channel_id=1, source_target_pairs={{0,4},{2,6},{4,0},{6,2},{8,12},{10,14},{12,8},{14,10},{1,5},{3,7},... | collective-permute-start | bytes 313352 | tf_op jit(solution)/shard_map/ppermute | solution.py:215
  30.2 8.1 %collective-permute-start.9 = (s16[24,2176]{1,0:T(8,128)(2,1)S(1)}, s16[24,2176]{1,0:T(8,128)(2,1)S(1)}, u32[]{:S(2)}, u32[]{:S(2)}) collective-permute-start(s16[24,2176]{1,0:T(8,128)(2,1)S(1)} %get-tuple-element.45), channel_id=1, source_target_pairs={{0,2},{2,0},{4,6},{6,4},{8,10},{10,8},{12,14},{14,12},{1,3},{3,1},... | collective-permute-start | bytes 313352 | tf_op jit(solution)/shard_map/ppermute | solution.py:215
  30.7 7.6 %collective-permute-start.10 = (s16[24,2176]{1,0:T(8,128)(2,1)S(1)}, s16[24,2176]{1,0:T(8,128)(2,1)S(1)}, u32[]{:S(2)}, u32[]{:S(2)}) collective-permute-start(s16[24,2176]{1,0:T(8,128)(2,1)S(1)} %get-tuple-element.46), channel_id=1, source_target_pairs={{0,6},{2,4},{4,2},{6,0},{8,14},{10,12},{12,10},{14,8},{1,7},{3,5},... | collective-permute-start | bytes 313352 | tf_op jit(solution)/shard_map/ppermute | solution.py:215
  34.9 10.6 %collective-permute-start.12 = (s16[24,2176]{1,0:T(8,128)(2,1)S(1)}, s16[24,2176]{1,0:T(8,128)(2,1)S(1)}, u32[]{:S(2)}, u32[]{:S(2)}) collective-permute-start(s16[24,2176]{1,0:T(8,128)(2,1)S(1)} %get-tuple-element.50), channel_id=1, source_target_pairs={{0,8},{2,10},{4,12},{6,14},{8,0},{10,2},{12,4},{14,6},{1,9},{3,11}... | collective-permute-start | bytes 313352 | tf_op jit(solution)/shard_map/ppermute | solution.py:215
  36.8 8.7 %collective-permute-start.13 = (s16[24,2176]{1,0:T(8,128)(2,1)S(1)}, s16[24,2176]{1,0:T(8,128)(2,1)S(1)}, u32[]{:S(2)}, u32[]{:S(2)}) collective-permute-start(s16[24,2176]{1,0:T(8,128)(2,1)S(1)} %get-tuple-element.51), channel_id=1, source_target_pairs={{0,12},{2,14},{4,8},{6,10},{8,4},{10,6},{12,0},{14,2},{1,13},{3,15... | collective-permute-start | bytes 313352 | tf_op jit(solution)/shard_map/ppermute | solution.py:215

commit v7 on v6

--- a/solution.py
+++ b/solution.py
@@ -103,13 +103,18 @@
     scales = [scale_of(ref[:, columns:]) for ref in got_refs]
     codes = jnp.zeros((rows, LANES), jnp.float32)
     lane = lane_of(rows)
-    for head in range(columns // HEAD):
-        at = slice(head * HEAD, (head + 1) * HEAD)
+    heads = range(columns // HEAD)
+    spans = [slice(head * HEAD, (head + 1) * HEAD) for head in heads]
+    totals = []
+    for head, at in zip(heads, spans):
         total = keep_ref[:, at]
         for ref, scale in zip(got_refs, scales):
             total = total + decode(ref[:, at], scale[:, head : head + 1])
-        coded, code = encode(total)
+        totals.append(total)
+    pairs = [encode(total) for total in totals]
+    for head, (_, code) in zip(heads, pairs):
         codes = jnp.where(lane == head, code, codes)
+    for at, (coded, _) in zip(spans, pairs):
         for k, ref in enumerate(out_refs):
             ref[:, at] = coded[k * tok : (k + 1) * tok]
     codes = codes.astype(jnp.int32).astype(jnp.int16)

time: 47.3 us -> 46.6 us (0.985)
  Pallas kernels: 16.8 us -> 15.9 us
    pallas_call x1, Pallas kernels: 1.26 us -> 0.36 us  [per_device(): local(functools.partial(middle, seqs), [jax.ShapeDtypeStruct((tok, wide),...]
  transfers between devices with their start and end apart: 14 -> 14, of which waited for: 2 -> 3; matrix products, arithmetic and copies ran while one was open for 2% -> 2% of each run, Pallas kernels for 30% -> 29%
where the time goes in v7:
time: 46.6 us; the launch traced here: 46.4 us
  starting transfers between devices  21.6 us (46%)
  Pallas kernels  15.9 us (34%)
  waiting for transfers between devices  6.87 us (15%)
  other arithmetic  1.09 us (2%)
  between operations  0.85 us (2%)
    ppermute x12, starting transfers between devices, cross(): return lax.ppermute(array, ('tensor', 'seq'), pairs)  21 us
    ppermute x12, waiting for transfers between devices, cross(): return lax.ppermute(array, ('tensor', 'seq'), pairs)  6.87 us
    pallas_call x1, Pallas kernels, loaded(): local(load, [pltpu.VMEM((part, columns), weight.dtype)] * cores, [hbm], 4...  5.93 us
    pallas_call x2, Pallas kernels, projected(): local(functools.partial(second_half, len(keeps), tile), [jax.ShapeDtypeSt...  3.38 us
    pallas_call x2, Pallas kernels, projected(): local(functools.partial(first_half, tile), jax.ShapeDtypeStruct((rows, co...  2.98 us
    pallas_call x1, Pallas kernels, per_device(): local(functools.partial(final, near, chunks, tok), [jax.ShapeDtypeStruct(...  1.64 us
    pallas_call x1, Pallas kernels, per_device(): local(take, [pltpu.VMEM((tok, part), hidden_rows.dtype)] * seqs, [hbm], 4...  0.97 us
  transfers between devices with their start and end apart: 14, of which 3 were waited for; matrix products, arithmetic and copies ran while one was open for 2% of the time, Pallas kernels for 29%

profile of v7, /device:TPU:0, one launch (start us, length us, event | category | flops | bytes accessed | tf_op | source)
XLA Modules:
  0.0 46.4 jit_solution(18262026622021082908)
XLA Ops:
  0.6 1.0 %shard_map.59 = (bf16[24,2048]{1,0:T(8,128)(2,1)S(1)}, bf16[24,2048]{1,0:T(8,128)(2,1)S(1)}) custom-call(bf16[24,8192]{1,0:T(8,128)(2,1)} %rows_ref.1), custom_call_target="tpu_custom_call" | custom-call | tf_op jit(solution)/shard_map/pallas_call | solution.py:268
  1.6 6.0 %collective-permute-start.5 = (bf16[24,2048]{1,0:T(8,128)(2,1)S(1)}, bf16[24,2048]{1,0:T(8,128)(2,1)S(1)}, u32[]{:S(2)}, u32[]{:S(2)}) collective-permute-start(bf16[24,2048]{1,0:T(8,128)(2,1)S(1)} %get-tuple-element.29), channel_id=1, source_target_pairs={{0,14},{2,12},{4,10},{6,8},{8,6},{10,4},{12,2},{14,0},{1,15},{3,13... | collective-permute-start | bytes 294920 | tf_op jit(solution)/shard_map/ppermute | solution.py:220
  7.6 0.0 collective-permute-start.4
  7.7 0.9 %collective-permute-start.2 = (bf16[24,2048]{1,0:T(8,128)(2,1)S(1)}, bf16[24,2048]{1,0:T(8,128)(2,1)S(1)}, u32[]{:S(2)}, u32[]{:S(2)}) collective-permute-start(bf16[24,2048]{1,0:T(8,128)(2,1)S(1)} %get-tuple-element.29), channel_id=1, source_target_pairs={{0,2},{2,0},{4,6},{6,4},{8,10},{10,8},{12,14},{14,12},{1,3},{3,1},... | collective-permute-start | bytes 294920 | tf_op jit(solution)/shard_map/ppermute | solution.py:220
  8.5 2.5 %collective-permute-start.1 = (bf16[24,2048]{1,0:T(8,128)(2,1)S(1)}, bf16[24,2048]{1,0:T(8,128)(2,1)S(1)}, u32[]{:S(2)}, u32[]{:S(2)}) collective-permute-start(bf16[24,2048]{1,0:T(8,128)(2,1)S(1)} %get-tuple-element.39), channel_id=1, source_target_pairs={{0,12},{2,14},{4,8},{6,10},{8,4},{10,6},{12,0},{14,2},{1,13},{3,15... | collective-permute-start | bytes 294920 | tf_op jit(solution)/shard_map/ppermute | solution.py:220
  11.0 1.0 %collective-permute-start = (bf16[24,2048]{1,0:T(8,128)(2,1)S(1)}, bf16[24,2048]{1,0:T(8,128)(2,1)S(1)}, u32[]{:S(2)}, u32[]{:S(2)}) collective-permute-start(bf16[24,2048]{1,0:T(8,128)(2,1)S(1)} %get-tuple-element.39), channel_id=1, source_target_pairs={{0,8},{2,10},{4,12},{6,14},{8,0},{10,2},{12,4},{14,6},{1,9},{3,11}... | collective-permute-start | bytes 294920 | tf_op jit(solution)/shard_map/ppermute | solution.py:220
  12.1 0.7 %select_reduce_fusion.1 = s32[4]{0:T(128)S(1)} fusion(s32[4]{0:T(128)} %param.6), kind=kLoop, calls=%fused_computation.16 | loop fusion | flops 44 | bytes 32 | tf_op jit(solution)/shard_map/reduce_sum | solution.py:257
  12.8 0.1 select_reduce_fusion
  12.9 0.1 fusion.2
  13.0 0.1 pad_maximum_fusion.2
  13.1 0.0 collective-permute-done.2
  13.1 1.9 %collective-permute-start.3 = (bf16[48,2048]{1,0:T(8,128)(2,1)S(1)}, bf16[48,2048]{1,0:T(8,128)(2,1)S(1)}, u32[]{:S(2)}, u32[]{:S(2)}) collective-permute-start(bf16[48,2048]{1,0:T(8,128)(2,1)S(1)} %pad_maximum_fusion), channel_id=1, source_target_pairs={{0,4},{2,6},{4,0},{6,2},{8,12},{10,14},{12,8},{14,10},{1,5},{3,7},... | collective-permute-start | bytes 589832 | tf_op jit(solution)/shard_map/ppermute | solution.py:220
  15.0 5.9 %shard_map.60 = (bf16[2048,2048]{1,0:T(8,128)(2,1)S(1)}, bf16[2048,2048]{1,0:T(8,128)(2,1)S(1)}) custom-call(bf16[4096,2048]{1,0:T(8,128)(2,1)} %bitcast.5), custom_call_target="tpu_custom_call" | custom-call | bytes 33554432 | tf_op jit(solution)/shard_map/pallas_call | solution.py:247
  21.0 0.0 collective-permute-done.5
  21.0 0.1 collective-permute-done.4
  21.1 0.1 collective-permute-start.6
  21.2 1.6 %shard_map.61.acc_ref = f32[48,2048]{1,0:T(8,128)S(1)} custom-call(bf16[48,2048]{1,0:T(8,128)(2,1)S(1)} %pad_maximum_fusion.1.rows_ref, bf16[2048,2048]{1,0:T(8,128)(2,1)S(1)} %get-tuple-element.36.w_ref), custom_call_target="tpu_custom_call" | custom-call | flops 402653184 | bytes 393216 | tf_op jit(solution)/shard_map/pallas_call | solution.py:301
  22.8 0.0 collective-permute-done.3
  22.8 0.0 collective-permute-done.6.rows_ref
  22.8 1.7 %shard_map.62 = s16[48,2176]{1,0:T(8,128)(2,1)S(1)} custom-call(bf16[48,2048]{1,0:T(8,128)(2,1)S(1)} %collective-permute-done.6.rows_ref, bf16[2048,2048]{1,0:T(8,128)(2,1)S(1)} %get-tuple-element.35.w_ref, f32[48,2048]{1,0:T(8,128)S(1)} %shard_map.61.acc_ref), custom_call_target="tpu_custom_call" | custom-call | flops 402653184 | bytes 393216 | tf_op jit(solution)/shard_map/pallas_call | solution.py:308
  24.6 0.0 collective-permute-done.1
  24.6 0.0 collective-permute-done
  24.7 0.0 copy-start
  24.7 0.6 %collective-permute-start.7 = (bf16[144,2048]{1,0:T(8,128)(2,1)S(1)}, bf16[144,2048]{1,0:T(8,128)(2,1)S(1)}, u32[]{:S(2)}, u32[]{:S(2)}) collective-permute-start(bf16[144,2048]{1,0:T(8,128)(2,1)S(1)} %constant_dynamic-update-slice_fusion.rows_ref), channel_id=1, source_target_pairs={{0,1},{1,0},{2,3},{3,2},{4,5},{5,4},{6,7},{7,6},{8,9},{9,8},{10,11... | collective-permute-start | bytes 1769480 | tf_op jit(solution)/shard_map/ppermute | solution.py:215
  25.3 1.7 %collective-permute-start.11 = (s16[48,2176]{1,0:T(8,128)(2,1)S(1)}, s16[48,2176]{1,0:T(8,128)(2,1)S(1)}, u32[]{:S(2)}, u32[]{:S(2)}) collective-permute-start(s16[48,2176]{1,0:T(8,128)(2,1)S(1)} %shard_map.62), channel_id=1, source_target_pairs={{0,2},{2,0},{4,6},{6,4},{8,10},{10,8},{12,14},{14,12},{1,3},{3,1},... | collective-permute-start | bytes 626696 | tf_op jit(solution)/shard_map/ppermute | solution.py:220
  27.0 1.4 %shard_map.63.acc_ref = f32[144,2048]{1,0:T(8,128)S(1)} custom-call(bf16[144,2048]{1,0:T(8,128)(2,1)S(1)} %constant_dynamic-update-slice_fusion.rows_ref, bf16[2048,2048]{1,0:T(8,128)(2,1)S(1)} %get-tuple-element.36.w_ref), custom_call_target="tpu_custom_call" | custom-call | flops 1207959552 | bytes 1179648 | tf_op jit(solution)/shard_map/pallas_call | solution.py:301
  28.5 0.0 collective-permute-done.7.rows_ref
  28.5 1.6 %shard_map.64 = (f32[48,2048]{1,0:T(8,128)S(1)}, f32[24,2048]{1,0:T(8,128)S(1)}, s16[24,2176]{1,0:T(8,128)(2,1)S(1)}, s16[24,2176]{1,0:T(8,128)(2,1)S(1)}, s16[24,2176]{1,0:T(8,128)(2,1)S(1)}) custom-call(bf16[144,2048]{1,0:T(8,128)(2,1)S(1)} %collective-permute-done.7.rows_ref, bf16[2048,2048]{1,0:T(8,128)(2,1)S(1)} %get-tuple-element.35.w_ref, ...), custom_call_target="tpu_custom_call" | custom-call | flops 1207959552 | bytes 1179648 | tf_op jit(solution)/shard_map/pallas_call | solution.py:308
  30.1 0.1 collective-permute-start.8
  30.2 0.5 %collective-permute-start.9 = (s16[24,2176]{1,0:T(8,128)(2,1)S(1)}, s16[24,2176]{1,0:T(8,128)(2,1)S(1)}, u32[]{:S(2)}, u32[]{:S(2)}) collective-permute-start(s16[24,2176]{1,0:T(8,128)(2,1)S(1)} %get-tuple-element.45), channel_id=1, source_target_pairs={{0,2},{2,0},{4,6},{6,4},{8,10},{10,8},{12,14},{14,12},{1,3},{3,1},... | collective-permute-start | bytes 313352 | tf_op jit(solution)/shard_map/ppermute | solution.py:220
  30.7 2.9 %collective-permute-start.10 = (s16[24,2176]{1,0:T(8,128)(2,1)S(1)}, s16[24,2176]{1,0:T(8,128)(2,1)S(1)}, u32[]{:S(2)}, u32[]{:S(2)}) collective-permute-start(s16[24,2176]{1,0:T(8,128)(2,1)S(1)} %get-tuple-element.46), channel_id=1, source_target_pairs={{0,6},{2,4},{4,2},{6,0},{8,14},{10,12},{12,10},{14,8},{1,7},{3,5},... | collective-permute-start | bytes 313352 | tf_op jit(solution)/shard_map/ppermute | solution.py:220
  33.7 0.0 collective-permute-done.11.refs_0_
  33.7 0.4 shard_map.66
  34.1 1.9 %collective-permute-start.12 = (s16[24,2176]{1,0:T(8,128)(2,1)S(1)}, s16[24,2176]{1,0:T(8,128)(2,1)S(1)}, u32[]{:S(2)}, u32[]{:S(2)}) collective-permute-start(s16[24,2176]{1,0:T(8,128)(2,1)S(1)} %get-tuple-element.50), channel_id=1, source_target_pairs={{0,8},{2,10},{4,12},{6,14},{8,0},{10,2},{12,4},{14,6},{1,9},{3,11}... | collective-permute-start | bytes 313352 | tf_op jit(solution)/shard_map/ppermute | solution.py:220
  36.0 1.5 %collective-permute-start.13 = (s16[24,2176]{1,0:T(8,128)(2,1)S(1)}, s16[24,2176]{1,0:T(8,128)(2,1)S(1)}, u32[]{:S(2)}, u32[]{:S(2)}) collective-permute-start(s16[24,2176]{1,0:T(8,128)(2,1)S(1)} %get-tuple-element.51), channel_id=1, source_target_pairs={{0,12},{2,14},{4,8},{6,10},{8,4},{10,6},{12,0},{14,2},{1,13},{3,15... | collective-permute-start | bytes 313352 | tf_op jit(solution)/shard_map/ppermute | solution.py:220
  37.4 0.0 collective-permute-done.8.refs_1_
  37.4 0.1 collective-permute-done.9.refs_2_
  37.5 0.0 collective-permute-done.10.refs_3_
  37.5 0.0 copy-done
  37.5 0.6 %shard_map.65.near_ref = f32[768,128]{1,0:T(8,128)S(1)} custom-call(f32[24,2048]{1,0:T(8,128)S(1)} %get-tuple-element.43.refs_0_, s16[24,2176]{1,0:T(8,128)(2,1)S(1)} %collective-permute-done.8.refs_1_, s16[24,2176]{1,0:T(8,128)(2,1)S(1)} %collective-permute-done.9.refs_2_, s16[24,2176]{1,0:T(8,128)(2,1)S(1)} %collective-permute-done.10.refs_3_, ...), custom_call_target="tpu_custom_call" | custom-call | flops 75497472 | bytes 786432 | tf_op jit(solution)/shard_map/pallas_call | solution.py:339
  38.2 6.6 %collective-permute-done.12.refs_0_ = s16[24,2176]{1,0:T(8,128)(2,1)S(1)} collective-permute-done((s16[24,2176]{1,0:T(8,128)(2,1)S(1)}, s16[24,2176]{1,0:T(8,128)(2,1)S(1)}, u32[]{:S(2)}, u32[]{:S(2)}) %collective-permute-start.12) | collective-permute-done | bytes 104480 | tf_op jit(solution)/shard_map/ppermute | solution.py:220
  44.8 0.0 collective-permute-done.13.refs_1_
  44.8 1.6 %shard_map.67 = (bf16[24,8192]{1,0:T(8,128)(2,1)}, f32[1,24]{1,0:T(1,128)}) custom-call(f32[768,128]{1,0:T(8,128)S(1)} %shard_map.65.near_ref, s16[24,2176]{1,0:T(8,128)(2,1)S(1)} %collective-permute-done.12.refs_0_, s16[24,2176]{1,0:T(8,128)(2,1)S(1)} %collective-permute-done.13.refs_1_, f32[24,128]{1,0:T(8,128)S(1)} %get-tuple-element.47.refs_4_.refs_2_, ...), custom_call_target="tpu_custom_call" | custom-call | bytes 1572864 | tf_op jit(solution)/shard_map/pallas_call | solution.py:347
  (12 shorter events, 0.1 us)
Async XLA Ops:
  1.6 19.4 %collective-permute-start.5 = (bf16[24,2048]{1,0:T(8,128)(2,1)S(1)}, bf16[24,2048]{1,0:T(8,128)(2,1)S(1)}, u32[]{:S(2)}, u32[]{:S(2)}) collective-permute-start(bf16[24,2048]{1,0:T(8,128)(2,1)S(1)} %get-tuple-element.29), channel_id=1, source_target_pairs={{0,14},{2,12},{4,10},{6,8},{8,6},{10,4},{12,2},{14,0},{1,15},{3,13... | collective-permute-start | bytes 294920 | tf_op jit(solution)/shard_map/ppermute | solution.py:220
  7.6 13.5 %collective-permute-start.4 = (bf16[24,2048]{1,0:T(8,128)(2,1)S(1)}, bf16[24,2048]{1,0:T(8,128)(2,1)S(1)}, u32[]{:S(2)}, u32[]{:S(2)}) collective-permute-start(bf16[24,2048]{1,0:T(8,128)(2,1)S(1)} %get-tuple-element.29), channel_id=1, source_target_pairs={{0,10},{2,8},{4,14},{6,12},{8,2},{10,0},{12,6},{14,4},{1,11},{3,9}... | collective-permute-start | bytes 294920 | tf_op jit(solution)/shard_map/ppermute | solution.py:220
  7.7 5.5 %collective-permute-start.2 = (bf16[24,2048]{1,0:T(8,128)(2,1)S(1)}, bf16[24,2048]{1,0:T(8,128)(2,1)S(1)}, u32[]{:S(2)}, u32[]{:S(2)}) collective-permute-start(bf16[24,2048]{1,0:T(8,128)(2,1)S(1)} %get-tuple-element.29), channel_id=1, source_target_pairs={{0,2},{2,0},{4,6},{6,4},{8,10},{10,8},{12,14},{14,12},{1,3},{3,1},... | collective-permute-start | bytes 294920 | tf_op jit(solution)/shard_map/ppermute | solution.py:220
  8.5 16.0 %collective-permute-start.1 = (bf16[24,2048]{1,0:T(8,128)(2,1)S(1)}, bf16[24,2048]{1,0:T(8,128)(2,1)S(1)}, u32[]{:S(2)}, u32[]{:S(2)}) collective-permute-start(bf16[24,2048]{1,0:T(8,128)(2,1)S(1)} %get-tuple-element.39), channel_id=1, source_target_pairs={{0,12},{2,14},{4,8},{6,10},{8,4},{10,6},{12,0},{14,2},{1,13},{3,15... | collective-permute-start | bytes 294920 | tf_op jit(solution)/shard_map/ppermute | solution.py:220
  11.0 13.6 %collective-permute-start = (bf16[24,2048]{1,0:T(8,128)(2,1)S(1)}, bf16[24,2048]{1,0:T(8,128)(2,1)S(1)}, u32[]{:S(2)}, u32[]{:S(2)}) collective-permute-start(bf16[24,2048]{1,0:T(8,128)(2,1)S(1)} %get-tuple-element.39), channel_id=1, source_target_pairs={{0,8},{2,10},{4,12},{6,14},{8,0},{10,2},{12,4},{14,6},{1,9},{3,11}... | collective-permute-start | bytes 294920 | tf_op jit(solution)/shard_map/ppermute | solution.py:220
  13.1 9.7 %collective-permute-start.3 = (bf16[48,2048]{1,0:T(8,128)(2,1)S(1)}, bf16[48,2048]{1,0:T(8,128)(2,1)S(1)}, u32[]{:S(2)}, u32[]{:S(2)}) collective-permute-start(bf16[48,2048]{1,0:T(8,128)(2,1)S(1)} %pad_maximum_fusion), channel_id=1, source_target_pairs={{0,4},{2,6},{4,0},{6,2},{8,12},{10,14},{12,8},{14,10},{1,5},{3,7},... | collective-permute-start | bytes 589832 | tf_op jit(solution)/shard_map/ppermute | solution.py:220
  21.1 1.7 %collective-permute-start.6 = (bf16[48,2048]{1,0:T(8,128)(2,1)S(1)}, bf16[48,2048]{1,0:T(8,128)(2,1)S(1)}, u32[]{:S(2)}, u32[]{:S(2)}) collective-permute-start(bf16[48,2048]{1,0:T(8,128)(2,1)S(1)} %pad_maximum_fusion.1.rows_ref), channel_id=1, source_target_pairs={{0,1},{1,0},{2,3},{3,2},{4,5},{5,4},{6,7},{7,6},{8,9},{9,8},{10,11... | collective-permute-start | bytes 589832 | tf_op jit(solution)/shard_map/ppermute | solution.py:215
  24.7 12.8 %copy-start = (s32[8192]{0:T(1024)S(1)}, s32[8192]{0:T(1024)}, u32[]{:S(2)}) copy-start(s32[8192]{0:T(1024)} %param.7) | copy-start | bytes 98308
  24.7 3.7 %collective-permute-start.7 = (bf16[144,2048]{1,0:T(8,128)(2,1)S(1)}, bf16[144,2048]{1,0:T(8,128)(2,1)S(1)}, u32[]{:S(2)}, u32[]{:S(2)}) collective-permute-start(bf16[144,2048]{1,0:T(8,128)(2,1)S(1)} %constant_dynamic-update-slice_fusion.rows_ref), channel_id=1, source_target_pairs={{0,1},{1,0},{2,3},{3,2},{4,5},{5,4},{6,7},{7,6},{8,9},{9,8},{10,11... | collective-permute-start | bytes 1769480 | tf_op jit(solution)/shard_map/ppermute | solution.py:215
  25.3 8.4 %collective-permute-start.11 = (s16[48,2176]{1,0:T(8,128)(2,1)S(1)}, s16[48,2176]{1,0:T(8,128)(2,1)S(1)}, u32[]{:S(2)}, u32[]{:S(2)}) collective-permute-start(s16[48,2176]{1,0:T(8,128)(2,1)S(1)} %shard_map.62), channel_id=1, source_target_pairs={{0,2},{2,0},{4,6},{6,4},{8,10},{10,8},{12,14},{14,12},{1,3},{3,1},... | collective-permute-start | bytes 626696 | tf_op jit(solution)/shard_map/ppermute | solution.py:220
  30.1 7.3 %collective-permute-start.8 = (s16[24,2176]{1,0:T(8,128)(2,1)S(1)}, s16[24,2176]{1,0:T(8,128)(2,1)S(1)}, u32[]{:S(2)}, u32[]{:S(2)}) collective-permute-start(s16[24,2176]{1,0:T(8,128)(2,1)S(1)} %get-tuple-element.44), channel_id=1, source_target_pairs={{0,4},{2,6},{4,0},{6,2},{8,12},{10,14},{12,8},{14,10},{1,5},{3,7},... | collective-permute-start | bytes 313352 | tf_op jit(solution)/shard_map/ppermute | solution.py:220
  30.2 7.3 %collective-permute-start.9 = (s16[24,2176]{1,0:T(8,128)(2,1)S(1)}, s16[24,2176]{1,0:T(8,128)(2,1)S(1)}, u32[]{:S(2)}, u32[]{:S(2)}) collective-permute-start(s16[24,2176]{1,0:T(8,128)(2,1)S(1)} %get-tuple-element.45), channel_id=1, source_target_pairs={{0,2},{2,0},{4,6},{6,4},{8,10},{10,8},{12,14},{14,12},{1,3},{3,1},... | collective-permute-start | bytes 313352 | tf_op jit(solution)/shard_map/ppermute | solution.py:220
  30.7 6.8 %collective-permute-start.10 = (s16[24,2176]{1,0:T(8,128)(2,1)S(1)}, s16[24,2176]{1,0:T(8,128)(2,1)S(1)}, u32[]{:S(2)}, u32[]{:S(2)}) collective-permute-start(s16[24,2176]{1,0:T(8,128)(2,1)S(1)} %get-tuple-element.46), channel_id=1, source_target_pairs={{0,6},{2,4},{4,2},{6,0},{8,14},{10,12},{12,10},{14,8},{1,7},{3,5},... | collective-permute-start | bytes 313352 | tf_op jit(solution)/shard_map/ppermute | solution.py:220
  34.1 10.7 %collective-permute-start.12 = (s16[24,2176]{1,0:T(8,128)(2,1)S(1)}, s16[24,2176]{1,0:T(8,128)(2,1)S(1)}, u32[]{:S(2)}, u32[]{:S(2)}) collective-permute-start(s16[24,2176]{1,0:T(8,128)(2,1)S(1)} %get-tuple-element.50), channel_id=1, source_target_pairs={{0,8},{2,10},{4,12},{6,14},{8,0},{10,2},{12,4},{14,6},{1,9},{3,11}... | collective-permute-start | bytes 313352 | tf_op jit(solution)/shard_map/ppermute | solution.py:220
  36.0 8.8 %collective-permute-start.13 = (s16[24,2176]{1,0:T(8,128)(2,1)S(1)}, s16[24,2176]{1,0:T(8,128)(2,1)S(1)}, u32[]{:S(2)}, u32[]{:S(2)}) collective-permute-start(s16[24,2176]{1,0:T(8,128)(2,1)S(1)} %get-tuple-element.51), channel_id=1, source_target_pairs={{0,12},{2,14},{4,8},{6,10},{8,4},{10,6},{12,0},{14,2},{1,13},{3,15... | collective-permute-start | bytes 313352 | tf_op jit(solution)/shard_map/ppermute | solution.py:220
